TPU v7x, 32 devices: a whole 2x2x4 slice. The times are simulated.
32 devices in a mesh: grp: 2 (over y), term: 4 (over z), sub: 2 (over x), pair: 2 (over core).
Axes of the slice: x: 2, y: 2, z: 4, core: 2. Of those that a mesh axis runs over, the one named last changes fastest.
Arguments:
- psi: bfloat16 [8, 256, 256], P(('grp', 'term'), 'pair'), parts along dimension 0, may hold values from -6 to 6
- left_blocks: bfloat16 [16, 8, 256, 256], P(('grp', 'term', 'sub'), None, 'pair'), parts along dimension 0, may hold values from -0.046875 to 0.046875
- right_blocks: bfloat16 [16, 8, 256, 256], P(('grp', 'term', 'sub')), parts along dimension 0, may hold values from -0.375 to 0.375
- left_index: int32 [16, 72], P(('grp', 'term', 'sub')), parts along dimension 0, may hold values from 0 to 7
- right_index: int32 [16, 72], P(('grp', 'term', 'sub')), parts along dimension 0, may hold values from 0 to 7
- block_source: int32 [16, 72], P(('grp', 'term', 'sub')), parts along dimension 0, may hold values from 0 to 3
- block_target: int32 [16, 72], P(('grp', 'term', 'sub')), parts along dimension 0, may hold values from 0 to 3
- block_count: int32 [16], P(('grp', 'term', 'sub')), parts along dimension 0, may hold values from 36 to 72, as said below
- sector_energy: float32 [8], P(('grp', 'term')), parts along dimension 0, may hold values from 0.3 to 3
Outputs:
- sigma_first: bfloat16 [8, 256, 256], P(('grp', 'term'), 'pair'), parts along dimension 0
- sigma_second: bfloat16 [8, 256, 256], P(('grp', 'term'), 'pair'), parts along dimension 0
There are 2 independent parts, one for each index of `grp`. A program takes and returns all parts, laid end to end along the dimension named above; each array names one. Nothing has to cross between parts.
Inputs may be any that keep to these rules, and one draw needn't show every extreme that they name: `block_count`: some term sublist has all 72 slots live in every draw.
All inputs are finite; a program needn't handle non-finite values.
Results may differ from a plain program's by a relative error of at most 0.0074.
Values may be sent and summed in bfloat16 or wider, within the bound.
No kernel may reach another device: no remote copies, remote signals or barrier semaphores. Data moves between devices by JAX's collectives and lax.ppermute only.
A program may use at most 64 MiB of HBM per device.

v0:
```python
import jax
import jax.numpy as jnp
from jax import lax
from jax.sharding import PartitionSpec as P

slot_batch = 8


def gather_sectors(vector):
    pieces = lax.all_gather(vector, ("term", "pair"), axis=1, tiled=True)
    return pieces.reshape(lax.axis_size("term"), -1, vector.shape[2])


def apply_blocks(
    full_vector,
    left_blocks,
    right_blocks,
    left_index,
    right_index,
    block_source,
    block_target,
    block_count,
):
    half_rows = left_blocks.shape[2]
    columns = left_blocks.shape[3]
    sectors = full_vector.shape[0]
    lefts = left_blocks[0]
    rights = right_blocks[0]
    live_count = block_count[0]
    start_totals = jnp.zeros((sectors, half_rows, columns), jnp.float32)

    def one_turn(turn_index, totals):
        first_slot = turn_index * slot_batch
        pick_left = lax.dynamic_slice_in_dim(left_index[0], first_slot, slot_batch)
        pick_right = lax.dynamic_slice_in_dim(right_index[0], first_slot, slot_batch)
        pick_source = lax.dynamic_slice_in_dim(block_source[0], first_slot, slot_batch)
        pick_target = lax.dynamic_slice_in_dim(block_target[0], first_slot, slot_batch)
        left_part = jnp.take(lefts, pick_left, axis=0)
        right_part = jnp.take(rights, pick_right, axis=0)
        source_part = jnp.take(full_vector, pick_source, axis=0)
        half = jnp.einsum(
            "kij,kjl->kil", left_part, source_part, preferred_element_type=jnp.float32
        ).astype(jnp.bfloat16)
        product = jnp.einsum("kil,kml->kim", half, right_part, preferred_element_type=jnp.float32)
        alive = (first_slot + jnp.arange(slot_batch) < live_count).astype(jnp.float32)
        return totals.at[pick_target].add(product * alive[:, None, None])

    turn_count = (live_count + slot_batch - 1) // slot_batch
    return lax.fori_loop(0, turn_count, one_turn, start_totals)


def owner_sigma(totals, vector_own, sector_energy):
    energy = sector_energy[:, None, None]
    partial_sum = lax.psum(totals, "sub")
    mine = lax.psum_scatter(partial_sum, "term", scatter_dimension=0, tiled=True)
    return (mine + energy * vector_own.astype(jnp.float32)).astype(jnp.bfloat16)


def on_device(
    psi,
    left_blocks,
    right_blocks,
    left_index,
    right_index,
    block_source,
    block_target,
    block_count,
    sector_energy,
):
    operands = (
        left_blocks,
        right_blocks,
        left_index,
        right_index,
        block_source,
        block_target,
        block_count,
    )
    totals = apply_blocks(gather_sectors(psi), *operands)
    sigma_first = owner_sigma(totals, psi, sector_energy)
    vector = psi.astype(jnp.float32)
    sigma = sigma_first.astype(jnp.float32)
    entries = lax.axis_size("term") * lax.axis_size("pair") * psi.shape[1] * psi.shape[2]
    norm_psi, correlation = lax.psum(
        (jnp.sum(vector * vector), jnp.sum(vector * sigma)), ("term", "pair")
    )
    theta = correlation / norm_psi
    resid = sigma - theta * vector
    resid_sum = lax.psum(jnp.sum(resid * resid), ("term", "pair"))
    scale = lax.rsqrt(resid_sum / entries + 1e-06)
    correction = (resid * scale).astype(jnp.bfloat16)
    totals_second = apply_blocks(gather_sectors(correction), *operands)
    sigma_second = owner_sigma(totals_second, correction, sector_energy)
    return (sigma_first, sigma_second)


def solution(mesh):
    placed = (
        P(("grp", "term"), "pair", None),
        P(("grp", "term", "sub"), None, "pair", None),
        P(("grp", "term", "sub"), None, None, None),
        P(("grp", "term", "sub"), None),
        P(("grp", "term", "sub"), None),
        P(("grp", "term", "sub"), None),
        P(("grp", "term", "sub"), None),
        P(("grp", "term", "sub")),
        P(("grp", "term")),
    )
    return jax.shard_map(
        on_device,
        mesh=mesh,
        in_specs=placed,
        out_specs=(P(("grp", "term"), "pair", None), P(("grp", "term"), "pair", None)),
        check_vma=False,
    )
```

profile of v0, /device:TPU:0, one launch (start us, length us, event | category | flops | bytes accessed | tf_op | source)
XLA Modules:
  0.0 367.2 jit_solution(17409332800522922452)
XLA Ops:
  8.0 16.8 %all_gather.6 = bf16[1,1024,256]{2,1,0:T(8,128)(2,1)S(1)} all-gather(bf16[1,128,256]{2,1,0:T(8,128)(2,1)} %param.19), channel_id=1, replica_groups=mesh['grp'=2,'term'=4,'sub'=2,'pair'=2] {'term','pair'}, dimensions={1}, use_global_device_ids=true | all-gather | bytes 589824 | tf_op jit(solution)/shard_map/all_gather | solution.py:10
  25.5 67.3 %while.20 = (s32[]{:T(128)}, f32[4,128,256]{2,1,0:T(8,128)S(1)}, s32[]{:T(128)}, s32[1,72]{1,0:T(1,128)S(1)}, s32[1,72]{1,0:T(1,128)S(1)}, /*index=5*/bf16[8,128...) while((s32[]{:T(128)}, f32[4,128,256]{2,1,0:T(8,128)S(1)}, ...), condition=%wide.region_2.0_spmd, body=%wide.region_0.5_spmd.sunk | while | flops 270535872 | bytes 12071711 | solution.py:49
  31.0 3.2 convolution_multiply_fusion.4
  34.2 2.5 scatter_fusion
  42.2 3.2 convolution_multiply_fusion.4
  45.4 2.4 scatter_fusion
  53.4 3.2 convolution_multiply_fusion.4
  56.6 2.4 scatter_fusion
  64.7 3.2 convolution_multiply_fusion.4
  67.8 2.4 scatter_fusion
  75.9 3.2 convolution_multiply_fusion.4
  79.1 2.5 scatter_fusion
  87.1 3.2 convolution_multiply_fusion.4
  90.3 2.4 scatter_fusion
  93.6 56.4 %reduce-scatter.3.cloned.1.call-done = f32[1,128,256]{2,1,0:T(8,128)} async-done(((f32[4,128,256]{2,1,0:T(8,128)}), f32[1,128,256]{2,1,0:T(8,128)}) %reduce-scatter.3.cloned.1.call-update) | async-done | bytes 131088 | tf_op jit(solution)/shard_map/reduce_scatter | solution.py:55
  150.8 21.3 %all-reduce.4.cloned.1.call-done = f32[1,128,256]{2,1,0:T(8,128)} async-done(((f32[1,128,256]{2,1,0:T(8,128)}), f32[1,128,256]{2,1,0:T(8,128)}) %all-reduce.4.cloned.1.call-update) | async-done | bytes 131088 | tf_op jit(solution)/shard_map/psum | solution.py:54
  173.6 16.6 %all-reduce = (f32[]{:T(128)}, f32[]{:T(128)}) all-reduce(f32[]{:T(128)} %get-tuple-element.124, f32[]{:T(128)} %get-tuple-element.123), channel_id=1, replica_groups=mesh['grp'=2,'term'=4,'sub'=2,'pair'=2] {'term','pair'}, use_global_device_ids=true, to_apply=%region_6.10 | all-reduce | flops 2 | bytes 16 | tf_op jit(solution)/shard_map/psum | solution.py:84
  192.3 14.3 %psum.38 = f32[]{:T(128)} all-reduce(f32[]{:T(128)} %multiply_reduce_fusion), channel_id=1, replica_groups=mesh['grp'=2,'term'=4,'sub'=2,'pair'=2] {'term','pair'}, use_global_device_ids=true, to_apply=%region_10.14 | all-reduce | flops 1 | bytes 8 | tf_op jit(solution)/shard_map/psum | solution.py:89
  207.4 15.2 %all_gather.7 = bf16[1,1024,256]{2,1,0:T(8,128)(2,1)S(1)} all-gather(bf16[1,128,256]{2,1,0:T(8,128)(2,1)S(1)} %multiply_convert_fusion), channel_id=1, replica_groups=mesh['grp'=2,'term'=4,'sub'=2,'pair'=2] {'term','pair'}, dimensions={1}, use_global_device_ids=true | all-gather | bytes 589824 | tf_op jit(solution)/shard_map/all_gather | solution.py:10
  222.6 63.1 %while.21 = (s32[]{:T(128)}, f32[4,128,256]{2,1,0:T(8,128)S(1)}, s32[]{:T(128)}, s32[1,72]{1,0:T(1,128)S(1)}, s32[1,72]{1,0:T(1,128)S(1)}, /*index=5*/bf16[8,128...) while((s32[]{:T(128)}, f32[4,128,256]{2,1,0:T(8,128)S(1)}, ...), condition=%wide.region_13.17_spmd, body=%wide.region_11.16_spmd.sunk | while | flops 270535872 | bytes 12071711 | solution.py:49
  227.4 3.3 convolution_multiply_fusion.5
  230.7 2.5 scatter_fusion.1
  237.9 3.3 convolution_multiply_fusion.5
  241.2 2.4 scatter_fusion.1
  248.4 3.3 convolution_multiply_fusion.5
  251.7 2.4 scatter_fusion.1
  258.9 3.3 convolution_multiply_fusion.5
  269.4 3.3 convolution_multiply_fusion.5
  272.7 2.5 scatter_fusion.1
  280.0 3.3 convolution_multiply_fusion.5
  286.6 50.6 %reduce-scatter.5.cloned.1.call-done = f32[1,128,256]{2,1,0:T(8,128)} async-done(((f32[4,128,256]{2,1,0:T(8,128)}), f32[1,128,256]{2,1,0:T(8,128)}) %reduce-scatter.5.cloned.1.call-update) | async-done | bytes 131088 | tf_op jit(solution)/shard_map/reduce_scatter | solution.py:55
  337.2 21.9 %all-reduce.6.cloned.1.call-done = f32[1,128,256]{2,1,0:T(8,128)} async-done(((f32[1,128,256]{2,1,0:T(8,128)}), f32[1,128,256]{2,1,0:T(8,128)}) %all-reduce.6.cloned.1.call-update) | async-done | bytes 131088 | tf_op jit(solution)/shard_map/psum | solution.py:54
  (144 shorter events, 72.7 us)
Async XLA Ops:
  7.2 17.6 %copy-start = (bf16[1,8,256,256]{3,2,1,0:T(8,128)(2,1)S(1)}, bf16[1,8,256,256]{3,2,1,0:T(8,128)(2,1)}, u32[]{:S(2)}) copy-start(bf16[1,8,256,256]{3,2,1,0:T(8,128)(2,1)} %param.21) | copy-start | bytes 3145732
  7.2 142.9 %reduce-scatter.3.cloned.1.call-start = ((), (), s32[]{:S(2)}) async-start(), calls=%async_computation.2 | async-start | bytes 655360 | tf_op jit(solution)/shard_map/reduce_scatter | solution.py:55
  24.8 0.7 copy-start.6
  24.8 0.7 copy-start.7
  24.8 0.7 copy-start.8
  24.8 0.7 copy-start.9
  92.7 0.8 copy-start.2
  93.6 78.5 %all-reduce.4.cloned.1.call-start = ((), (), s32[]{:S(2)}) async-start(), calls=%async_computation.3 | async-start | bytes 262144 | tf_op jit(solution)/shard_map/psum | solution.py:54
  150.1 22.0 %copy-start.4 = (bf16[1,128,256]{2,1,0:T(8,128)(2,1)S(1)}, bf16[1,128,256]{2,1,0:T(8,128)(2,1)}, u32[]{:S(2)}) copy-start(bf16[1,128,256]{2,1,0:T(8,128)(2,1)} %param.19) | copy-start | bytes 196612
  150.1 187.1 %reduce-scatter.5.cloned.1.call-start = ((), (), s32[]{:S(2)}) async-start(), calls=%async_computation.4 | async-start | bytes 655360 | tf_op jit(solution)/shard_map/reduce_scatter | solution.py:55
  173.6 33.7 %copy-start.5 = (bf16[1,128,256]{2,1,0:T(8,128)(2,1)}, bf16[1,128,256]{2,1,0:T(8,128)(2,1)S(1)}, u32[]{:S(2)}) copy-start(bf16[1,128,256]{2,1,0:T(8,128)(2,1)S(1)} %get-tuple-element.183) | copy-start | bytes 196612
  207.4 15.2 %copy-start.3 = (bf16[8,128,256]{2,1,0:T(8,128)(2,1)S(1)}, bf16[8,128,256]{2,1,0:T(8,128)(2,1)}, u32[]{:S(2)}) copy-start(bf16[8,128,256]{2,1,0:T(8,128)(2,1)} %get-tuple-element.453) | copy-start | bytes 1572868
  285.7 0.8 copy-start.1
  286.5 72.6 %all-reduce.6.cloned.1.call-start = ((), (), s32[]{:S(2)}) async-start(), calls=%async_computation.5 | async-start | bytes 262144 | tf_op jit(solution)/shard_map/psum | solution.py:54
Sparse Core Ops, SparseCore 0:
  93.7 56.3 reduce-scatter.2
  152.3 19.7 all-reduce.3
  286.6 50.5 reduce-scatter.4
  339.3 19.7 all-reduce.5
where the time goes:
time: 369 us; the launch traced here: 367 us
  waiting for transfers between devices  150 us (41%)
  blocking collectives  62.8 us (17%)
  local copies, waits for them, and re-layouts  53.1 us (14%)
  other arithmetic  44 us (12%)
  matrix products  38.7 us (10%)
  between operations  17.4 us (5%)
    reduce_scatter x2, waiting for transfers between devices, owner_sigma(): lax.psum_scatter(partial_sum, 'term', scatter_dimension=0, tiled=True)  107 us
    psum x2, waiting for transfers between devices, owner_sigma(): partial_sum = lax.psum(totals, 'sub')  43.2 us
    dot_general x12, matrix products, one_turn(): jnp.einsum('kil,kml->kim', half, right_part, preferred_element_type=jnp.f...  38.7 us
    all_gather x2, blocking collectives, gather_sectors(): pieces = lax.all_gather(vector, ('term', 'pair'), axis=1, tiled=True)  31.9 us
    scatter-add x12, other arithmetic, one_turn(): return totals.at[pick_target].add(product * alive[:, None, None])  29.4 us
    gather x12, local copies, waits for them, and re-layouts, one_turn(): right_part = jnp.take(rights, pick_right, axis=0)  19.2 us
    gather x12, local copies, waits for them, and re-layouts, one_turn(): left_part = jnp.take(lefts, pick_left, axis=0)  18 us
    psum x1, blocking collectives, on_device(): lax.psum((jnp.sum(vector * vector), jnp.sum(vector * sigma)), ('term', 'p...  16.6 us
  transfers between devices with their start and end apart: 4, of which 4 were waited for; matrix products, arithmetic and copies ran while one was open for 0% of the time, Pallas kernels for 0%

commit v1 on v0

v1 whole, which is shorter than its diff:
```python
import functools

import jax
import jax.numpy as jnp
from jax import lax
from jax.experimental import pallas as pl
from jax.experimental.pallas import tpu as pltpu
from jax.sharding import PartitionSpec as P

unroll_slots = 4
vmem_bytes = 48 * 1024 * 1024
whole_vmem = pl.BlockSpec(memory_space=pltpu.VMEM)
whole_smem = pl.BlockSpec(memory_space=pltpu.SMEM)


def plan_kernel(
    sectors, rights, lefts, me_ref, left_ref, right_ref, source_ref, target_ref, count_ref, plan_ref, next_ref
):
    me = me_ref[0]
    live = count_ref[0]
    groups = sectors * rights

    def group_of(slot):
        return (target_ref[0, slot] ^ me) * rights + right_ref[0, slot]

    def clear(group, carry):
        next_ref[group] = 0
        return carry

    def count(slot, carry):
        group = group_of(slot)
        next_ref[group] = next_ref[group] + 1
        return carry

    def start(group, total):
        size = next_ref[group]
        next_ref[group] = total
        return total + size

    def fill(slot, carry):
        group = group_of(slot)
        place = next_ref[group]
        next_ref[group] = place + 1
        half = (source_ref[0, slot] ^ me) * lefts + left_ref[0, slot]
        plan_ref[place] = half + group * 4096
        return carry

    def pad(place, carry):
        plan_ref[place] = groups * 4096
        return carry

    def mark(back, carry):
        place = live - 1 - back
        word = plan_ref[place]
        before = plan_ref[jnp.maximum(place - 1, 0)]
        same = (place > 0) & ((word // 4096) == (before // 4096))
        plan_ref[place] = word + jnp.where(same, 1 << 24, 0)
        return carry

    lax.fori_loop(0, groups, clear, 0)
    lax.fori_loop(0, live, count, 0)
    lax.fori_loop(0, groups, start, 0)
    lax.fori_loop(0, live, fill, 0)
    lax.fori_loop(live, plan_ref.shape[0], pad, 0)
    lax.fori_loop(0, live, mark, 0)


def make_plan(me, indices, block_count, sectors, lefts, rights):
    slots = indices[0].shape[1]
    padded = -(-slots // unroll_slots) * unroll_slots
    return pl.pallas_call(
        functools.partial(plan_kernel, sectors, rights, lefts),
        out_shape=jax.ShapeDtypeStruct((padded,), jnp.int32),
        in_specs=[whole_smem] * 6,
        out_specs=whole_smem,
        scratch_shapes=[pltpu.SMEM((sectors * rights,), jnp.int32)],
        cost_estimate=pl.CostEstimate(flops=4000000, bytes_accessed=4000000, transcendentals=0),
    )(me, *indices, block_count)


def multiply(sectors, live, plan_ref, left_ref, right_ref, vector, halves, sums, out_refs):
    lefts, half_rows, columns = left_ref.shape
    rights = right_ref.shape[0] // columns
    left_all = left_ref[...].reshape(lefts * half_rows, columns)
    sums[...] = jnp.zeros_like(sums)
    for j in range(sectors):
        half = jnp.dot(left_all, vector[j], preferred_element_type=jnp.float32)
        halves[j * lefts : (j + 1) * lefts] = half.astype(jnp.bfloat16).reshape(lefts, half_rows, columns)

    def some_slots(turn, total):
        for step in range(unroll_slots):
            word = plan_ref[turn * unroll_slots + step]
            half = word & 4095
            group = (word >> 12) & 4095
            keep = (word >> 24).astype(jnp.float32)
            row = pl.multiple_of((group // rights) * half_rows, half_rows)
            column = pl.multiple_of((group % rights) * columns, columns)
            total = total * keep + halves[half].astype(jnp.float32)
            sums[pl.ds(row, half_rows), pl.ds(column, columns)] = total.astype(jnp.bfloat16)
        return total

    turns = (live + unroll_slots - 1) // unroll_slots
    lax.fori_loop(0, turns, some_slots, jnp.zeros((half_rows, columns), jnp.float32))
    product = jnp.dot(sums[: sectors * half_rows], right_ref[...], preferred_element_type=jnp.float32)
    for j in range(sectors):
        out_refs[j][...] = product[j * half_rows : (j + 1) * half_rows].astype(out_refs[j].dtype)


def join(core, vector, j, mine, other):
    rows = mine.shape[0]
    vector[j, pl.ds(pl.multiple_of(core * rows, rows), rows)] = mine
    vector[j, pl.ds(pl.multiple_of((1 - core) * rows, rows), rows)] = other


def first_kernel(sectors, core_ref, count_ref, plan_ref, left_ref, right_ref, *refs):
    mine, other = refs[:sectors], refs[sectors : 2 * sectors]
    out_refs = refs[2 * sectors : 3 * sectors]
    vector, halves, sums = refs[3 * sectors :]
    for j in range(sectors):
        join(core_ref[0], vector, j, mine[j][...], other[j][...])
    multiply(sectors, count_ref[0], plan_ref, left_ref, right_ref, vector, halves, sums, out_refs)


def second_kernel(sectors, core_ref, count_ref, plan_ref, left_ref, right_ref, *refs):
    pieces = 2 * sectors
    psis, sigmas = refs[:pieces], refs[pieces : 2 * pieces]
    out_refs = refs[2 * pieces : 2 * pieces + sectors]
    own_ref = refs[2 * pieces + sectors]
    vector, halves, sums = refs[2 * pieces + sectors + 1 :]

    def wide(ref):
        return ref[...].astype(jnp.float32)

    norm = sum(wide(p) * wide(p) for p in psis)
    correlation = sum(wide(p) * wide(s) for p, s in zip(psis, sigmas))
    theta = jnp.sum(correlation) / jnp.sum(norm)
    square = jnp.zeros_like(norm)
    for p, s in zip(psis, sigmas):
        resid = wide(s) - theta * wide(p)
        square = square + resid * resid
    entries = pieces * norm.shape[0] * norm.shape[1]
    scale = lax.rsqrt(jnp.sum(square) / entries + 1e-06)
    for j in range(sectors):
        mine, other = (
            ((wide(sigmas[i]) - theta * wide(psis[i])) * scale).astype(jnp.bfloat16) for i in (j, sectors + j)
        )
        if j == 0:
            own_ref[...] = mine
        join(core_ref[0], vector, j, mine, other)
    multiply(sectors, count_ref[0], plan_ref, left_ref, right_ref, vector, halves, sums, out_refs)


def call_product(kernel, sectors, scalars, left, right, pieces, gives_own):
    lefts, half_rows, columns = left.shape
    rights = right.shape[0] // columns
    shape = (half_rows, columns)
    outs = [jax.ShapeDtypeStruct(shape, jnp.float32)]
    outs += [jax.ShapeDtypeStruct(shape, jnp.bfloat16)] * (sectors - 1 + gives_own)
    return pl.pallas_call(
        functools.partial(kernel, sectors),
        out_shape=outs,
        in_specs=[whole_smem] * len(scalars) + [whole_vmem] * (2 + len(pieces)),
        out_specs=[whole_vmem] * len(outs),
        scratch_shapes=[
            pltpu.VMEM((sectors, 2 * half_rows, columns), jnp.bfloat16),
            pltpu.VMEM((sectors * lefts, half_rows, columns), jnp.bfloat16),
            pltpu.VMEM(((sectors + 1) * half_rows, rights * columns), jnp.bfloat16),
        ],
        compiler_params=pltpu.CompilerParams(vmem_limit_bytes=vmem_bytes),
    )(*scalars, left, right, *pieces)


def swap(value, axis, bit):
    return lax.ppermute(value, axis, [(i, i ^ bit) for i in range(lax.axis_size(axis))])


def gather(own):
    sectors = lax.axis_size("term")
    mine = {0: own}
    for j in reversed(range(1, sectors)):
        mine[j] = swap(own, "term", j)
    other = {j: swap(mine[j], "pair", 1) for j in (0, *reversed(range(1, sectors)))}
    return [mine[j] for j in range(sectors)] + [other[j] for j in range(sectors)]


def owner_sum(parts):
    sent = {j: swap(parts[j], "term", j) for j in reversed(range(1, len(parts)))}
    total = parts[0]
    for j in range(1, len(parts)):
        total = total + sent[j].astype(jnp.float32)
    bit = 1
    while bit < lax.axis_size("sub"):
        rounded = total.astype(jnp.bfloat16)
        total = rounded.astype(jnp.float32) + swap(rounded, "sub", bit).astype(jnp.float32)
        bit *= 2
    return total


def on_device(
    psi,
    left_blocks,
    right_blocks,
    left_index,
    right_index,
    block_source,
    block_target,
    block_count,
    sector_energy,
):
    sectors = lax.axis_size("term")
    lefts, rights = left_blocks.shape[1], right_blocks.shape[1]
    me = lax.axis_index("term").astype(jnp.int32).reshape(1)
    core = lax.axis_index("pair").astype(jnp.int32).reshape(1)
    left = left_blocks[0]
    right = jnp.swapaxes(right_blocks[0], 1, 2).reshape(-1, right_blocks.shape[2])
    own = psi[0]
    psis = gather(own)
    plan = make_plan(
        me, (left_index, right_index, block_source, block_target), block_count, sectors, lefts, rights
    )
    scalars = (core, block_count, plan)
    parts = call_product(first_kernel, sectors, scalars, left, right, psis, False)
    energy = sector_energy[0]
    sigma_first = (owner_sum(parts) + energy * own.astype(jnp.float32)).astype(jnp.bfloat16)
    *parts, correction = call_product(
        second_kernel, sectors, scalars, left, right, psis + gather(sigma_first), True
    )
    sigma_second = (owner_sum(parts) + energy * correction.astype(jnp.float32)).astype(jnp.bfloat16)
    return (sigma_first[None], sigma_second[None])


def solution(mesh):
    placed = (
        P(("grp", "term"), "pair", None),
        P(("grp", "term", "sub"), None, "pair", None),
        P(("grp", "term", "sub"), None, None, None),
        P(("grp", "term", "sub"), None),
        P(("grp", "term", "sub"), None),
        P(("grp", "term", "sub"), None),
        P(("grp", "term", "sub"), None),
        P(("grp", "term", "sub")),
        P(("grp", "term")),
    )
    return jax.shard_map(
        on_device,
        mesh=mesh,
        in_specs=placed,
        out_specs=(P(("grp", "term"), "pair", None), P(("grp", "term"), "pair", None)),
        check_vma=False,
    )
```

time: 369 us -> 65.5 us (0.18)
  waiting for transfers between devices: 150 us -> 26.6 us
  blocking collectives: 62.8 us -> 0 us
  local copies, waits for them, and re-layouts: 53.1 us -> 2.19 us
  other arithmetic: 44 us -> 0.77 us
  matrix products: 38.7 us -> 0 us
  starting transfers between devices: 0.16 us -> 22 us
  between operations: 17.4 us -> 2.08 us
  Pallas kernels: 0 us -> 11.9 us
    reduce_scatter x2 -> x0, waiting for transfers between devices: 107 us -> none  [owner_sigma(): lax.psum_scatter(partial_sum, 'term', scatter_dimension=0, tiled=True)]
    gather x36 -> x0, local copies, waits for them, and re-layouts: 50.8 us -> none  [the longest x12 19.2 us: one_turn(): right_part = jnp.take(rights, pick_right, axis=0)]
    psum x2 -> x0, waiting for transfers between devices: 43.2 us -> none  [owner_sigma(): partial_sum = lax.psum(totals, 'sub')]
    dot_general x12 -> x0, matrix products: 38.7 us -> none  [one_turn(): jnp.einsum('kil,kml->kim', half, right_part, preferred_element_type=jnp.f...]
    all_gather x2 -> x0, blocking collectives: 31.9 us -> none  [gather_sectors(): pieces = lax.all_gather(vector, ('term', 'pair'), axis=1, tiled=True)]
    psum x2 -> x0, blocking collectives: 30.9 us -> none  [the longest x1 16.6 us: on_device(): lax.psum((jnp.sum(vector * vector), jnp.sum(vector * sigma)), ('term', 'p...]
    scatter-add x12 -> x0, other arithmetic: 29.4 us -> none  [one_turn(): return totals.at[pick_target].add(product * alive[:, None, None])]
    ppermute x0 -> x22, waiting for transfers between devices: none -> 26.6 us  [swap(): lax.ppermute(value, axis, [(i, i ^ bit) for i in range(lax.axis_size(axis...]
  transfers between devices with their start and end apart: 4 -> 22, of which waited for: 4 -> 13; matrix products, arithmetic and copies ran while one was open for 0% -> 2% of each run, Pallas kernels for 0% -> 5%
where the time goes in v1:
time: 65.5 us; the launch traced here: 65.6 us
  waiting for transfers between devices  26.6 us (41%)
  starting transfers between devices  22 us (34%)
  Pallas kernels  11.9 us (18%)
  local copies, waits for them, and re-layouts  2.19 us (3%)
  between operations  2.08 us (3%)
  other arithmetic  0.77 us (1%)
    ppermute x22, waiting for transfers between devices, swap(): lax.ppermute(value, axis, [(i, i ^ bit) for i in range(lax.axis_size(axis...  26.6 us
    ppermute x22, starting transfers between devices, swap(): lax.ppermute(value, axis, [(i, i ^ bit) for i in range(lax.axis_size(axis...  22 us
    pallas_call x2, Pallas kernels, call_product(): pl.pallas_call(functools.partial(kernel, sectors), out_shape=outs, in_spe...  8.64 us
    pallas_call x1, Pallas kernels, make_plan(): pl.pallas_call(functools.partial(plan_kernel, sectors, rights, lefts), ou...  3.25 us
    transpose x1, local copies, waits for them, and re-layouts, on_device(): jnp.swapaxes(right_blocks[0], 1, 2).reshape(-1, right_blocks.shape[2])  1.54 us
  transfers between devices with their start and end apart: 22, of which 13 were waited for; matrix products, arithmetic and copies ran while one was open for 2% of the time, Pallas kernels for 5%

profile of v1, /device:TPU:0, one launch (start us, length us, event | category | flops | bytes accessed | tf_op | source)
XLA Modules:
  0.0 65.6 jit_solution(17681030948098131462)
XLA Ops:
  0.6 5.1 %collective-permute-start.2 = (bf16[128,256]{1,0:T(8,128)(2,1)}, bf16[128,256]{1,0:T(8,128)(2,1)S(1)}, u32[]{:S(2)}, u32[]{:S(2)}) collective-permute-start(bf16[128,256]{1,0:T(8,128)(2,1)} %bitcast.19), channel_id=1, source_target_pairs={{0,12},{4,8},{8,4},{12,0},{1,13},{5,9},{9,5},{13,1},{2,14},{6,10},... | collective-permute-start | bytes 196616 | tf_op jit(solution)/shard_map/ppermute | solution.py:174
  5.7 0.6 collective-permute-start
  6.4 2.2 %collective-permute-done.2.refs_3_ = bf16[128,256]{1,0:T(8,128)(2,1)S(1)} collective-permute-done((bf16[128,256]{1,0:T(8,128)(2,1)}, bf16[128,256]{1,0:T(8,128)(2,1)S(1)}, u32[]{:S(2)}, u32[]{:S(2)}) %collective-permute-start.2) | collective-permute-done | bytes 65568 | tf_op jit(solution)/shard_map/ppermute | solution.py:174
  8.6 3.0 %collective-permute-done.1.refs_2_ = bf16[128,256]{1,0:T(8,128)(2,1)S(1)} collective-permute-done((bf16[128,256]{1,0:T(8,128)(2,1)}, bf16[128,256]{1,0:T(8,128)(2,1)S(1)}, u32[]{:S(2)}, u32[]{:S(2)}) %collective-permute-start.1) | collective-permute-done | bytes 65568 | tf_op jit(solution)/shard_map/ppermute | solution.py:174
  11.6 0.5 collective-permute-start.4
  12.7 1.5 %copy.11 = bf16[8,256,256]{2,1,0:T(8,128)(2,1)S(1)} copy(bf16[8,256,256]{1,2,0:T(8,128)(2,1)} %bitcast.26) | data formatting | bytes 2097152 | tf_op jit(solution)/shard_map/transpose | solution.py:215
  14.3 3.2 %shard_map.104.plan_ref = s32[72]{0:T(128)} custom-call(s32[1]{0:T(128)} %bitcast.1.me_ref, s32[1,72]{1,0:T(1,128)} %left_ref.1, s32[1,72]{1,0:T(1,128)} %right_ref.1, s32[1,72]{1,0:T(1,128)} %source_ref.1, s32[1,72]{1,0:T(1,128)} %target_ref.1, s32[1]{0:T(128)S(6)} %copy.12.count_ref), custom_call_target="tpu_custom_call" | custom-call | flops 4000000 | bytes 4000000 | tf_op jit(solution)/shard_map/pallas_call | solution.py:71
  17.6 0.6 copy-done.3
  18.3 3.9 %shard_map.105 = (f32[128,256]{1,0:T(8,128)S(1)}, bf16[128,256]{1,0:T(8,128)(2,1)S(1)}, bf16[128,256]{1,0:T(8,128)(2,1)S(1)}, bf16[128,256]{1,0:T(8,128)(2,1)S(1)}) custom-call(s32[1]{0:T(128)} %bitcast.core_ref, s32[1]{0:T(128)S(6)} %copy.12.count_ref, s32[72]{0:T(128)S(1)} %copy-done.3, bf16[8,128,256]{2,1,0:T(8,128)(2,1)S(1)} %bitcast.17, ...), custom_call_target="tpu_custom_call" | custom-call | tf_op jit(solution)/shard_map/pallas_call | solution.py:159
  22.2 2.3 %collective-permute-start.7 = (bf16[128,256]{1,0:T(8,128)(2,1)S(1)}, bf16[128,256]{1,0:T(8,128)(2,1)S(1)}, u32[]{:S(2)}, u32[]{:S(2)}) collective-permute-start(bf16[128,256]{1,0:T(8,128)(2,1)S(1)} %get-tuple-element.12), channel_id=1, source_target_pairs={{0,4},{4,0},{8,12},{12,8},{1,5},{5,1},{9,13},{13,9},{2,6},{6,2},{1... | collective-permute-start | bytes 196616 | tf_op jit(solution)/shard_map/ppermute | solution.py:174
  24.5 1.2 %collective-permute-start.8 = (bf16[128,256]{1,0:T(8,128)(2,1)S(1)}, bf16[128,256]{1,0:T(8,128)(2,1)S(1)}, u32[]{:S(2)}, u32[]{:S(2)}) collective-permute-start(bf16[128,256]{1,0:T(8,128)(2,1)S(1)} %get-tuple-element.13), channel_id=1, source_target_pairs={{0,8},{4,12},{8,0},{12,4},{1,9},{5,13},{9,1},{13,5},{2,10},{6,14},... | collective-permute-start | bytes 196616 | tf_op jit(solution)/shard_map/ppermute | solution.py:174
  25.7 1.2 %collective-permute-start.9 = (bf16[128,256]{1,0:T(8,128)(2,1)S(1)}, bf16[128,256]{1,0:T(8,128)(2,1)S(1)}, u32[]{:S(2)}, u32[]{:S(2)}) collective-permute-start(bf16[128,256]{1,0:T(8,128)(2,1)S(1)} %get-tuple-element.14), channel_id=1, source_target_pairs={{0,12},{4,8},{8,4},{12,0},{1,13},{5,9},{9,5},{13,1},{2,14},{6,10},... | collective-permute-start | bytes 196616 | tf_op jit(solution)/shard_map/ppermute | solution.py:174
  26.9 0.3 collective-permute-done.7
  27.3 5.0 %collective-permute-done.8 = bf16[128,256]{1,0:T(8,128)(2,1)S(1)} collective-permute-done((bf16[128,256]{1,0:T(8,128)(2,1)S(1)}, bf16[128,256]{1,0:T(8,128)(2,1)S(1)}, u32[]{:S(2)}, u32[]{:S(2)}) %collective-permute-start.8) | collective-permute-done | bytes 65568 | tf_op jit(solution)/shard_map/ppermute | solution.py:174
  32.3 1.2 %collective-permute-start.10 = (bf16[128,256]{1,0:T(8,128)(2,1)S(1)}, bf16[128,256]{1,0:T(8,128)(2,1)S(1)}, u32[]{:S(2)}, u32[]{:S(2)}) collective-permute-start(bf16[128,256]{1,0:T(8,128)(2,1)S(1)} %add_convert_fusion.3), channel_id=1, source_target_pairs={{0,2},{2,0},{1,3},{3,1},{4,6},{6,4},{5,7},{7,5},{8,10},{10,8},{9,1... | collective-permute-start | bytes 196616 | tf_op jit(solution)/shard_map/ppermute | solution.py:174
  34.2 2.5 %collective-permute-done.10 = bf16[128,256]{1,0:T(8,128)(2,1)S(1)} collective-permute-done((bf16[128,256]{1,0:T(8,128)(2,1)S(1)}, bf16[128,256]{1,0:T(8,128)(2,1)S(1)}, u32[]{:S(2)}, u32[]{:S(2)}) %collective-permute-start.10) | collective-permute-done | bytes 65568 | tf_op jit(solution)/shard_map/ppermute | solution.py:174
  36.7 1.5 %collective-permute-start.13 = (bf16[128,256]{1,0:T(8,128)(2,1)S(1)}, bf16[128,256]{1,0:T(8,128)(2,1)S(1)}, u32[]{:S(2)}, u32[]{:S(2)}) collective-permute-start(bf16[128,256]{1,0:T(8,128)(2,1)S(1)} %add_convert_fusion.2.refs_8_), channel_id=1, source_target_pairs={{0,12},{4,8},{8,4},{12,0},{1,13},{5,9},{9,5},{13,1},{2,14},{6,10},... | collective-permute-start | bytes 196616 | tf_op jit(solution)/shard_map/ppermute | solution.py:174
  38.2 1.9 %collective-permute-start.12 = (bf16[128,256]{1,0:T(8,128)(2,1)S(1)}, bf16[128,256]{1,0:T(8,128)(2,1)S(1)}, u32[]{:S(2)}, u32[]{:S(2)}) collective-permute-start(bf16[128,256]{1,0:T(8,128)(2,1)S(1)} %add_convert_fusion.2.refs_8_), channel_id=1, source_target_pairs={{0,8},{4,12},{8,0},{12,4},{1,9},{5,13},{9,1},{13,5},{2,10},{6,14},... | collective-permute-start | bytes 196616 | tf_op jit(solution)/shard_map/ppermute | solution.py:174
  40.1 1.0 %collective-permute-start.11 = (bf16[128,256]{1,0:T(8,128)(2,1)S(1)}, bf16[128,256]{1,0:T(8,128)(2,1)S(1)}, u32[]{:S(2)}, u32[]{:S(2)}) collective-permute-start(bf16[128,256]{1,0:T(8,128)(2,1)S(1)} %add_convert_fusion.2.refs_8_), channel_id=1, source_target_pairs={{0,4},{4,0},{8,12},{12,8},{1,5},{5,1},{9,13},{13,9},{2,6},{6,2},{1... | collective-permute-start | bytes 196616 | tf_op jit(solution)/shard_map/ppermute | solution.py:174
  41.2 1.8 %collective-permute-done.13.refs_11_ = bf16[128,256]{1,0:T(8,128)(2,1)S(1)} collective-permute-done((bf16[128,256]{1,0:T(8,128)(2,1)S(1)}, bf16[128,256]{1,0:T(8,128)(2,1)S(1)}, u32[]{:S(2)}, u32[]{:S(2)}) %collective-permute-start.13) | collective-permute-done | bytes 65568 | tf_op jit(solution)/shard_map/ppermute | solution.py:174
  43.0 2.4 %collective-permute-done.12.refs_10_ = bf16[128,256]{1,0:T(8,128)(2,1)S(1)} collective-permute-done((bf16[128,256]{1,0:T(8,128)(2,1)S(1)}, bf16[128,256]{1,0:T(8,128)(2,1)S(1)}, u32[]{:S(2)}, u32[]{:S(2)}) %collective-permute-start.12) | collective-permute-done | bytes 65568 | tf_op jit(solution)/shard_map/ppermute | solution.py:174
  45.5 0.3 collective-permute-start.15
  45.9 0.7 %collective-permute-done.16.refs_14_ = bf16[128,256]{1,0:T(8,128)(2,1)S(1)} collective-permute-done((bf16[128,256]{1,0:T(8,128)(2,1)S(1)}, bf16[128,256]{1,0:T(8,128)(2,1)S(1)}, u32[]{:S(2)}, u32[]{:S(2)}) %collective-permute-start.16) | collective-permute-done | bytes 65568 | tf_op jit(solution)/shard_map/ppermute | solution.py:174
  46.8 4.7 %shard_map.106 = (f32[128,256]{1,0:T(8,128)S(1)}, bf16[128,256]{1,0:T(8,128)(2,1)S(1)}, bf16[128,256]{1,0:T(8,128)(2,1)S(1)}, bf16[128,256]{1,0:T(8,128)(2,1)S(1)}, bf16[128,256]{1,0:T(8,128)(2,1)S(1)}) custom-call(s32[1]{0:T(128)} %bitcast.core_ref, s32[1]{0:T(128)S(6)} %copy.12.count_ref, s32[72]{0:T(128)S(1)} %copy-done.3, ...), custom_call_target="tpu_custom_call" | custom-call | tf_op jit(solution)/shard_map/pallas_call | solution.py:159
  51.5 0.8 %collective-permute-start.18 = (bf16[128,256]{1,0:T(8,128)(2,1)S(1)}, bf16[128,256]{1,0:T(8,128)(2,1)S(1)}, u32[]{:S(2)}, u32[]{:S(2)}) collective-permute-start(bf16[128,256]{1,0:T(8,128)(2,1)S(1)} %get-tuple-element.16), channel_id=1, source_target_pairs={{0,4},{4,0},{8,12},{12,8},{1,5},{5,1},{9,13},{13,9},{2,6},{6,2},{1... | collective-permute-start | bytes 196616 | tf_op jit(solution)/shard_map/ppermute | solution.py:174
  52.3 1.4 %collective-permute-start.19 = (bf16[128,256]{1,0:T(8,128)(2,1)S(1)}, bf16[128,256]{1,0:T(8,128)(2,1)S(1)}, u32[]{:S(2)}, u32[]{:S(2)}) collective-permute-start(bf16[128,256]{1,0:T(8,128)(2,1)S(1)} %get-tuple-element.17), channel_id=1, source_target_pairs={{0,8},{4,12},{8,0},{12,4},{1,9},{5,13},{9,1},{13,5},{2,10},{6,14},... | collective-permute-start | bytes 196616 | tf_op jit(solution)/shard_map/ppermute | solution.py:174
  53.7 2.2 %collective-permute-start.20 = (bf16[128,256]{1,0:T(8,128)(2,1)S(1)}, bf16[128,256]{1,0:T(8,128)(2,1)S(1)}, u32[]{:S(2)}, u32[]{:S(2)}) collective-permute-start(bf16[128,256]{1,0:T(8,128)(2,1)S(1)} %get-tuple-element.18), channel_id=1, source_target_pairs={{0,12},{4,8},{8,4},{12,0},{1,13},{5,9},{9,5},{13,1},{2,14},{6,10},... | collective-permute-start | bytes 196616 | tf_op jit(solution)/shard_map/ppermute | solution.py:174
  55.9 0.7 %collective-permute-done.18 = bf16[128,256]{1,0:T(8,128)(2,1)S(1)} collective-permute-done((bf16[128,256]{1,0:T(8,128)(2,1)S(1)}, bf16[128,256]{1,0:T(8,128)(2,1)S(1)}, u32[]{:S(2)}, u32[]{:S(2)}) %collective-permute-start.18) | collective-permute-done | bytes 65568 | tf_op jit(solution)/shard_map/ppermute | solution.py:174
  56.6 4.0 %collective-permute-done.19 = bf16[128,256]{1,0:T(8,128)(2,1)S(1)} collective-permute-done((bf16[128,256]{1,0:T(8,128)(2,1)S(1)}, bf16[128,256]{1,0:T(8,128)(2,1)S(1)}, u32[]{:S(2)}, u32[]{:S(2)}) %collective-permute-start.19) | collective-permute-done | bytes 65568 | tf_op jit(solution)/shard_map/ppermute | solution.py:174
  60.6 0.6 collective-permute-start.21
  61.2 3.8 %collective-permute-done.21 = bf16[128,256]{1,0:T(8,128)(2,1)S(1)} collective-permute-done((bf16[128,256]{1,0:T(8,128)(2,1)S(1)}, bf16[128,256]{1,0:T(8,128)(2,1)S(1)}, u32[]{:S(2)}, u32[]{:S(2)}) %collective-permute-start.21) | collective-permute-done | bytes 65568 | tf_op jit(solution)/shard_map/ppermute | solution.py:174
  64.9 0.7 %fusion = bf16[1,128,256]{2,1,0:T(8,128)(2,1)} fusion(bf16[128,256]{1,0:T(8,128)(2,1)S(1)} %get-tuple-element.19, bf16[128,256]{1,0:T(8,128)(2,1)S(1)} %collective-permute-done.21, bf16[128,256]{1,0:T(8,128)(2,1)S(1)} %add_convert_fusion.1, f32[]{:T(128)} %bitcast.14), kind=kLoop, calls=%fused_computation.4 | loop fusion | flops 229376 | bytes 262148 | tf_op jit(solution)/shard_map/broadcast_in_dim | solution.py:229
  (28 shorter events, 0.5 us)
Async XLA Ops:
  0.6 7.9 %collective-permute-start.2 = (bf16[128,256]{1,0:T(8,128)(2,1)}, bf16[128,256]{1,0:T(8,128)(2,1)S(1)}, u32[]{:S(2)}, u32[]{:S(2)}) collective-permute-start(bf16[128,256]{1,0:T(8,128)(2,1)} %bitcast.19), channel_id=1, source_target_pairs={{0,12},{4,8},{8,4},{12,0},{1,13},{5,9},{9,5},{13,1},{2,14},{6,10},... | collective-permute-start | bytes 196616 | tf_op jit(solution)/shard_map/ppermute | solution.py:174
  5.7 5.8 %collective-permute-start.1 = (bf16[128,256]{1,0:T(8,128)(2,1)}, bf16[128,256]{1,0:T(8,128)(2,1)S(1)}, u32[]{:S(2)}, u32[]{:S(2)}) collective-permute-start(bf16[128,256]{1,0:T(8,128)(2,1)} %bitcast.20), channel_id=1, source_target_pairs={{0,8},{4,12},{8,0},{12,4},{1,9},{5,13},{9,1},{13,5},{2,10},{6,14},... | collective-permute-start | bytes 196616 | tf_op jit(solution)/shard_map/ppermute | solution.py:174
  5.7 5.8 %collective-permute-start = (bf16[128,256]{1,0:T(8,128)(2,1)}, bf16[128,256]{1,0:T(8,128)(2,1)S(1)}, u32[]{:S(2)}, u32[]{:S(2)}) collective-permute-start(bf16[128,256]{1,0:T(8,128)(2,1)} %bitcast.21), channel_id=1, source_target_pairs={{0,4},{4,0},{8,12},{12,8},{1,5},{5,1},{9,13},{13,9},{2,6},{6,2},{1... | collective-permute-start | bytes 196616 | tf_op jit(solution)/shard_map/ppermute | solution.py:174
  6.4 11.2 %collective-permute-start.3 = (bf16[128,256]{1,0:T(8,128)(2,1)}, bf16[128,256]{1,0:T(8,128)(2,1)S(1)}, u32[]{:S(2)}, u32[]{:S(2)}) collective-permute-start(bf16[128,256]{1,0:T(8,128)(2,1)} %bitcast.22), channel_id=1, source_target_pairs={{0,1},{1,0},{2,3},{3,2},{4,5},{5,4},{6,7},{7,6},{8,9},{9,8},{10,11... | collective-permute-start | bytes 196616 | tf_op jit(solution)/shard_map/ppermute | solution.py:174
  8.6 9.0 %collective-permute-start.6 = (bf16[128,256]{1,0:T(8,128)(2,1)S(1)}, bf16[128,256]{1,0:T(8,128)(2,1)S(1)}, u32[]{:S(2)}, u32[]{:S(2)}) collective-permute-start(bf16[128,256]{1,0:T(8,128)(2,1)S(1)} %collective-permute-done.2.refs_3_), channel_id=1, source_target_pairs={{0,1},{1,0},{2,3},{3,2},{4,5},{5,4},{6,7},{7,6},{8,9},{9,8},{10,11... | collective-permute-start | bytes 196616 | tf_op jit(solution)/shard_map/ppermute | solution.py:174
  11.6 6.0 %collective-permute-start.5 = (bf16[128,256]{1,0:T(8,128)(2,1)S(1)}, bf16[128,256]{1,0:T(8,128)(2,1)S(1)}, u32[]{:S(2)}, u32[]{:S(2)}) collective-permute-start(bf16[128,256]{1,0:T(8,128)(2,1)S(1)} %collective-permute-done.1.refs_2_), channel_id=1, source_target_pairs={{0,1},{1,0},{2,3},{3,2},{4,5},{5,4},{6,7},{7,6},{8,9},{9,8},{10,11... | collective-permute-start | bytes 196616 | tf_op jit(solution)/shard_map/ppermute | solution.py:174
  11.6 6.0 %collective-permute-start.4 = (bf16[128,256]{1,0:T(8,128)(2,1)S(1)}, bf16[128,256]{1,0:T(8,128)(2,1)S(1)}, u32[]{:S(2)}, u32[]{:S(2)}) collective-permute-start(bf16[128,256]{1,0:T(8,128)(2,1)S(1)} %collective-permute-done.refs_1_), channel_id=1, source_target_pairs={{0,1},{1,0},{2,3},{3,2},{4,5},{5,4},{6,7},{7,6},{8,9},{9,8},{10,11... | collective-permute-start | bytes 196616 | tf_op jit(solution)/shard_map/ppermute | solution.py:174
  12.7 4.9 %copy-start = (bf16[1,8,128,256]{3,2,1,0:T(8,128)(2,1)S(1)}, bf16[1,8,128,256]{3,2,1,0:T(8,128)(2,1)}, u32[]{:S(2)}) copy-start(bf16[1,8,128,256]{3,2,1,0:T(8,128)(2,1)} %param.10) | copy-start | bytes 1572868
  12.7 4.9 %copy-start.1 = (bf16[1,128,256]{2,1,0:T(8,128)(2,1)S(1)}, bf16[1,128,256]{2,1,0:T(8,128)(2,1)}, u32[]{:S(2)}) copy-start(bf16[1,128,256]{2,1,0:T(8,128)(2,1)} %param.9) | copy-start | bytes 196612
  17.6 0.7 %copy-start.3 = (s32[72]{0:T(128)S(1)}, s32[72]{0:T(128)}, u32[]{:S(2)}) copy-start(s32[72]{0:T(128)} %shard_map.104.plan_ref) | copy-start | bytes 868
  22.2 5.1 %collective-permute-start.7 = (bf16[128,256]{1,0:T(8,128)(2,1)S(1)}, bf16[128,256]{1,0:T(8,128)(2,1)S(1)}, u32[]{:S(2)}, u32[]{:S(2)}) collective-permute-start(bf16[128,256]{1,0:T(8,128)(2,1)S(1)} %get-tuple-element.12), channel_id=1, source_target_pairs={{0,4},{4,0},{8,12},{12,8},{1,5},{5,1},{9,13},{13,9},{2,6},{6,2},{1... | collective-permute-start | bytes 196616 | tf_op jit(solution)/shard_map/ppermute | solution.py:174
  24.5 7.8 %collective-permute-start.8 = (bf16[128,256]{1,0:T(8,128)(2,1)S(1)}, bf16[128,256]{1,0:T(8,128)(2,1)S(1)}, u32[]{:S(2)}, u32[]{:S(2)}) collective-permute-start(bf16[128,256]{1,0:T(8,128)(2,1)S(1)} %get-tuple-element.13), channel_id=1, source_target_pairs={{0,8},{4,12},{8,0},{12,4},{1,9},{5,13},{9,1},{13,5},{2,10},{6,14},... | collective-permute-start | bytes 196616 | tf_op jit(solution)/shard_map/ppermute | solution.py:174
  25.7 6.5 %collective-permute-start.9 = (bf16[128,256]{1,0:T(8,128)(2,1)S(1)}, bf16[128,256]{1,0:T(8,128)(2,1)S(1)}, u32[]{:S(2)}, u32[]{:S(2)}) collective-permute-start(bf16[128,256]{1,0:T(8,128)(2,1)S(1)} %get-tuple-element.14), channel_id=1, source_target_pairs={{0,12},{4,8},{8,4},{12,0},{1,13},{5,9},{9,5},{13,1},{2,14},{6,10},... | collective-permute-start | bytes 196616 | tf_op jit(solution)/shard_map/ppermute | solution.py:174
  32.3 4.3 %collective-permute-start.10 = (bf16[128,256]{1,0:T(8,128)(2,1)S(1)}, bf16[128,256]{1,0:T(8,128)(2,1)S(1)}, u32[]{:S(2)}, u32[]{:S(2)}) collective-permute-start(bf16[128,256]{1,0:T(8,128)(2,1)S(1)} %add_convert_fusion.3), channel_id=1, source_target_pairs={{0,2},{2,0},{1,3},{3,1},{4,6},{6,4},{5,7},{7,5},{8,10},{10,8},{9,1... | collective-permute-start | bytes 196616 | tf_op jit(solution)/shard_map/ppermute | solution.py:174
  36.7 14.8 %copy-start.2 = (bf16[128,256]{1,0:T(8,128)(2,1)}, bf16[128,256]{1,0:T(8,128)(2,1)S(1)}, u32[]{:S(2)}) copy-start(bf16[128,256]{1,0:T(8,128)(2,1)S(1)} %add_convert_fusion.2.refs_8_) | copy-start | bytes 196612
  36.7 6.2 %collective-permute-start.13 = (bf16[128,256]{1,0:T(8,128)(2,1)S(1)}, bf16[128,256]{1,0:T(8,128)(2,1)S(1)}, u32[]{:S(2)}, u32[]{:S(2)}) collective-permute-start(bf16[128,256]{1,0:T(8,128)(2,1)S(1)} %add_convert_fusion.2.refs_8_), channel_id=1, source_target_pairs={{0,12},{4,8},{8,4},{12,0},{1,13},{5,9},{9,5},{13,1},{2,14},{6,10},... | collective-permute-start | bytes 196616 | tf_op jit(solution)/shard_map/ppermute | solution.py:174
  38.2 7.1 %collective-permute-start.12 = (bf16[128,256]{1,0:T(8,128)(2,1)S(1)}, bf16[128,256]{1,0:T(8,128)(2,1)S(1)}, u32[]{:S(2)}, u32[]{:S(2)}) collective-permute-start(bf16[128,256]{1,0:T(8,128)(2,1)S(1)} %add_convert_fusion.2.refs_8_), channel_id=1, source_target_pairs={{0,8},{4,12},{8,0},{12,4},{1,9},{5,13},{9,1},{13,5},{2,10},{6,14},... | collective-permute-start | bytes 196616 | tf_op jit(solution)/shard_map/ppermute | solution.py:174
  40.1 5.4 %collective-permute-start.11 = (bf16[128,256]{1,0:T(8,128)(2,1)S(1)}, bf16[128,256]{1,0:T(8,128)(2,1)S(1)}, u32[]{:S(2)}, u32[]{:S(2)}) collective-permute-start(bf16[128,256]{1,0:T(8,128)(2,1)S(1)} %add_convert_fusion.2.refs_8_), channel_id=1, source_target_pairs={{0,4},{4,0},{8,12},{12,8},{1,5},{5,1},{9,13},{13,9},{2,6},{6,2},{1... | collective-permute-start | bytes 196616 | tf_op jit(solution)/shard_map/ppermute | solution.py:174
  41.2 4.7 %collective-permute-start.14 = (bf16[128,256]{1,0:T(8,128)(2,1)S(1)}, bf16[128,256]{1,0:T(8,128)(2,1)S(1)}, u32[]{:S(2)}, u32[]{:S(2)}) collective-permute-start(bf16[128,256]{1,0:T(8,128)(2,1)S(1)} %add_convert_fusion.2.refs_8_), channel_id=1, source_target_pairs={{0,1},{1,0},{2,3},{3,2},{4,5},{5,4},{6,7},{7,6},{8,9},{9,8},{10,11... | collective-permute-start | bytes 196616 | tf_op jit(solution)/shard_map/ppermute | solution.py:174
  43.0 2.9 %collective-permute-start.17 = (bf16[128,256]{1,0:T(8,128)(2,1)S(1)}, bf16[128,256]{1,0:T(8,128)(2,1)S(1)}, u32[]{:S(2)}, u32[]{:S(2)}) collective-permute-start(bf16[128,256]{1,0:T(8,128)(2,1)S(1)} %collective-permute-done.13.refs_11_), channel_id=1, source_target_pairs={{0,1},{1,0},{2,3},{3,2},{4,5},{5,4},{6,7},{7,6},{8,9},{9,8},{10,11... | collective-permute-start | bytes 196616 | tf_op jit(solution)/shard_map/ppermute | solution.py:174
  45.3 1.3 %collective-permute-start.16 = (bf16[128,256]{1,0:T(8,128)(2,1)S(1)}, bf16[128,256]{1,0:T(8,128)(2,1)S(1)}, u32[]{:S(2)}, u32[]{:S(2)}) collective-permute-start(bf16[128,256]{1,0:T(8,128)(2,1)S(1)} %collective-permute-done.12.refs_10_), channel_id=1, source_target_pairs={{0,1},{1,0},{2,3},{3,2},{4,5},{5,4},{6,7},{7,6},{8,9},{9,8},{10,11... | collective-permute-start | bytes 196616 | tf_op jit(solution)/shard_map/ppermute | solution.py:174
  45.5 1.3 %collective-permute-start.15 = (bf16[128,256]{1,0:T(8,128)(2,1)S(1)}, bf16[128,256]{1,0:T(8,128)(2,1)S(1)}, u32[]{:S(2)}, u32[]{:S(2)}) collective-permute-start(bf16[128,256]{1,0:T(8,128)(2,1)S(1)} %collective-permute-done.11.refs_9_), channel_id=1, source_target_pairs={{0,1},{1,0},{2,3},{3,2},{4,5},{5,4},{6,7},{7,6},{8,9},{9,8},{10,11... | collective-permute-start | bytes 196616 | tf_op jit(solution)/shard_map/ppermute | solution.py:174
  51.5 5.1 %collective-permute-start.18 = (bf16[128,256]{1,0:T(8,128)(2,1)S(1)}, bf16[128,256]{1,0:T(8,128)(2,1)S(1)}, u32[]{:S(2)}, u32[]{:S(2)}) collective-permute-start(bf16[128,256]{1,0:T(8,128)(2,1)S(1)} %get-tuple-element.16), channel_id=1, source_target_pairs={{0,4},{4,0},{8,12},{12,8},{1,5},{5,1},{9,13},{13,9},{2,6},{6,2},{1... | collective-permute-start | bytes 196616 | tf_op jit(solution)/shard_map/ppermute | solution.py:174
  52.3 8.3 %collective-permute-start.19 = (bf16[128,256]{1,0:T(8,128)(2,1)S(1)}, bf16[128,256]{1,0:T(8,128)(2,1)S(1)}, u32[]{:S(2)}, u32[]{:S(2)}) collective-permute-start(bf16[128,256]{1,0:T(8,128)(2,1)S(1)} %get-tuple-element.17), channel_id=1, source_target_pairs={{0,8},{4,12},{8,0},{12,4},{1,9},{5,13},{9,1},{13,5},{2,10},{6,14},... | collective-permute-start | bytes 196616 | tf_op jit(solution)/shard_map/ppermute | solution.py:174
  53.7 6.8 %collective-permute-start.20 = (bf16[128,256]{1,0:T(8,128)(2,1)S(1)}, bf16[128,256]{1,0:T(8,128)(2,1)S(1)}, u32[]{:S(2)}, u32[]{:S(2)}) collective-permute-start(bf16[128,256]{1,0:T(8,128)(2,1)S(1)} %get-tuple-element.18), channel_id=1, source_target_pairs={{0,12},{4,8},{8,4},{12,0},{1,13},{5,9},{9,5},{13,1},{2,14},{6,10},... | collective-permute-start | bytes 196616 | tf_op jit(solution)/shard_map/ppermute | solution.py:174
  60.6 4.3 %collective-permute-start.21 = (bf16[128,256]{1,0:T(8,128)(2,1)S(1)}, bf16[128,256]{1,0:T(8,128)(2,1)S(1)}, u32[]{:S(2)}, u32[]{:S(2)}) collective-permute-start(bf16[128,256]{1,0:T(8,128)(2,1)S(1)} %add_convert_fusion.1), channel_id=1, source_target_pairs={{0,2},{2,0},{1,3},{3,1},{4,6},{6,4},{5,7},{7,5},{8,10},{10,8},{9,1... | collective-permute-start | bytes 196616 | tf_op jit(solution)/shard_map/ppermute | solution.py:174

commit v2 on v1

v2 whole, which is shorter than its diff:
```python
import functools

import jax
import jax.numpy as jnp
from jax import lax
from jax.experimental import pallas as pl
from jax.experimental.pallas import tpu as pltpu
from jax.sharding import PartitionSpec as P

unroll_slots = 4
wide_sectors = 4
step_lefts = 2
whole_vmem = pl.BlockSpec(memory_space=pltpu.VMEM)
whole_smem = pl.BlockSpec(memory_space=pltpu.SMEM)
stays_out = pl.BlockSpec(memory_space=pltpu.HBM)


def make_plan(me, left_index, right_index, source, target, live, sectors, lefts, rights):
    slots = left_index.shape[0]
    padded = -(-slots // unroll_slots) * unroll_slots
    number = jnp.arange(slots, dtype=jnp.int32)
    alive = number < live
    group = jnp.where(alive, right_index * sectors + (target ^ me), rights * sectors)
    half = jnp.where(alive, (source ^ me) * lefts + left_index, 0)
    same = group[None, :] == group[:, None]
    before = number[None, :] < number[:, None]
    place = jnp.sum(((group[None, :] < group[:, None]) | (same & before)).astype(jnp.int32), axis=1)
    goes_on = jnp.max((same & before).astype(jnp.int32), axis=1)
    word = half + (group << 12) + (goes_on << 24)
    put = place[None, :] == jnp.arange(padded, dtype=jnp.int32)[:, None]
    empty = jnp.arange(padded, dtype=jnp.int32) >= slots
    return jnp.sum(jnp.where(put, word[None, :], 0), axis=1) + jnp.where(empty, (rights * sectors) << 12, 0)


def multiply(sectors, live, plan_ref, copies, left_ref, right_ref, vector, halves, sums, out_refs):
    lefts, half_rows, columns = left_ref.shape
    rights = right_ref.shape[0]
    left_all = left_ref.reshape(lefts * half_rows, columns)
    sums[...] = jnp.zeros_like(sums)
    copies[1].wait()
    for first in range(0, sectors, wide_sectors):
        chosen = range(first, min(first + wide_sectors, sectors))
        wide = jnp.concatenate([vector[j] for j in chosen], axis=1)
        for left in range(0, lefts, step_lefts):
            rows = left_all[left * half_rows : (left + step_lefts) * half_rows, :]
            half = jnp.dot(rows, wide, preferred_element_type=jnp.float32).astype(jnp.bfloat16)
            for place, j in enumerate(chosen):
                part = half[:, place * columns : (place + 1) * columns]
                halves[j * lefts + left : j * lefts + left + step_lefts] = part.reshape(-1, half_rows, columns)

    def some_slots(turn, total):
        for step in range(unroll_slots):
            word = plan_ref[turn * unroll_slots + step]
            keep = (word >> 24).astype(jnp.float32)
            total = total * keep + halves[word & 4095].astype(jnp.float32)
            sums[(word >> 12) & 4095] = total.astype(jnp.bfloat16)
        return total

    turns = (live + unroll_slots - 1) // unroll_slots
    lax.fori_loop(0, turns, some_slots, jnp.zeros((half_rows, columns), jnp.float32))
    copies[2].wait()
    product = 0
    for r in range(rights):
        rows = sums[r * sectors : (r + 1) * sectors].reshape(sectors * half_rows, columns)
        product = product + lax.dot_general(
            rows, right_ref[r], (((1,), (1,)), ((), ())), preferred_element_type=jnp.float32
        )
    for j in range(sectors):
        out_refs[j][...] = product[j * half_rows : (j + 1) * half_rows].astype(out_refs[j].dtype)


def join(core, vector, j, mine, other):
    rows = mine.shape[0]
    vector[j, pl.ds(pl.multiple_of(core * rows, rows), rows)] = mine
    vector[j, pl.ds(pl.multiple_of((1 - core) * rows, rows), rows)] = other


def fetch(sources, places, arrived):
    copies = [pltpu.make_async_copy(*pair, arrived.at[i]) for i, pair in enumerate(zip(sources, places))]
    for copy in copies:
        copy.start()
    return copies


def first_kernel(sectors, core_ref, count_ref, plan_ref, left_hbm, right_hbm, own_hbm, *refs):
    mine, other = refs[: sectors - 1], refs[sectors - 1 : 2 * sectors - 1]
    out_refs = refs[2 * sectors - 1 : 3 * sectors - 1]
    left, right, own, arrived, vector, halves, sums = refs[3 * sectors - 1 :]
    copies = fetch((own_hbm, left_hbm, right_hbm), (own, left, right), arrived)
    for j in range(1, sectors):
        join(core_ref[0], vector, j, mine[j - 1][...], other[j][...])
    copies[0].wait()
    join(core_ref[0], vector, 0, own[...], other[0][...])
    multiply(sectors, count_ref[0], plan_ref, copies, left, right, vector, halves, sums, out_refs)


def second_kernel(sectors, core_ref, count_ref, plan_ref, left_hbm, right_hbm, own_hbm, *refs):
    pieces = 2 * sectors
    psis, sigmas = refs[: pieces - 1], refs[pieces - 1 : 2 * pieces - 1]
    out_refs = refs[2 * pieces - 1 : 2 * pieces + sectors - 1]
    own_ref = refs[2 * pieces + sectors - 1]
    left, right, own, arrived, vector, halves, sums = refs[2 * pieces + sectors :]
    copies = fetch((own_hbm, left_hbm, right_hbm), (own, left, right), arrived)
    copies[0].wait()
    psis = (own, *psis)

    def wide(ref):
        return ref[...].astype(jnp.float32)

    norm = sum(wide(p) * wide(p) for p in psis)
    correlation = sum(wide(p) * wide(s) for p, s in zip(psis, sigmas))
    theta = jnp.sum(correlation) / jnp.sum(norm)
    square = jnp.zeros_like(norm)
    for p, s in zip(psis, sigmas):
        resid = wide(s) - theta * wide(p)
        square = square + resid * resid
    entries = pieces * norm.shape[0] * norm.shape[1]
    scale = lax.rsqrt(jnp.sum(square) / entries + 1e-06)
    for j in range(sectors):
        mine, other = (
            ((wide(sigmas[i]) - theta * wide(psis[i])) * scale).astype(jnp.bfloat16) for i in (j, sectors + j)
        )
        if j == 0:
            own_ref[...] = mine
        join(core_ref[0], vector, j, mine, other)
    multiply(sectors, count_ref[0], plan_ref, copies, left, right, vector, halves, sums, out_refs)


def call_product(kernel, sectors, scalars, left, right, pieces, gives_own):
    lefts, half_rows, columns = left.shape
    rights = right.shape[0]
    shape = (half_rows, columns)
    block_bytes = half_rows * columns * 2
    outs = [jax.ShapeDtypeStruct(shape, jnp.float32)]
    outs += [jax.ShapeDtypeStruct(shape, jnp.bfloat16)] * (sectors - 1 + gives_own)
    return pl.pallas_call(
        functools.partial(kernel, sectors),
        out_shape=outs,
        in_specs=[whole_smem] * len(scalars) + [stays_out] * 3 + [whole_vmem] * (len(pieces) - 1),
        out_specs=[whole_vmem] * len(outs),
        scratch_shapes=[
            pltpu.VMEM(left.shape, jnp.bfloat16),
            pltpu.VMEM(right.shape, jnp.bfloat16),
            pltpu.VMEM(shape, jnp.bfloat16),
            pltpu.SemaphoreType.DMA((3,)),
            pltpu.VMEM((sectors, 2 * half_rows, columns), jnp.bfloat16),
            pltpu.VMEM((sectors * lefts, half_rows, columns), jnp.bfloat16),
            pltpu.VMEM((sectors * rights + 1, half_rows, columns), jnp.bfloat16),
        ],
        compiler_params=pltpu.CompilerParams(
            vmem_limit_bytes=block_bytes * (sectors * (lefts + rights + 24) + 64)
        ),
    )(*scalars, *(pltpu.with_memory_space_constraint(x, pltpu.HBM) for x in (left, right, pieces[0])), *pieces[1:])


def swap(value, axis, bit):
    return lax.ppermute(value, axis, [(i, i ^ bit) for i in range(lax.axis_size(axis))])


def gather(own):
    sectors = lax.axis_size("term")
    mine = {0: own}
    for j in reversed(range(1, sectors)):
        mine[j] = swap(own, "term", j)
    other = {j: swap(mine[j], "pair", 1) for j in (0, *reversed(range(1, sectors)))}
    return [mine[j] for j in range(sectors)] + [other[j] for j in range(sectors)]


def owner_sum(parts):
    sent = {j: swap(parts[j], "term", j) for j in reversed(range(1, len(parts)))}
    total = parts[0]
    for j in range(1, len(parts)):
        total = total + sent[j].astype(jnp.float32)
    bit = 1
    while bit < lax.axis_size("sub"):
        rounded = total.astype(jnp.bfloat16)
        total = rounded.astype(jnp.float32) + swap(rounded, "sub", bit).astype(jnp.float32)
        bit *= 2
    return total


def on_device(
    psi,
    left_blocks,
    right_blocks,
    left_index,
    right_index,
    block_source,
    block_target,
    block_count,
    sector_energy,
):
    sectors = lax.axis_size("term")
    lefts, rights = left_blocks.shape[1], right_blocks.shape[1]
    me = lax.axis_index("term").astype(jnp.int32)
    core = lax.axis_index("pair").astype(jnp.int32).reshape(1)
    left = left_blocks[0]
    right = right_blocks[0]
    own = psi[0]
    psis = gather(own)
    indices = (left_index[0], right_index[0], block_source[0], block_target[0])
    plan = make_plan(me, *indices, block_count[0], sectors, lefts, rights)
    scalars = (core, block_count, plan)
    parts = call_product(first_kernel, sectors, scalars, left, right, psis, False)
    energy = sector_energy[0]
    sigma_first = (owner_sum(parts) + energy * own.astype(jnp.float32)).astype(jnp.bfloat16)
    *parts, correction = call_product(
        second_kernel, sectors, scalars, left, right, psis + gather(sigma_first), True
    )
    sigma_second = (owner_sum(parts) + energy * correction.astype(jnp.float32)).astype(jnp.bfloat16)
    return (sigma_first[None], sigma_second[None])


def solution(mesh):
    placed = (
        P(("grp", "term"), "pair", None),
        P(("grp", "term", "sub"), None, "pair", None),
        P(("grp", "term", "sub"), None, None, None),
        P(("grp", "term", "sub"), None),
        P(("grp", "term", "sub"), None),
        P(("grp", "term", "sub"), None),
        P(("grp", "term", "sub"), None),
        P(("grp", "term", "sub")),
        P(("grp", "term")),
    )
    return jax.shard_map(
        on_device,
        mesh=mesh,
        in_specs=placed,
        out_specs=(P(("grp", "term"), "pair", None), P(("grp", "term"), "pair", None)),
        check_vma=False,
    )
```

time: 65.5 us -> 60 us (0.916)
  waiting for transfers between devices: 26.6 us -> 22.2 us
  Pallas kernels: 11.9 us -> 9.08 us
  starting transfers between devices: 22 us -> 23.8 us
  local copies, waits for them, and re-layouts: 2.19 us -> 1.33 us
    ppermute x22, waiting for transfers between devices: 26.6 us -> 22.2 us  [swap(): lax.ppermute(value, axis, [(i, i ^ bit) for i in range(lax.axis_size(axis...]
    pallas_call x1 -> x0, Pallas kernels: 3.25 us -> none  [make_plan(): pl.pallas_call(functools.partial(plan_kernel, sectors, rights, lefts), ou...]
    ppermute x22, starting transfers between devices: 22 us -> 23.8 us  [swap(): lax.ppermute(value, axis, [(i, i ^ bit) for i in range(lax.axis_size(axis...]
    transpose x1 -> x0, local copies, waits for them, and re-layouts: 1.54 us -> none  [on_device(): jnp.swapaxes(right_blocks[0], 1, 2).reshape(-1, right_blocks.shape[2])]
    unnamed x8 -> x12, local copies, waits for them, and re-layouts: 0.65 us -> 1.33 us
  transfers between devices with their start and end apart: 22 -> 22, of which waited for: 13 -> 14; matrix products, arithmetic and copies ran while one was open for 2% -> 1% of each run, Pallas kernels for 5% -> 0%
where the time goes in v2:
time: 60 us; the launch traced here: 59.6 us
  starting transfers between devices  23.8 us (40%)
  waiting for transfers between devices  22.2 us (37%)
  Pallas kernels  9.08 us (15%)
  between operations  2.05 us (3%)
  local copies, waits for them, and re-layouts  1.33 us (2%)
  other arithmetic  1.07 us (2%)
    ppermute x22, starting transfers between devices, swap(): lax.ppermute(value, axis, [(i, i ^ bit) for i in range(lax.axis_size(axis...  23.8 us
    ppermute x22, waiting for transfers between devices, swap(): lax.ppermute(value, axis, [(i, i ^ bit) for i in range(lax.axis_size(axis...  22.2 us
    pallas_call x2, Pallas kernels, call_product(): pl.pallas_call(functools.partial(kernel, sectors), out_shape=outs, in_spe...  9.08 us
    unnamed x12, local copies, waits for them, and re-layouts  1.33 us
  transfers between devices with their start and end apart: 22, of which 14 were waited for; matrix products, arithmetic and copies ran while one was open for 1% of the time, Pallas kernels for 0%

profile of v2, /device:TPU:0, one launch (start us, length us, event | category | flops | bytes accessed | tf_op | source)
XLA Modules:
  0.0 59.6 jit_solution(5624913831189978639)
XLA Ops:
  0.6 0.5 collective-permute-start.3
  1.1 4.7 %collective-permute-start.2 = (bf16[128,256]{1,0:T(8,128)(2,1)}, bf16[128,256]{1,0:T(8,128)(2,1)S(1)}, u32[]{:S(2)}, u32[]{:S(2)}) collective-permute-start(bf16[128,256]{1,0:T(8,128)(2,1)} %bitcast.31), channel_id=1, source_target_pairs={{0,12},{4,8},{8,4},{12,0},{1,13},{5,9},{9,5},{13,1},{2,14},{6,10},... | collective-permute-start | bytes 196616 | tf_op jit(solution)/shard_map/ppermute | solution.py:157
  5.8 0.6 %collective-permute-start = (bf16[128,256]{1,0:T(8,128)(2,1)}, bf16[128,256]{1,0:T(8,128)(2,1)S(1)}, u32[]{:S(2)}, u32[]{:S(2)}) collective-permute-start(bf16[128,256]{1,0:T(8,128)(2,1)} %bitcast.33), channel_id=1, source_target_pairs={{0,4},{4,0},{8,12},{12,8},{1,5},{5,1},{9,13},{13,9},{2,6},{6,2},{1... | collective-permute-start | bytes 196616 | tf_op jit(solution)/shard_map/ppermute | solution.py:157
  7.1 0.6 %copy-done.4 = s32[1,72]{1,0:T(1,128)S(1)} copy-done((s32[1,72]{1,0:T(1,128)S(1)}, s32[1,72]{1,0:T(1,128)}, u32[]{:S(2)}) %copy-start.4) | copy-done | bytes 312
  8.0 0.6 %copy-done.2 = s32[1,72]{1,0:T(1,128)S(1)} copy-done((s32[1,72]{1,0:T(1,128)S(1)}, s32[1,72]{1,0:T(1,128)}, u32[]{:S(2)}) %copy-start.2) | copy-done | bytes 312
  8.9 3.2 %collective-permute-done.1.refs_1_ = bf16[128,256]{1,0:T(8,128)(2,1)S(1)} collective-permute-done((bf16[128,256]{1,0:T(8,128)(2,1)}, bf16[128,256]{1,0:T(8,128)(2,1)S(1)}, u32[]{:S(2)}, u32[]{:S(2)}) %collective-permute-start.1) | collective-permute-done | bytes 65568 | tf_op jit(solution)/shard_map/ppermute | solution.py:157
  12.1 0.5 collective-permute-start.4
  12.6 0.7 %collective-permute-done.5.refs_5_ = bf16[128,256]{1,0:T(8,128)(2,1)S(1)} collective-permute-done((bf16[128,256]{1,0:T(8,128)(2,1)S(1)}, bf16[128,256]{1,0:T(8,128)(2,1)S(1)}, u32[]{:S(2)}, u32[]{:S(2)}) %collective-permute-start.5) | collective-permute-done | bytes 65568 | tf_op jit(solution)/shard_map/ppermute | solution.py:157
  13.5 4.2 %shard_map.104 = (f32[128,256]{1,0:T(8,128)S(1)}, bf16[128,256]{1,0:T(8,128)(2,1)S(1)}, bf16[128,256]{1,0:T(8,128)(2,1)S(1)}, bf16[128,256]{1,0:T(8,128)(2,1)S(1)}) custom-call(s32[1]{0:T(128)} %bitcast.core_ref, s32[1]{0:T(128)} %copy.11.count_ref, s32[72]{0:T(128)S(1)} %fusion.4.plan_ref, bf16[8,128,256]{2,1,0:T(8,128)(2,1)} %bitcast.28, ...), custom_call_target="tpu_custom_call" | custom-call | tf_op jit(solution)/shard_map/pallas_call | solution.py:136
  17.7 0.8 %collective-permute-start.7 = (bf16[128,256]{1,0:T(8,128)(2,1)S(1)}, bf16[128,256]{1,0:T(8,128)(2,1)S(1)}, u32[]{:S(2)}, u32[]{:S(2)}) collective-permute-start(bf16[128,256]{1,0:T(8,128)(2,1)S(1)} %get-tuple-element.12), channel_id=1, source_target_pairs={{0,4},{4,0},{8,12},{12,8},{1,5},{5,1},{9,13},{13,9},{2,6},{6,2},{1... | collective-permute-start | bytes 196616 | tf_op jit(solution)/shard_map/ppermute | solution.py:157
  18.6 2.0 %collective-permute-start.8 = (bf16[128,256]{1,0:T(8,128)(2,1)S(1)}, bf16[128,256]{1,0:T(8,128)(2,1)S(1)}, u32[]{:S(2)}, u32[]{:S(2)}) collective-permute-start(bf16[128,256]{1,0:T(8,128)(2,1)S(1)} %get-tuple-element.13), channel_id=1, source_target_pairs={{0,8},{4,12},{8,0},{12,4},{1,9},{5,13},{9,1},{13,5},{2,10},{6,14},... | collective-permute-start | bytes 196616 | tf_op jit(solution)/shard_map/ppermute | solution.py:157
  20.6 1.6 %collective-permute-start.9 = (bf16[128,256]{1,0:T(8,128)(2,1)S(1)}, bf16[128,256]{1,0:T(8,128)(2,1)S(1)}, u32[]{:S(2)}, u32[]{:S(2)}) collective-permute-start(bf16[128,256]{1,0:T(8,128)(2,1)S(1)} %get-tuple-element.14), channel_id=1, source_target_pairs={{0,12},{4,8},{8,4},{12,0},{1,13},{5,9},{9,5},{13,1},{2,14},{6,10},... | collective-permute-start | bytes 196616 | tf_op jit(solution)/shard_map/ppermute | solution.py:157
  22.2 0.7 %collective-permute-done.7 = bf16[128,256]{1,0:T(8,128)(2,1)S(1)} collective-permute-done((bf16[128,256]{1,0:T(8,128)(2,1)S(1)}, bf16[128,256]{1,0:T(8,128)(2,1)S(1)}, u32[]{:S(2)}, u32[]{:S(2)}) %collective-permute-start.7) | collective-permute-done | bytes 65568 | tf_op jit(solution)/shard_map/ppermute | solution.py:157
  22.8 4.2 %collective-permute-done.8 = bf16[128,256]{1,0:T(8,128)(2,1)S(1)} collective-permute-done((bf16[128,256]{1,0:T(8,128)(2,1)S(1)}, bf16[128,256]{1,0:T(8,128)(2,1)S(1)}, u32[]{:S(2)}, u32[]{:S(2)}) %collective-permute-start.8) | collective-permute-done | bytes 65568 | tf_op jit(solution)/shard_map/ppermute | solution.py:157
  27.0 1.7 %collective-permute-start.10 = (bf16[128,256]{1,0:T(8,128)(2,1)S(1)}, bf16[128,256]{1,0:T(8,128)(2,1)S(1)}, u32[]{:S(2)}, u32[]{:S(2)}) collective-permute-start(bf16[128,256]{1,0:T(8,128)(2,1)S(1)} %add_convert_fusion.3), channel_id=1, source_target_pairs={{0,2},{2,0},{1,3},{3,1},{4,6},{6,4},{5,7},{7,5},{8,10},{10,8},{9,1... | collective-permute-start | bytes 196616 | tf_op jit(solution)/shard_map/ppermute | solution.py:157
  29.4 2.0 %collective-permute-done.10 = bf16[128,256]{1,0:T(8,128)(2,1)S(1)} collective-permute-done((bf16[128,256]{1,0:T(8,128)(2,1)S(1)}, bf16[128,256]{1,0:T(8,128)(2,1)S(1)}, u32[]{:S(2)}, u32[]{:S(2)}) %collective-permute-start.10) | collective-permute-done | bytes 65568 | tf_op jit(solution)/shard_map/ppermute | solution.py:157
  31.4 1.9 %collective-permute-start.13 = (bf16[128,256]{1,0:T(8,128)(2,1)S(1)}, bf16[128,256]{1,0:T(8,128)(2,1)S(1)}, u32[]{:S(2)}, u32[]{:S(2)}) collective-permute-start(bf16[128,256]{1,0:T(8,128)(2,1)S(1)} %add_convert_fusion.2.refs_7_), channel_id=1, source_target_pairs={{0,12},{4,8},{8,4},{12,0},{1,13},{5,9},{9,5},{13,1},{2,14},{6,10},... | collective-permute-start | bytes 196616 | tf_op jit(solution)/shard_map/ppermute | solution.py:157
  33.4 0.8 %collective-permute-start.12 = (bf16[128,256]{1,0:T(8,128)(2,1)S(1)}, bf16[128,256]{1,0:T(8,128)(2,1)S(1)}, u32[]{:S(2)}, u32[]{:S(2)}) collective-permute-start(bf16[128,256]{1,0:T(8,128)(2,1)S(1)} %add_convert_fusion.2.refs_7_), channel_id=1, source_target_pairs={{0,8},{4,12},{8,0},{12,4},{1,9},{5,13},{9,1},{13,5},{2,10},{6,14},... | collective-permute-start | bytes 196616 | tf_op jit(solution)/shard_map/ppermute | solution.py:157
  34.2 1.7 %collective-permute-start.11 = (bf16[128,256]{1,0:T(8,128)(2,1)S(1)}, bf16[128,256]{1,0:T(8,128)(2,1)S(1)}, u32[]{:S(2)}, u32[]{:S(2)}) collective-permute-start(bf16[128,256]{1,0:T(8,128)(2,1)S(1)} %add_convert_fusion.2.refs_7_), channel_id=1, source_target_pairs={{0,4},{4,0},{8,12},{12,8},{1,5},{5,1},{9,13},{13,9},{2,6},{6,2},{1... | collective-permute-start | bytes 196616 | tf_op jit(solution)/shard_map/ppermute | solution.py:157
  35.9 1.7 %collective-permute-done.13.refs_10_ = bf16[128,256]{1,0:T(8,128)(2,1)S(1)} collective-permute-done((bf16[128,256]{1,0:T(8,128)(2,1)S(1)}, bf16[128,256]{1,0:T(8,128)(2,1)S(1)}, u32[]{:S(2)}, u32[]{:S(2)}) %collective-permute-start.13) | collective-permute-done | bytes 65568 | tf_op jit(solution)/shard_map/ppermute | solution.py:157
  37.6 1.6 %collective-permute-done.12.refs_9_ = bf16[128,256]{1,0:T(8,128)(2,1)S(1)} collective-permute-done((bf16[128,256]{1,0:T(8,128)(2,1)S(1)}, bf16[128,256]{1,0:T(8,128)(2,1)S(1)}, u32[]{:S(2)}, u32[]{:S(2)}) %collective-permute-start.12) | collective-permute-done | bytes 65568 | tf_op jit(solution)/shard_map/ppermute | solution.py:157
  39.2 0.5 collective-permute-start.15
  39.7 0.7 %collective-permute-done.16.refs_13_ = bf16[128,256]{1,0:T(8,128)(2,1)S(1)} collective-permute-done((bf16[128,256]{1,0:T(8,128)(2,1)S(1)}, bf16[128,256]{1,0:T(8,128)(2,1)S(1)}, u32[]{:S(2)}, u32[]{:S(2)}) %collective-permute-start.16) | collective-permute-done | bytes 65568 | tf_op jit(solution)/shard_map/ppermute | solution.py:157
  40.6 4.9 %shard_map.105 = (f32[128,256]{1,0:T(8,128)S(1)}, bf16[128,256]{1,0:T(8,128)(2,1)S(1)}, bf16[128,256]{1,0:T(8,128)(2,1)S(1)}, bf16[128,256]{1,0:T(8,128)(2,1)S(1)}, bf16[128,256]{1,0:T(8,128)(2,1)S(1)}) custom-call(s32[1]{0:T(128)} %bitcast.core_ref, s32[1]{0:T(128)} %copy.11.count_ref, s32[72]{0:T(128)S(1)} %fusion.4.plan_ref, ...), custom_call_target="tpu_custom_call" | custom-call | tf_op jit(solution)/shard_map/pallas_call | solution.py:136
  45.5 0.6 %collective-permute-start.18 = (bf16[128,256]{1,0:T(8,128)(2,1)S(1)}, bf16[128,256]{1,0:T(8,128)(2,1)S(1)}, u32[]{:S(2)}, u32[]{:S(2)}) collective-permute-start(bf16[128,256]{1,0:T(8,128)(2,1)S(1)} %get-tuple-element.16), channel_id=1, source_target_pairs={{0,4},{4,0},{8,12},{12,8},{1,5},{5,1},{9,13},{13,9},{2,6},{6,2},{1... | collective-permute-start | bytes 196616 | tf_op jit(solution)/shard_map/ppermute | solution.py:157
  46.1 1.7 %collective-permute-start.19 = (bf16[128,256]{1,0:T(8,128)(2,1)S(1)}, bf16[128,256]{1,0:T(8,128)(2,1)S(1)}, u32[]{:S(2)}, u32[]{:S(2)}) collective-permute-start(bf16[128,256]{1,0:T(8,128)(2,1)S(1)} %get-tuple-element.17), channel_id=1, source_target_pairs={{0,8},{4,12},{8,0},{12,4},{1,9},{5,13},{9,1},{13,5},{2,10},{6,14},... | collective-permute-start | bytes 196616 | tf_op jit(solution)/shard_map/ppermute | solution.py:157
  47.8 2.1 %collective-permute-start.20 = (bf16[128,256]{1,0:T(8,128)(2,1)S(1)}, bf16[128,256]{1,0:T(8,128)(2,1)S(1)}, u32[]{:S(2)}, u32[]{:S(2)}) collective-permute-start(bf16[128,256]{1,0:T(8,128)(2,1)S(1)} %get-tuple-element.18), channel_id=1, source_target_pairs={{0,12},{4,8},{8,4},{12,0},{1,13},{5,9},{9,5},{13,1},{2,14},{6,10},... | collective-permute-start | bytes 196616 | tf_op jit(solution)/shard_map/ppermute | solution.py:157
  49.9 0.7 %collective-permute-done.18 = bf16[128,256]{1,0:T(8,128)(2,1)S(1)} collective-permute-done((bf16[128,256]{1,0:T(8,128)(2,1)S(1)}, bf16[128,256]{1,0:T(8,128)(2,1)S(1)}, u32[]{:S(2)}, u32[]{:S(2)}) %collective-permute-start.18) | collective-permute-done | bytes 65568 | tf_op jit(solution)/shard_map/ppermute | solution.py:157
  50.6 3.9 %collective-permute-done.19 = bf16[128,256]{1,0:T(8,128)(2,1)S(1)} collective-permute-done((bf16[128,256]{1,0:T(8,128)(2,1)S(1)}, bf16[128,256]{1,0:T(8,128)(2,1)S(1)}, u32[]{:S(2)}, u32[]{:S(2)}) %collective-permute-start.19) | collective-permute-done | bytes 65568 | tf_op jit(solution)/shard_map/ppermute | solution.py:157
  54.6 1.9 %collective-permute-start.21 = (bf16[128,256]{1,0:T(8,128)(2,1)S(1)}, bf16[128,256]{1,0:T(8,128)(2,1)S(1)}, u32[]{:S(2)}, u32[]{:S(2)}) collective-permute-start(bf16[128,256]{1,0:T(8,128)(2,1)S(1)} %add_convert_fusion.1), channel_id=1, source_target_pairs={{0,2},{2,0},{1,3},{3,1},{4,6},{6,4},{5,7},{7,5},{8,10},{10,8},{9,1... | collective-permute-start | bytes 196616 | tf_op jit(solution)/shard_map/ppermute | solution.py:157
  56.5 2.4 %collective-permute-done.21 = bf16[128,256]{1,0:T(8,128)(2,1)S(1)} collective-permute-done((bf16[128,256]{1,0:T(8,128)(2,1)S(1)}, bf16[128,256]{1,0:T(8,128)(2,1)S(1)}, u32[]{:S(2)}, u32[]{:S(2)}) %collective-permute-start.21) | collective-permute-done | bytes 65568 | tf_op jit(solution)/shard_map/ppermute | solution.py:157
  58.9 0.7 %fusion = bf16[1,128,256]{2,1,0:T(8,128)(2,1)} fusion(bf16[128,256]{1,0:T(8,128)(2,1)S(1)} %get-tuple-element.19, bf16[128,256]{1,0:T(8,128)(2,1)S(1)} %collective-permute-done.21, bf16[128,256]{1,0:T(8,128)(2,1)S(1)} %add_convert_fusion.1, f32[]{:T(128)} %bitcast.24), kind=kLoop, calls=%fused_computation.4 | loop fusion | flops 229376 | bytes 262148 | tf_op jit(solution)/shard_map/broadcast_in_dim | solution.py:211
  (36 shorter events, 1.0 us)
Async XLA Ops:
  0.6 12.0 %collective-permute-start.3 = (bf16[128,256]{1,0:T(8,128)(2,1)}, bf16[128,256]{1,0:T(8,128)(2,1)S(1)}, u32[]{:S(2)}, u32[]{:S(2)}) collective-permute-start(bf16[128,256]{1,0:T(8,128)(2,1)} %bitcast.30), channel_id=1, source_target_pairs={{0,1},{1,0},{2,3},{3,2},{4,5},{5,4},{6,7},{7,6},{8,9},{9,8},{10,11... | collective-permute-start | bytes 196616 | tf_op jit(solution)/shard_map/ppermute | solution.py:157
  1.1 7.7 %collective-permute-start.2 = (bf16[128,256]{1,0:T(8,128)(2,1)}, bf16[128,256]{1,0:T(8,128)(2,1)S(1)}, u32[]{:S(2)}, u32[]{:S(2)}) collective-permute-start(bf16[128,256]{1,0:T(8,128)(2,1)} %bitcast.31), channel_id=1, source_target_pairs={{0,12},{4,8},{8,4},{12,0},{1,13},{5,9},{9,5},{13,1},{2,14},{6,10},... | collective-permute-start | bytes 196616 | tf_op jit(solution)/shard_map/ppermute | solution.py:157
  5.8 6.3 %collective-permute-start.1 = (bf16[128,256]{1,0:T(8,128)(2,1)}, bf16[128,256]{1,0:T(8,128)(2,1)S(1)}, u32[]{:S(2)}, u32[]{:S(2)}) collective-permute-start(bf16[128,256]{1,0:T(8,128)(2,1)} %bitcast.32), channel_id=1, source_target_pairs={{0,8},{4,12},{8,0},{12,4},{1,9},{5,13},{9,1},{13,5},{2,10},{6,14},... | collective-permute-start | bytes 196616 | tf_op jit(solution)/shard_map/ppermute | solution.py:157
  5.8 6.3 %collective-permute-start = (bf16[128,256]{1,0:T(8,128)(2,1)}, bf16[128,256]{1,0:T(8,128)(2,1)S(1)}, u32[]{:S(2)}, u32[]{:S(2)}) collective-permute-start(bf16[128,256]{1,0:T(8,128)(2,1)} %bitcast.33), channel_id=1, source_target_pairs={{0,4},{4,0},{8,12},{12,8},{1,5},{5,1},{9,13},{13,9},{2,6},{6,2},{1... | collective-permute-start | bytes 196616 | tf_op jit(solution)/shard_map/ppermute | solution.py:157
  7.1 0.7 %copy-start.4 = (s32[1,72]{1,0:T(1,128)S(1)}, s32[1,72]{1,0:T(1,128)}, u32[]{:S(2)}) copy-start(s32[1,72]{1,0:T(1,128)} %param.15) | copy-start | bytes 868
  7.1 0.7 %copy-start.5 = (s32[1,72]{1,0:T(1,128)S(1)}, s32[1,72]{1,0:T(1,128)}, u32[]{:S(2)}) copy-start(s32[1,72]{1,0:T(1,128)} %param.13) | copy-start | bytes 868
  8.0 0.7 %copy-start.2 = (s32[1,72]{1,0:T(1,128)S(1)}, s32[1,72]{1,0:T(1,128)}, u32[]{:S(2)}) copy-start(s32[1,72]{1,0:T(1,128)} %param.12) | copy-start | bytes 868
  8.0 0.7 %copy-start.3 = (s32[1,72]{1,0:T(1,128)S(1)}, s32[1,72]{1,0:T(1,128)}, u32[]{:S(2)}) copy-start(s32[1,72]{1,0:T(1,128)} %param.14) | copy-start | bytes 868
  8.9 3.7 %collective-permute-start.6 = (bf16[128,256]{1,0:T(8,128)(2,1)S(1)}, bf16[128,256]{1,0:T(8,128)(2,1)S(1)}, u32[]{:S(2)}, u32[]{:S(2)}) collective-permute-start(bf16[128,256]{1,0:T(8,128)(2,1)S(1)} %collective-permute-done.2.refs_2_), channel_id=1, source_target_pairs={{0,1},{1,0},{2,3},{3,2},{4,5},{5,4},{6,7},{7,6},{8,9},{9,8},{10,11... | collective-permute-start | bytes 196616 | tf_op jit(solution)/shard_map/ppermute | solution.py:157
  12.1 1.3 %collective-permute-start.5 = (bf16[128,256]{1,0:T(8,128)(2,1)S(1)}, bf16[128,256]{1,0:T(8,128)(2,1)S(1)}, u32[]{:S(2)}, u32[]{:S(2)}) collective-permute-start(bf16[128,256]{1,0:T(8,128)(2,1)S(1)} %collective-permute-done.1.refs_1_), channel_id=1, source_target_pairs={{0,1},{1,0},{2,3},{3,2},{4,5},{5,4},{6,7},{7,6},{8,9},{9,8},{10,11... | collective-permute-start | bytes 196616 | tf_op jit(solution)/shard_map/ppermute | solution.py:157
  12.1 1.4 %collective-permute-start.4 = (bf16[128,256]{1,0:T(8,128)(2,1)S(1)}, bf16[128,256]{1,0:T(8,128)(2,1)S(1)}, u32[]{:S(2)}, u32[]{:S(2)}) collective-permute-start(bf16[128,256]{1,0:T(8,128)(2,1)S(1)} %collective-permute-done.refs_0_), channel_id=1, source_target_pairs={{0,1},{1,0},{2,3},{3,2},{4,5},{5,4},{6,7},{7,6},{8,9},{9,8},{10,11... | collective-permute-start | bytes 196616 | tf_op jit(solution)/shard_map/ppermute | solution.py:157
  17.7 5.1 %collective-permute-start.7 = (bf16[128,256]{1,0:T(8,128)(2,1)S(1)}, bf16[128,256]{1,0:T(8,128)(2,1)S(1)}, u32[]{:S(2)}, u32[]{:S(2)}) collective-permute-start(bf16[128,256]{1,0:T(8,128)(2,1)S(1)} %get-tuple-element.12), channel_id=1, source_target_pairs={{0,4},{4,0},{8,12},{12,8},{1,5},{5,1},{9,13},{13,9},{2,6},{6,2},{1... | collective-permute-start | bytes 196616 | tf_op jit(solution)/shard_map/ppermute | solution.py:157
  18.6 8.4 %collective-permute-start.8 = (bf16[128,256]{1,0:T(8,128)(2,1)S(1)}, bf16[128,256]{1,0:T(8,128)(2,1)S(1)}, u32[]{:S(2)}, u32[]{:S(2)}) collective-permute-start(bf16[128,256]{1,0:T(8,128)(2,1)S(1)} %get-tuple-element.13), channel_id=1, source_target_pairs={{0,8},{4,12},{8,0},{12,4},{1,9},{5,13},{9,1},{13,5},{2,10},{6,14},... | collective-permute-start | bytes 196616 | tf_op jit(solution)/shard_map/ppermute | solution.py:157
  20.6 6.4 %collective-permute-start.9 = (bf16[128,256]{1,0:T(8,128)(2,1)S(1)}, bf16[128,256]{1,0:T(8,128)(2,1)S(1)}, u32[]{:S(2)}, u32[]{:S(2)}) collective-permute-start(bf16[128,256]{1,0:T(8,128)(2,1)S(1)} %get-tuple-element.14), channel_id=1, source_target_pairs={{0,12},{4,8},{8,4},{12,0},{1,13},{5,9},{9,5},{13,1},{2,14},{6,10},... | collective-permute-start | bytes 196616 | tf_op jit(solution)/shard_map/ppermute | solution.py:157
  27.0 4.4 %copy-start.1 = (bf16[1,128,256]{2,1,0:T(8,128)(2,1)S(1)}, bf16[1,128,256]{2,1,0:T(8,128)(2,1)}, u32[]{:S(2)}) copy-start(bf16[1,128,256]{2,1,0:T(8,128)(2,1)} %param.9) | copy-start | bytes 196612
  27.0 4.3 %collective-permute-start.10 = (bf16[128,256]{1,0:T(8,128)(2,1)S(1)}, bf16[128,256]{1,0:T(8,128)(2,1)S(1)}, u32[]{:S(2)}, u32[]{:S(2)}) collective-permute-start(bf16[128,256]{1,0:T(8,128)(2,1)S(1)} %add_convert_fusion.3), channel_id=1, source_target_pairs={{0,2},{2,0},{1,3},{3,1},{4,6},{6,4},{5,7},{7,5},{8,10},{10,8},{9,1... | collective-permute-start | bytes 196616 | tf_op jit(solution)/shard_map/ppermute | solution.py:157
  31.4 14.1 %copy-start = (bf16[128,256]{1,0:T(8,128)(2,1)}, bf16[128,256]{1,0:T(8,128)(2,1)S(1)}, u32[]{:S(2)}) copy-start(bf16[128,256]{1,0:T(8,128)(2,1)S(1)} %add_convert_fusion.2.refs_7_) | copy-start | bytes 196612
  31.4 6.1 %collective-permute-start.13 = (bf16[128,256]{1,0:T(8,128)(2,1)S(1)}, bf16[128,256]{1,0:T(8,128)(2,1)S(1)}, u32[]{:S(2)}, u32[]{:S(2)}) collective-permute-start(bf16[128,256]{1,0:T(8,128)(2,1)S(1)} %add_convert_fusion.2.refs_7_), channel_id=1, source_target_pairs={{0,12},{4,8},{8,4},{12,0},{1,13},{5,9},{9,5},{13,1},{2,14},{6,10},... | collective-permute-start | bytes 196616 | tf_op jit(solution)/shard_map/ppermute | solution.py:157
  33.4 5.8 %collective-permute-start.12 = (bf16[128,256]{1,0:T(8,128)(2,1)S(1)}, bf16[128,256]{1,0:T(8,128)(2,1)S(1)}, u32[]{:S(2)}, u32[]{:S(2)}) collective-permute-start(bf16[128,256]{1,0:T(8,128)(2,1)S(1)} %add_convert_fusion.2.refs_7_), channel_id=1, source_target_pairs={{0,8},{4,12},{8,0},{12,4},{1,9},{5,13},{9,1},{13,5},{2,10},{6,14},... | collective-permute-start | bytes 196616 | tf_op jit(solution)/shard_map/ppermute | solution.py:157
  34.2 5.0 %collective-permute-start.11 = (bf16[128,256]{1,0:T(8,128)(2,1)S(1)}, bf16[128,256]{1,0:T(8,128)(2,1)S(1)}, u32[]{:S(2)}, u32[]{:S(2)}) collective-permute-start(bf16[128,256]{1,0:T(8,128)(2,1)S(1)} %add_convert_fusion.2.refs_7_), channel_id=1, source_target_pairs={{0,4},{4,0},{8,12},{12,8},{1,5},{5,1},{9,13},{13,9},{2,6},{6,2},{1... | collective-permute-start | bytes 196616 | tf_op jit(solution)/shard_map/ppermute | solution.py:157
  35.9 3.8 %collective-permute-start.14 = (bf16[128,256]{1,0:T(8,128)(2,1)S(1)}, bf16[128,256]{1,0:T(8,128)(2,1)S(1)}, u32[]{:S(2)}, u32[]{:S(2)}) collective-permute-start(bf16[128,256]{1,0:T(8,128)(2,1)S(1)} %add_convert_fusion.2.refs_7_), channel_id=1, source_target_pairs={{0,1},{1,0},{2,3},{3,2},{4,5},{5,4},{6,7},{7,6},{8,9},{9,8},{10,11... | collective-permute-start | bytes 196616 | tf_op jit(solution)/shard_map/ppermute | solution.py:157
  37.6 2.1 %collective-permute-start.17 = (bf16[128,256]{1,0:T(8,128)(2,1)S(1)}, bf16[128,256]{1,0:T(8,128)(2,1)S(1)}, u32[]{:S(2)}, u32[]{:S(2)}) collective-permute-start(bf16[128,256]{1,0:T(8,128)(2,1)S(1)} %collective-permute-done.13.refs_10_), channel_id=1, source_target_pairs={{0,1},{1,0},{2,3},{3,2},{4,5},{5,4},{6,7},{7,6},{8,9},{9,8},{10,11... | collective-permute-start | bytes 196616 | tf_op jit(solution)/shard_map/ppermute | solution.py:157
  39.1 1.3 %collective-permute-start.16 = (bf16[128,256]{1,0:T(8,128)(2,1)S(1)}, bf16[128,256]{1,0:T(8,128)(2,1)S(1)}, u32[]{:S(2)}, u32[]{:S(2)}) collective-permute-start(bf16[128,256]{1,0:T(8,128)(2,1)S(1)} %collective-permute-done.12.refs_9_), channel_id=1, source_target_pairs={{0,1},{1,0},{2,3},{3,2},{4,5},{5,4},{6,7},{7,6},{8,9},{9,8},{10,11... | collective-permute-start | bytes 196616 | tf_op jit(solution)/shard_map/ppermute | solution.py:157
  39.2 1.4 %collective-permute-start.15 = (bf16[128,256]{1,0:T(8,128)(2,1)S(1)}, bf16[128,256]{1,0:T(8,128)(2,1)S(1)}, u32[]{:S(2)}, u32[]{:S(2)}) collective-permute-start(bf16[128,256]{1,0:T(8,128)(2,1)S(1)} %collective-permute-done.11.refs_8_), channel_id=1, source_target_pairs={{0,1},{1,0},{2,3},{3,2},{4,5},{5,4},{6,7},{7,6},{8,9},{9,8},{10,11... | collective-permute-start | bytes 196616 | tf_op jit(solution)/shard_map/ppermute | solution.py:157
  45.5 5.1 %collective-permute-start.18 = (bf16[128,256]{1,0:T(8,128)(2,1)S(1)}, bf16[128,256]{1,0:T(8,128)(2,1)S(1)}, u32[]{:S(2)}, u32[]{:S(2)}) collective-permute-start(bf16[128,256]{1,0:T(8,128)(2,1)S(1)} %get-tuple-element.16), channel_id=1, source_target_pairs={{0,4},{4,0},{8,12},{12,8},{1,5},{5,1},{9,13},{13,9},{2,6},{6,2},{1... | collective-permute-start | bytes 196616 | tf_op jit(solution)/shard_map/ppermute | solution.py:157
  46.1 8.4 %collective-permute-start.19 = (bf16[128,256]{1,0:T(8,128)(2,1)S(1)}, bf16[128,256]{1,0:T(8,128)(2,1)S(1)}, u32[]{:S(2)}, u32[]{:S(2)}) collective-permute-start(bf16[128,256]{1,0:T(8,128)(2,1)S(1)} %get-tuple-element.17), channel_id=1, source_target_pairs={{0,8},{4,12},{8,0},{12,4},{1,9},{5,13},{9,1},{13,5},{2,10},{6,14},... | collective-permute-start | bytes 196616 | tf_op jit(solution)/shard_map/ppermute | solution.py:157
  47.8 6.7 %collective-permute-start.20 = (bf16[128,256]{1,0:T(8,128)(2,1)S(1)}, bf16[128,256]{1,0:T(8,128)(2,1)S(1)}, u32[]{:S(2)}, u32[]{:S(2)}) collective-permute-start(bf16[128,256]{1,0:T(8,128)(2,1)S(1)} %get-tuple-element.18), channel_id=1, source_target_pairs={{0,12},{4,8},{8,4},{12,0},{1,13},{5,9},{9,5},{13,1},{2,14},{6,10},... | collective-permute-start | bytes 196616 | tf_op jit(solution)/shard_map/ppermute | solution.py:157
  54.6 4.3 %collective-permute-start.21 = (bf16[128,256]{1,0:T(8,128)(2,1)S(1)}, bf16[128,256]{1,0:T(8,128)(2,1)S(1)}, u32[]{:S(2)}, u32[]{:S(2)}) collective-permute-start(bf16[128,256]{1,0:T(8,128)(2,1)S(1)} %add_convert_fusion.1), channel_id=1, source_target_pairs={{0,2},{2,0},{1,3},{3,1},{4,6},{6,4},{5,7},{7,5},{8,10},{10,8},{9,1... | collective-permute-start | bytes 196616 | tf_op jit(solution)/shard_map/ppermute | solution.py:157

commit v3 on v2

v3 whole, which is shorter than its diff:
```python
import functools

import jax
import jax.numpy as jnp
from jax import lax
from jax.experimental import pallas as pl
from jax.experimental.pallas import tpu as pltpu
from jax.sharding import PartitionSpec as P

unroll_slots = 4
wide_sectors = 4
step_lefts = 2
whole_vmem = pl.BlockSpec(memory_space=pltpu.VMEM)
whole_smem = pl.BlockSpec(memory_space=pltpu.SMEM)
stays_out = pl.BlockSpec(memory_space=pltpu.HBM)


def make_plan(me, left_index, right_index, source, target, live, sectors, lefts, rights):
    slots = left_index.shape[0]
    padded = -(-slots // unroll_slots) * unroll_slots
    number = jnp.arange(slots, dtype=jnp.int32)
    alive = number < live
    group = jnp.where(alive, right_index * sectors + (target ^ me), rights * sectors)
    half = jnp.where(alive, (source ^ me) * lefts + left_index, 0)
    same = group[None, :] == group[:, None]
    before = number[None, :] < number[:, None]
    place = jnp.sum(((group[None, :] < group[:, None]) | (same & before)).astype(jnp.int32), axis=1)
    goes_on = jnp.max((same & before).astype(jnp.int32), axis=1)
    word = half + (group << 12) + (goes_on << 24)
    put = place[None, :] == jnp.arange(padded, dtype=jnp.int32)[:, None]
    empty = jnp.arange(padded, dtype=jnp.int32) >= slots
    return jnp.sum(jnp.where(put, word[None, :], 0), axis=1) + jnp.where(empty, (rights * sectors) << 12, 0)


def half_products(sectors, left_ref, vector, halves):
    lefts, half_rows, columns = left_ref.shape
    left_all = left_ref.reshape(lefts * half_rows, columns)
    for first in range(0, sectors, wide_sectors):
        chosen = range(first, min(first + wide_sectors, sectors))
        wide = jnp.concatenate([vector[j] for j in chosen], axis=1)
        for left in range(0, lefts, step_lefts):
            rows = left_all[left * half_rows : (left + step_lefts) * half_rows, :]
            half = jnp.dot(rows, wide, preferred_element_type=jnp.float32).astype(jnp.bfloat16)
            for place, j in enumerate(chosen):
                part = half[:, place * columns : (place + 1) * columns]
                halves[j * lefts + left : j * lefts + left + step_lefts] = part.reshape(-1, half_rows, columns)


def sum_halves(live, plan_ref, halves, sums):
    def some_slots(turn, total):
        for step in range(unroll_slots):
            word = plan_ref[turn * unroll_slots + step]
            keep = (word >> 24).astype(jnp.float32)
            total = total * keep + halves[word & 4095].astype(jnp.float32)
            sums[(word >> 12) & 4095] = total.astype(jnp.bfloat16)
        return total

    turns = (live + unroll_slots - 1) // unroll_slots
    lax.fori_loop(0, turns, some_slots, jnp.zeros(halves.shape[1:], jnp.float32))


def all_targets(sectors, right_ref, sums, out_refs):
    half_rows, columns = sums.shape[1:]
    product = 0
    for r in range(right_ref.shape[0]):
        rows = sums[r * sectors : (r + 1) * sectors].reshape(sectors * half_rows, columns)
        product = product + lax.dot_general(
            rows, right_ref[r], (((1,), (1,)), ((), ())), preferred_element_type=jnp.float32
        )
    for j in range(sectors):
        out_refs[j][...] = product[j * half_rows : (j + 1) * half_rows].astype(out_refs[j].dtype)


def join(core, vector, j, mine, other):
    rows = mine.shape[0]
    vector[j, pl.ds(pl.multiple_of(core * rows, rows), rows)] = mine
    vector[j, pl.ds(pl.multiple_of((1 - core) * rows, rows), rows)] = other


def wide_of(ref):
    return ref[...].astype(jnp.float32)


def fetch_kernel(*refs):
    arrived = refs[-1]
    count = len(refs) // 2
    copies = [pltpu.make_async_copy(refs[i], refs[count + i], arrived.at[i]) for i in range(count)]
    for copy in copies:
        copy.start()
    for copy in copies:
        copy.wait()


def fetch(*arrays):
    return pl.pallas_call(
        fetch_kernel,
        out_shape=[pltpu.VMEM(x.shape, x.dtype) for x in arrays],
        in_specs=[stays_out] * len(arrays),
        out_specs=[whole_vmem] * len(arrays),
        scratch_shapes=[pltpu.SemaphoreType.DMA((len(arrays),))],
    )(*(pltpu.with_memory_space_constraint(x, pltpu.HBM) for x in arrays))


def first_kernel(sectors, core_ref, count_ref, plan_ref, left, right, *refs):
    psis, out_refs = refs[: 2 * sectors], refs[2 * sectors : -3]
    vector, halves, sums = refs[-3:]
    sums[...] = jnp.zeros_like(sums)
    for j in range(sectors):
        join(core_ref[0], vector, j, psis[j][...], psis[sectors + j][...])
    half_products(sectors, left, vector, halves)
    sum_halves(count_ref[0], plan_ref, halves, sums)
    all_targets(sectors, right, sums, out_refs)


def second_kernel(sectors, core_ref, count_ref, plan_ref, left, right, *refs):
    pieces = 2 * sectors
    psis, sigmas = refs[:pieces], refs[pieces : 2 * pieces]
    own_ref, *out_refs = refs[2 * pieces : -3]
    vector, halves, sums = refs[-3:]
    sums[...] = jnp.zeros_like(sums)
    norm = sum(wide_of(p) * wide_of(p) for p in psis)
    correlation = sum(wide_of(p) * wide_of(s) for p, s in zip(psis, sigmas))
    theta = jnp.sum(correlation) / jnp.sum(norm)
    square = jnp.zeros_like(norm)
    for p, s in zip(psis, sigmas):
        resid = wide_of(s) - theta * wide_of(p)
        square = square + resid * resid
    entries = pieces * norm.shape[0] * norm.shape[1]
    scale = lax.rsqrt(jnp.sum(square) / entries + 1e-06)
    for j in range(sectors):
        mine, other = (
            ((wide_of(sigmas[i]) - theta * wide_of(psis[i])) * scale).astype(jnp.bfloat16) for i in (j, sectors + j)
        )
        if j == 0:
            own_ref[...] = mine
        join(core_ref[0], vector, j, mine, other)
    half_products(sectors, left, vector, halves)
    sum_halves(count_ref[0], plan_ref, halves, sums)
    all_targets(sectors, right, sums, out_refs)


def call_product(kernel, sectors, lefts, rights, scalars, inside, kept):
    half_rows, columns = inside[-1].shape
    shape = (half_rows, columns)
    block_bytes = half_rows * columns * 2
    outs = [*kept, pltpu.VMEM(shape, jnp.float32)] + [pltpu.VMEM(shape, jnp.bfloat16)] * (sectors - 1)
    return pl.pallas_call(
        functools.partial(kernel, sectors),
        out_shape=outs,
        in_specs=[whole_smem] * len(scalars) + [whole_vmem] * len(inside),
        out_specs=[whole_vmem] * len(outs),
        scratch_shapes=[
            pltpu.VMEM((sectors, 2 * half_rows, columns), jnp.bfloat16),
            pltpu.VMEM((sectors * lefts, half_rows, columns), jnp.bfloat16),
            pltpu.VMEM((sectors * rights + 1, half_rows, columns), jnp.bfloat16),
        ],
        compiler_params=pltpu.CompilerParams(
            vmem_limit_bytes=block_bytes * (sectors * (lefts + rights + 24) + 64)
        ),
    )(
        *scalars,
        *(pltpu.with_memory_space_constraint(x, pltpu.VMEM) for x in inside),
    )


def swap(value, axis, bit):
    return lax.ppermute(value, axis, [(i, i ^ bit) for i in range(lax.axis_size(axis))])


def gather(own, kept):
    sectors = lax.axis_size("term")
    mine = {0: kept}
    for j in reversed(range(1, sectors)):
        mine[j] = swap(own, "term", j)
    other = {j: swap(mine[j], "pair", 1) for j in (0, *reversed(range(1, sectors)))}
    return [mine[j] for j in range(sectors)] + [other[j] for j in range(sectors)]


def owner_sum(parts):
    sent = {j: swap(parts[j], "term", j) for j in reversed(range(1, len(parts)))}
    total = parts[0]
    for j in range(1, len(parts)):
        total = total + sent[j].astype(jnp.float32)
    bit = 1
    while bit < lax.axis_size("sub"):
        rounded = total.astype(jnp.bfloat16)
        total = rounded.astype(jnp.float32) + swap(rounded, "sub", bit).astype(jnp.float32)
        bit *= 2
    return total


def on_device(
    psi,
    left_blocks,
    right_blocks,
    left_index,
    right_index,
    block_source,
    block_target,
    block_count,
    sector_energy,
):
    sectors = lax.axis_size("term")
    lefts, rights = left_blocks.shape[1], right_blocks.shape[1]
    me = lax.axis_index("term").astype(jnp.int32)
    core = lax.axis_index("pair").astype(jnp.int32).reshape(1)
    own = psi[0]
    left, right, own_kept = fetch(left_blocks[0], right_blocks[0], own)
    psis = gather(own, own_kept)
    indices = (left_index[0], right_index[0], block_source[0], block_target[0])
    plan = make_plan(me, *indices, block_count[0], sectors, lefts, rights)
    energy = sector_energy[0]
    call = functools.partial(
        call_product, sectors=sectors, lefts=lefts, rights=rights, scalars=(core, block_count, plan)
    )
    parts = call(first_kernel, inside=[left, right, *psis], kept=[])
    sigma_first = (owner_sum(parts) + energy * own.astype(jnp.float32)).astype(jnp.bfloat16)
    correction, *parts = call(
        second_kernel,
        inside=[left, right, *psis, *gather(sigma_first, sigma_first)],
        kept=[pltpu.VMEM(own.shape, own.dtype)],
    )
    sigma_second = (owner_sum(parts) + energy * correction.astype(jnp.float32)).astype(jnp.bfloat16)
    return (sigma_first[None], sigma_second[None])


def solution(mesh):
    placed = (
        P(("grp", "term"), "pair", None),
        P(("grp", "term", "sub"), None, "pair", None),
        P(("grp", "term", "sub"), None, None, None),
        P(("grp", "term", "sub"), None),
        P(("grp", "term", "sub"), None),
        P(("grp", "term", "sub"), None),
        P(("grp", "term", "sub"), None),
        P(("grp", "term", "sub")),
        P(("grp", "term")),
    )
    return jax.shard_map(
        on_device,
        mesh=mesh,
        in_specs=placed,
        out_specs=(P(("grp", "term"), "pair", None), P(("grp", "term"), "pair", None)),
        check_vma=False,
    )
```

time: 60 us -> 58 us (0.967)
  waiting for transfers between devices: 22.2 us -> 19.1 us
  starting transfers between devices: 23.8 us -> 24.9 us
    ppermute x22, waiting for transfers between devices: 22.2 us -> 19.1 us  [swap(): lax.ppermute(value, axis, [(i, i ^ bit) for i in range(lax.axis_size(axis...]
    pallas_call x0 -> x1, Pallas kernels: none -> 1.42 us  [fetch(): pl.pallas_call(fetch_kernel, out_shape=[pltpu.VMEM(x.shape, x.dtype) for...]
    pallas_call x2, Pallas kernels: 9.08 us -> 7.69 us  [call_product(): pl.pallas_call(functools.partial(kernel, sectors), out_shape=outs, in_spe...]
    ppermute x22, starting transfers between devices: 23.8 us -> 24.9 us  [swap(): lax.ppermute(value, axis, [(i, i ^ bit) for i in range(lax.axis_size(axis...]
  transfers between devices with their start and end apart: 22 -> 22, of which waited for: 14 -> 14; matrix products, arithmetic and copies ran while one was open for 1% -> 1% of each run, Pallas kernels for 0% -> 2%
where the time goes in v3:
time: 58 us; the launch traced here: 57.5 us
  starting transfers between devices  24.9 us (43%)
  waiting for transfers between devices  19.1 us (33%)
  Pallas kernels  9.1 us (16%)
  between operations  2.06 us (4%)
  local copies, waits for them, and re-layouts  1.33 us (2%)
  other arithmetic  1.07 us (2%)
    ppermute x22, starting transfers between devices, swap(): lax.ppermute(value, axis, [(i, i ^ bit) for i in range(lax.axis_size(axis...  24.9 us
    ppermute x22, waiting for transfers between devices, swap(): lax.ppermute(value, axis, [(i, i ^ bit) for i in range(lax.axis_size(axis...  19.1 us
    pallas_call x2, Pallas kernels, call_product(): pl.pallas_call(functools.partial(kernel, sectors), out_shape=outs, in_spe...  7.69 us
    pallas_call x1, Pallas kernels, fetch(): pl.pallas_call(fetch_kernel, out_shape=[pltpu.VMEM(x.shape, x.dtype) for...  1.42 us
    unnamed x12, local copies, waits for them, and re-layouts  1.33 us
  transfers between devices with their start and end apart: 22, of which 14 were waited for; matrix products, arithmetic and copies ran while one was open for 1% of the time, Pallas kernels for 2%

profile of v3, /device:TPU:0, one launch (start us, length us, event | category | flops | bytes accessed | tf_op | source)
XLA Modules:
  0.0 57.5 jit_solution(3838389945314880062)
XLA Ops:
  0.6 5.1 %collective-permute-start.2 = (bf16[128,256]{1,0:T(8,128)(2,1)}, bf16[128,256]{1,0:T(8,128)(2,1)S(1)}, u32[]{:S(2)}, u32[]{:S(2)}) collective-permute-start(bf16[128,256]{1,0:T(8,128)(2,1)} %bitcast.28), channel_id=1, source_target_pairs={{0,12},{4,8},{8,4},{12,0},{1,13},{5,9},{9,5},{13,1},{2,14},{6,10},... | collective-permute-start | bytes 196616 | tf_op jit(solution)/shard_map/ppermute | solution.py:167
  5.7 0.6 %collective-permute-start = (bf16[128,256]{1,0:T(8,128)(2,1)}, bf16[128,256]{1,0:T(8,128)(2,1)S(1)}, u32[]{:S(2)}, u32[]{:S(2)}) collective-permute-start(bf16[128,256]{1,0:T(8,128)(2,1)} %bitcast.30), channel_id=1, source_target_pairs={{0,4},{4,0},{8,12},{12,8},{1,5},{5,1},{9,13},{13,9},{2,6},{6,2},{1... | collective-permute-start | bytes 196616 | tf_op jit(solution)/shard_map/ppermute | solution.py:167
  6.4 1.4 %shard_map.104 = (bf16[8,128,256]{2,1,0:T(8,128)(2,1)S(1)}, bf16[8,256,256]{2,1,0:T(8,128)(2,1)S(1)}, bf16[128,256]{1,0:T(8,128)(2,1)S(1)}) custom-call(bf16[8,128,256]{2,1,0:T(8,128)(2,1)} %bitcast.27, bf16[8,256,256]{2,1,0:T(8,128)(2,1)} %bitcast.26, bf16[128,256]{1,0:T(8,128)(2,1)} %bitcast.31), custom_call_target="tpu_custom_call" | custom-call | tf_op jit(solution)/shard_map/pallas_call | solution.py:95
  8.6 0.6 %copy-done.4 = s32[1,72]{1,0:T(1,128)S(1)} copy-done((s32[1,72]{1,0:T(1,128)S(1)}, s32[1,72]{1,0:T(1,128)}, u32[]{:S(2)}) %copy-start.4) | copy-done | bytes 312
  9.4 0.6 %copy-done.2 = s32[1,72]{1,0:T(1,128)S(1)} copy-done((s32[1,72]{1,0:T(1,128)S(1)}, s32[1,72]{1,0:T(1,128)}, u32[]{:S(2)}) %copy-start.2) | copy-done | bytes 312
  10.2 0.6 collective-permute-start.6
  10.8 0.8 %collective-permute-done.1.refs_2_ = bf16[128,256]{1,0:T(8,128)(2,1)S(1)} collective-permute-done((bf16[128,256]{1,0:T(8,128)(2,1)}, bf16[128,256]{1,0:T(8,128)(2,1)S(1)}, u32[]{:S(2)}, u32[]{:S(2)}) %collective-permute-start.1) | collective-permute-done | bytes 65568 | tf_op jit(solution)/shard_map/ppermute | solution.py:167
  11.6 0.5 collective-permute-start.4
  12.1 0.7 %collective-permute-done.5.refs_6_ = bf16[128,256]{1,0:T(8,128)(2,1)S(1)} collective-permute-done((bf16[128,256]{1,0:T(8,128)(2,1)S(1)}, bf16[128,256]{1,0:T(8,128)(2,1)S(1)}, u32[]{:S(2)}, u32[]{:S(2)}) %collective-permute-start.5) | collective-permute-done | bytes 65568 | tf_op jit(solution)/shard_map/ppermute | solution.py:167
  13.0 3.5 %shard_map.105 = (f32[128,256]{1,0:T(8,128)S(1)}, bf16[128,256]{1,0:T(8,128)(2,1)S(1)}, bf16[128,256]{1,0:T(8,128)(2,1)S(1)}, bf16[128,256]{1,0:T(8,128)(2,1)S(1)}) custom-call(s32[1]{0:T(128)} %bitcast.core_ref, s32[1]{0:T(128)} %copy.11.count_ref, s32[72]{0:T(128)S(1)} %fusion.4.plan_ref, bf16[8,128,256]{2,1,0:T(8,128)(2,1)S(1)} %get-tuple-element.14.left, ...), custom_call_target="tpu_custom_call" | custom-call | tf_op jit(solution)/shard_map/pallas_call | solution.py:147
  16.4 0.6 collective-permute-start.7
  17.0 2.6 %collective-permute-start.8 = (bf16[128,256]{1,0:T(8,128)(2,1)S(1)}, bf16[128,256]{1,0:T(8,128)(2,1)S(1)}, u32[]{:S(2)}, u32[]{:S(2)}) collective-permute-start(bf16[128,256]{1,0:T(8,128)(2,1)S(1)} %get-tuple-element.19), channel_id=1, source_target_pairs={{0,8},{4,12},{8,0},{12,4},{1,9},{5,13},{9,1},{13,5},{2,10},{6,14},... | collective-permute-start | bytes 196616 | tf_op jit(solution)/shard_map/ppermute | solution.py:167
  19.6 1.3 %collective-permute-start.9 = (bf16[128,256]{1,0:T(8,128)(2,1)S(1)}, bf16[128,256]{1,0:T(8,128)(2,1)S(1)}, u32[]{:S(2)}, u32[]{:S(2)}) collective-permute-start(bf16[128,256]{1,0:T(8,128)(2,1)S(1)} %get-tuple-element.20), channel_id=1, source_target_pairs={{0,12},{4,8},{8,4},{12,0},{1,13},{5,9},{9,5},{13,1},{2,14},{6,10},... | collective-permute-start | bytes 196616 | tf_op jit(solution)/shard_map/ppermute | solution.py:167
  20.9 0.8 %collective-permute-done.7 = bf16[128,256]{1,0:T(8,128)(2,1)S(1)} collective-permute-done((bf16[128,256]{1,0:T(8,128)(2,1)S(1)}, bf16[128,256]{1,0:T(8,128)(2,1)S(1)}, u32[]{:S(2)}, u32[]{:S(2)}) %collective-permute-start.7) | collective-permute-done | bytes 65568 | tf_op jit(solution)/shard_map/ppermute | solution.py:167
  21.7 3.0 %collective-permute-done.8 = bf16[128,256]{1,0:T(8,128)(2,1)S(1)} collective-permute-done((bf16[128,256]{1,0:T(8,128)(2,1)S(1)}, bf16[128,256]{1,0:T(8,128)(2,1)S(1)}, u32[]{:S(2)}, u32[]{:S(2)}) %collective-permute-start.8) | collective-permute-done | bytes 65568 | tf_op jit(solution)/shard_map/ppermute | solution.py:167
  24.8 1.0 %collective-permute-done.9 = bf16[128,256]{1,0:T(8,128)(2,1)S(1)} collective-permute-done((bf16[128,256]{1,0:T(8,128)(2,1)S(1)}, bf16[128,256]{1,0:T(8,128)(2,1)S(1)}, u32[]{:S(2)}, u32[]{:S(2)}) %collective-permute-start.9) | collective-permute-done | bytes 65568 | tf_op jit(solution)/shard_map/ppermute | solution.py:167
  25.8 1.9 %collective-permute-start.10 = (bf16[128,256]{1,0:T(8,128)(2,1)S(1)}, bf16[128,256]{1,0:T(8,128)(2,1)S(1)}, u32[]{:S(2)}, u32[]{:S(2)}) collective-permute-start(bf16[128,256]{1,0:T(8,128)(2,1)S(1)} %add_convert_fusion.3), channel_id=1, source_target_pairs={{0,2},{2,0},{1,3},{3,1},{4,6},{6,4},{5,7},{7,5},{8,10},{10,8},{9,1... | collective-permute-start | bytes 196616 | tf_op jit(solution)/shard_map/ppermute | solution.py:167
  28.3 1.8 %collective-permute-done.10 = bf16[128,256]{1,0:T(8,128)(2,1)S(1)} collective-permute-done((bf16[128,256]{1,0:T(8,128)(2,1)S(1)}, bf16[128,256]{1,0:T(8,128)(2,1)S(1)}, u32[]{:S(2)}, u32[]{:S(2)}) %collective-permute-start.10) | collective-permute-done | bytes 65568 | tf_op jit(solution)/shard_map/ppermute | solution.py:167
  30.1 2.3 %collective-permute-start.13 = (bf16[128,256]{1,0:T(8,128)(2,1)S(1)}, bf16[128,256]{1,0:T(8,128)(2,1)S(1)}, u32[]{:S(2)}, u32[]{:S(2)}) collective-permute-start(bf16[128,256]{1,0:T(8,128)(2,1)S(1)} %add_convert_fusion.2.refs_8_), channel_id=1, source_target_pairs={{0,12},{4,8},{8,4},{12,0},{1,13},{5,9},{9,5},{13,1},{2,14},{6,10},... | collective-permute-start | bytes 196616 | tf_op jit(solution)/shard_map/ppermute | solution.py:167
  32.9 1.7 %collective-permute-start.11 = (bf16[128,256]{1,0:T(8,128)(2,1)S(1)}, bf16[128,256]{1,0:T(8,128)(2,1)S(1)}, u32[]{:S(2)}, u32[]{:S(2)}) collective-permute-start(bf16[128,256]{1,0:T(8,128)(2,1)S(1)} %add_convert_fusion.2.refs_8_), channel_id=1, source_target_pairs={{0,4},{4,0},{8,12},{12,8},{1,5},{5,1},{9,13},{13,9},{2,6},{6,2},{1... | collective-permute-start | bytes 196616 | tf_op jit(solution)/shard_map/ppermute | solution.py:167
  34.6 1.7 %collective-permute-done.13.refs_11_ = bf16[128,256]{1,0:T(8,128)(2,1)S(1)} collective-permute-done((bf16[128,256]{1,0:T(8,128)(2,1)S(1)}, bf16[128,256]{1,0:T(8,128)(2,1)S(1)}, u32[]{:S(2)}, u32[]{:S(2)}) %collective-permute-start.13) | collective-permute-done | bytes 65568 | tf_op jit(solution)/shard_map/ppermute | solution.py:167
  36.3 1.8 %collective-permute-done.12.refs_10_ = bf16[128,256]{1,0:T(8,128)(2,1)S(1)} collective-permute-done((bf16[128,256]{1,0:T(8,128)(2,1)S(1)}, bf16[128,256]{1,0:T(8,128)(2,1)S(1)}, u32[]{:S(2)}, u32[]{:S(2)}) %collective-permute-start.12) | collective-permute-done | bytes 65568 | tf_op jit(solution)/shard_map/ppermute | solution.py:167
  38.1 0.5 collective-permute-start.15
  38.6 0.7 %collective-permute-done.16.refs_14_ = bf16[128,256]{1,0:T(8,128)(2,1)S(1)} collective-permute-done((bf16[128,256]{1,0:T(8,128)(2,1)S(1)}, bf16[128,256]{1,0:T(8,128)(2,1)S(1)}, u32[]{:S(2)}, u32[]{:S(2)}) %collective-permute-start.16) | collective-permute-done | bytes 65568 | tf_op jit(solution)/shard_map/ppermute | solution.py:167
  39.5 4.2 %shard_map.106 = (bf16[128,256]{1,0:T(8,128)(2,1)S(1)}, f32[128,256]{1,0:T(8,128)S(1)}, bf16[128,256]{1,0:T(8,128)(2,1)S(1)}, bf16[128,256]{1,0:T(8,128)(2,1)S(1)}, bf16[128,256]{1,0:T(8,128)(2,1)S(1)}) custom-call(s32[1]{0:T(128)} %bitcast.core_ref, s32[1]{0:T(128)} %copy.11.count_ref, s32[72]{0:T(128)S(1)} %fusion.4.plan_ref, ...), custom_call_target="tpu_custom_call" | custom-call | tf_op jit(solution)/shard_map/pallas_call | solution.py:147
  44.0 1.9 %collective-permute-start.19 = (bf16[128,256]{1,0:T(8,128)(2,1)S(1)}, bf16[128,256]{1,0:T(8,128)(2,1)S(1)}, u32[]{:S(2)}, u32[]{:S(2)}) collective-permute-start(bf16[128,256]{1,0:T(8,128)(2,1)S(1)} %get-tuple-element.23), channel_id=1, source_target_pairs={{0,8},{4,12},{8,0},{12,4},{1,9},{5,13},{9,1},{13,5},{2,10},{6,14},... | collective-permute-start | bytes 196616 | tf_op jit(solution)/shard_map/ppermute | solution.py:167
  45.9 2.4 %collective-permute-start.20 = (bf16[128,256]{1,0:T(8,128)(2,1)S(1)}, bf16[128,256]{1,0:T(8,128)(2,1)S(1)}, u32[]{:S(2)}, u32[]{:S(2)}) collective-permute-start(bf16[128,256]{1,0:T(8,128)(2,1)S(1)} %get-tuple-element.24), channel_id=1, source_target_pairs={{0,12},{4,8},{8,4},{12,0},{1,13},{5,9},{9,5},{13,1},{2,14},{6,10},... | collective-permute-start | bytes 196616 | tf_op jit(solution)/shard_map/ppermute | solution.py:167
  48.3 1.1 %collective-permute-done.18 = bf16[128,256]{1,0:T(8,128)(2,1)S(1)} collective-permute-done((bf16[128,256]{1,0:T(8,128)(2,1)S(1)}, bf16[128,256]{1,0:T(8,128)(2,1)S(1)}, u32[]{:S(2)}, u32[]{:S(2)}) %collective-permute-start.18) | collective-permute-done | bytes 65568 | tf_op jit(solution)/shard_map/ppermute | solution.py:167
  49.3 3.1 %collective-permute-done.19 = bf16[128,256]{1,0:T(8,128)(2,1)S(1)} collective-permute-done((bf16[128,256]{1,0:T(8,128)(2,1)S(1)}, bf16[128,256]{1,0:T(8,128)(2,1)S(1)}, u32[]{:S(2)}, u32[]{:S(2)}) %collective-permute-start.19) | collective-permute-done | bytes 65568 | tf_op jit(solution)/shard_map/ppermute | solution.py:167
  52.4 2.2 %collective-permute-start.21 = (bf16[128,256]{1,0:T(8,128)(2,1)S(1)}, bf16[128,256]{1,0:T(8,128)(2,1)S(1)}, u32[]{:S(2)}, u32[]{:S(2)}) collective-permute-start(bf16[128,256]{1,0:T(8,128)(2,1)S(1)} %add_convert_fusion.1), channel_id=1, source_target_pairs={{0,2},{2,0},{1,3},{3,1},{4,6},{6,4},{5,7},{7,5},{8,10},{10,8},{9,1... | collective-permute-start | bytes 196616 | tf_op jit(solution)/shard_map/ppermute | solution.py:167
  54.6 2.2 %collective-permute-done.21 = bf16[128,256]{1,0:T(8,128)(2,1)S(1)} collective-permute-done((bf16[128,256]{1,0:T(8,128)(2,1)S(1)}, bf16[128,256]{1,0:T(8,128)(2,1)S(1)}, u32[]{:S(2)}, u32[]{:S(2)}) %collective-permute-start.21) | collective-permute-done | bytes 65568 | tf_op jit(solution)/shard_map/ppermute | solution.py:167
  56.8 0.7 %fusion = bf16[1,128,256]{2,1,0:T(8,128)(2,1)} fusion(bf16[128,256]{1,0:T(8,128)(2,1)S(1)} %get-tuple-element.25, bf16[128,256]{1,0:T(8,128)(2,1)S(1)} %collective-permute-done.21, bf16[128,256]{1,0:T(8,128)(2,1)S(1)} %add_convert_fusion.1, f32[]{:T(128)} %bitcast.24), kind=kLoop, calls=%fused_computation.4 | loop fusion | flops 229376 | bytes 262148 | tf_op jit(solution)/shard_map/broadcast_in_dim | solution.py:224
  (37 shorter events, 1.5 us)
Async XLA Ops:
  0.6 9.6 %collective-permute-start.2 = (bf16[128,256]{1,0:T(8,128)(2,1)}, bf16[128,256]{1,0:T(8,128)(2,1)S(1)}, u32[]{:S(2)}, u32[]{:S(2)}) collective-permute-start(bf16[128,256]{1,0:T(8,128)(2,1)} %bitcast.28), channel_id=1, source_target_pairs={{0,12},{4,8},{8,4},{12,0},{1,13},{5,9},{9,5},{13,1},{2,14},{6,10},... | collective-permute-start | bytes 196616 | tf_op jit(solution)/shard_map/ppermute | solution.py:167
  5.7 5.8 %collective-permute-start.1 = (bf16[128,256]{1,0:T(8,128)(2,1)}, bf16[128,256]{1,0:T(8,128)(2,1)S(1)}, u32[]{:S(2)}, u32[]{:S(2)}) collective-permute-start(bf16[128,256]{1,0:T(8,128)(2,1)} %bitcast.29), channel_id=1, source_target_pairs={{0,8},{4,12},{8,0},{12,4},{1,9},{5,13},{9,1},{13,5},{2,10},{6,14},... | collective-permute-start | bytes 196616 | tf_op jit(solution)/shard_map/ppermute | solution.py:167
  5.7 5.8 %collective-permute-start = (bf16[128,256]{1,0:T(8,128)(2,1)}, bf16[128,256]{1,0:T(8,128)(2,1)S(1)}, u32[]{:S(2)}, u32[]{:S(2)}) collective-permute-start(bf16[128,256]{1,0:T(8,128)(2,1)} %bitcast.30), channel_id=1, source_target_pairs={{0,4},{4,0},{8,12},{12,8},{1,5},{5,1},{9,13},{13,9},{2,6},{6,2},{1... | collective-permute-start | bytes 196616 | tf_op jit(solution)/shard_map/ppermute | solution.py:167
  7.8 4.3 %collective-permute-start.3 = (bf16[128,256]{1,0:T(8,128)(2,1)S(1)}, bf16[128,256]{1,0:T(8,128)(2,1)S(1)}, u32[]{:S(2)}, u32[]{:S(2)}) collective-permute-start(bf16[128,256]{1,0:T(8,128)(2,1)S(1)} %get-tuple-element.16.refs_0_), channel_id=1, source_target_pairs={{0,1},{1,0},{2,3},{3,2},{4,5},{5,4},{6,7},{7,6},{8,9},{9,8},{10,11... | collective-permute-start | bytes 196616 | tf_op jit(solution)/shard_map/ppermute | solution.py:167
  8.5 0.7 %copy-start.4 = (s32[1,72]{1,0:T(1,128)S(1)}, s32[1,72]{1,0:T(1,128)}, u32[]{:S(2)}) copy-start(s32[1,72]{1,0:T(1,128)} %param.15) | copy-start | bytes 868
  8.6 0.7 %copy-start.5 = (s32[1,72]{1,0:T(1,128)S(1)}, s32[1,72]{1,0:T(1,128)}, u32[]{:S(2)}) copy-start(s32[1,72]{1,0:T(1,128)} %param.13) | copy-start | bytes 868
  9.4 0.7 %copy-start.2 = (s32[1,72]{1,0:T(1,128)S(1)}, s32[1,72]{1,0:T(1,128)}, u32[]{:S(2)}) copy-start(s32[1,72]{1,0:T(1,128)} %param.12) | copy-start | bytes 868
  9.4 0.7 %copy-start.3 = (s32[1,72]{1,0:T(1,128)S(1)}, s32[1,72]{1,0:T(1,128)}, u32[]{:S(2)}) copy-start(s32[1,72]{1,0:T(1,128)} %param.14) | copy-start | bytes 868
  10.2 1.9 %collective-permute-start.6 = (bf16[128,256]{1,0:T(8,128)(2,1)S(1)}, bf16[128,256]{1,0:T(8,128)(2,1)S(1)}, u32[]{:S(2)}, u32[]{:S(2)}) collective-permute-start(bf16[128,256]{1,0:T(8,128)(2,1)S(1)} %collective-permute-done.2.refs_3_), channel_id=1, source_target_pairs={{0,1},{1,0},{2,3},{3,2},{4,5},{5,4},{6,7},{7,6},{8,9},{9,8},{10,11... | collective-permute-start | bytes 196616 | tf_op jit(solution)/shard_map/ppermute | solution.py:167
  11.6 1.3 %collective-permute-start.5 = (bf16[128,256]{1,0:T(8,128)(2,1)S(1)}, bf16[128,256]{1,0:T(8,128)(2,1)S(1)}, u32[]{:S(2)}, u32[]{:S(2)}) collective-permute-start(bf16[128,256]{1,0:T(8,128)(2,1)S(1)} %collective-permute-done.1.refs_2_), channel_id=1, source_target_pairs={{0,1},{1,0},{2,3},{3,2},{4,5},{5,4},{6,7},{7,6},{8,9},{9,8},{10,11... | collective-permute-start | bytes 196616 | tf_op jit(solution)/shard_map/ppermute | solution.py:167
  11.6 1.4 %collective-permute-start.4 = (bf16[128,256]{1,0:T(8,128)(2,1)S(1)}, bf16[128,256]{1,0:T(8,128)(2,1)S(1)}, u32[]{:S(2)}, u32[]{:S(2)}) collective-permute-start(bf16[128,256]{1,0:T(8,128)(2,1)S(1)} %collective-permute-done.refs_1_), channel_id=1, source_target_pairs={{0,1},{1,0},{2,3},{3,2},{4,5},{5,4},{6,7},{7,6},{8,9},{9,8},{10,11... | collective-permute-start | bytes 196616 | tf_op jit(solution)/shard_map/ppermute | solution.py:167
  16.4 5.3 %collective-permute-start.7 = (bf16[128,256]{1,0:T(8,128)(2,1)S(1)}, bf16[128,256]{1,0:T(8,128)(2,1)S(1)}, u32[]{:S(2)}, u32[]{:S(2)}) collective-permute-start(bf16[128,256]{1,0:T(8,128)(2,1)S(1)} %get-tuple-element.18), channel_id=1, source_target_pairs={{0,4},{4,0},{8,12},{12,8},{1,5},{5,1},{9,13},{13,9},{2,6},{6,2},{1... | collective-permute-start | bytes 196616 | tf_op jit(solution)/shard_map/ppermute | solution.py:167
  17.0 7.8 %collective-permute-start.8 = (bf16[128,256]{1,0:T(8,128)(2,1)S(1)}, bf16[128,256]{1,0:T(8,128)(2,1)S(1)}, u32[]{:S(2)}, u32[]{:S(2)}) collective-permute-start(bf16[128,256]{1,0:T(8,128)(2,1)S(1)} %get-tuple-element.19), channel_id=1, source_target_pairs={{0,8},{4,12},{8,0},{12,4},{1,9},{5,13},{9,1},{13,5},{2,10},{6,14},... | collective-permute-start | bytes 196616 | tf_op jit(solution)/shard_map/ppermute | solution.py:167
  19.6 6.1 %collective-permute-start.9 = (bf16[128,256]{1,0:T(8,128)(2,1)S(1)}, bf16[128,256]{1,0:T(8,128)(2,1)S(1)}, u32[]{:S(2)}, u32[]{:S(2)}) collective-permute-start(bf16[128,256]{1,0:T(8,128)(2,1)S(1)} %get-tuple-element.20), channel_id=1, source_target_pairs={{0,12},{4,8},{8,4},{12,0},{1,13},{5,9},{9,5},{13,1},{2,14},{6,10},... | collective-permute-start | bytes 196616 | tf_op jit(solution)/shard_map/ppermute | solution.py:167
  25.7 4.4 %copy-start.1 = (bf16[1,128,256]{2,1,0:T(8,128)(2,1)S(1)}, bf16[1,128,256]{2,1,0:T(8,128)(2,1)}, u32[]{:S(2)}) copy-start(bf16[1,128,256]{2,1,0:T(8,128)(2,1)} %param.9) | copy-start | bytes 196612
  25.8 4.3 %collective-permute-start.10 = (bf16[128,256]{1,0:T(8,128)(2,1)S(1)}, bf16[128,256]{1,0:T(8,128)(2,1)S(1)}, u32[]{:S(2)}, u32[]{:S(2)}) collective-permute-start(bf16[128,256]{1,0:T(8,128)(2,1)S(1)} %add_convert_fusion.3), channel_id=1, source_target_pairs={{0,2},{2,0},{1,3},{3,1},{4,6},{6,4},{5,7},{7,5},{8,10},{10,8},{9,1... | collective-permute-start | bytes 196616 | tf_op jit(solution)/shard_map/ppermute | solution.py:167
  30.1 13.6 %copy-start = (bf16[128,256]{1,0:T(8,128)(2,1)}, bf16[128,256]{1,0:T(8,128)(2,1)S(1)}, u32[]{:S(2)}) copy-start(bf16[128,256]{1,0:T(8,128)(2,1)S(1)} %add_convert_fusion.2.refs_8_) | copy-start | bytes 196612
  30.1 6.1 %collective-permute-start.13 = (bf16[128,256]{1,0:T(8,128)(2,1)S(1)}, bf16[128,256]{1,0:T(8,128)(2,1)S(1)}, u32[]{:S(2)}, u32[]{:S(2)}) collective-permute-start(bf16[128,256]{1,0:T(8,128)(2,1)S(1)} %add_convert_fusion.2.refs_8_), channel_id=1, source_target_pairs={{0,12},{4,8},{8,4},{12,0},{1,13},{5,9},{9,5},{13,1},{2,14},{6,10},... | collective-permute-start | bytes 196616 | tf_op jit(solution)/shard_map/ppermute | solution.py:167
  32.5 5.7 %collective-permute-start.12 = (bf16[128,256]{1,0:T(8,128)(2,1)S(1)}, bf16[128,256]{1,0:T(8,128)(2,1)S(1)}, u32[]{:S(2)}, u32[]{:S(2)}) collective-permute-start(bf16[128,256]{1,0:T(8,128)(2,1)S(1)} %add_convert_fusion.2.refs_8_), channel_id=1, source_target_pairs={{0,8},{4,12},{8,0},{12,4},{1,9},{5,13},{9,1},{13,5},{2,10},{6,14},... | collective-permute-start | bytes 196616 | tf_op jit(solution)/shard_map/ppermute | solution.py:167
  32.9 5.2 %collective-permute-start.11 = (bf16[128,256]{1,0:T(8,128)(2,1)S(1)}, bf16[128,256]{1,0:T(8,128)(2,1)S(1)}, u32[]{:S(2)}, u32[]{:S(2)}) collective-permute-start(bf16[128,256]{1,0:T(8,128)(2,1)S(1)} %add_convert_fusion.2.refs_8_), channel_id=1, source_target_pairs={{0,4},{4,0},{8,12},{12,8},{1,5},{5,1},{9,13},{13,9},{2,6},{6,2},{1... | collective-permute-start | bytes 196616 | tf_op jit(solution)/shard_map/ppermute | solution.py:167
  34.6 4.0 %collective-permute-start.14 = (bf16[128,256]{1,0:T(8,128)(2,1)S(1)}, bf16[128,256]{1,0:T(8,128)(2,1)S(1)}, u32[]{:S(2)}, u32[]{:S(2)}) collective-permute-start(bf16[128,256]{1,0:T(8,128)(2,1)S(1)} %add_convert_fusion.2.refs_8_), channel_id=1, source_target_pairs={{0,1},{1,0},{2,3},{3,2},{4,5},{5,4},{6,7},{7,6},{8,9},{9,8},{10,11... | collective-permute-start | bytes 196616 | tf_op jit(solution)/shard_map/ppermute | solution.py:167
  36.3 2.4 %collective-permute-start.17 = (bf16[128,256]{1,0:T(8,128)(2,1)S(1)}, bf16[128,256]{1,0:T(8,128)(2,1)S(1)}, u32[]{:S(2)}, u32[]{:S(2)}) collective-permute-start(bf16[128,256]{1,0:T(8,128)(2,1)S(1)} %collective-permute-done.13.refs_11_), channel_id=1, source_target_pairs={{0,1},{1,0},{2,3},{3,2},{4,5},{5,4},{6,7},{7,6},{8,9},{9,8},{10,11... | collective-permute-start | bytes 196616 | tf_op jit(solution)/shard_map/ppermute | solution.py:167
  38.1 1.3 %collective-permute-start.16 = (bf16[128,256]{1,0:T(8,128)(2,1)S(1)}, bf16[128,256]{1,0:T(8,128)(2,1)S(1)}, u32[]{:S(2)}, u32[]{:S(2)}) collective-permute-start(bf16[128,256]{1,0:T(8,128)(2,1)S(1)} %collective-permute-done.12.refs_10_), channel_id=1, source_target_pairs={{0,1},{1,0},{2,3},{3,2},{4,5},{5,4},{6,7},{7,6},{8,9},{9,8},{10,11... | collective-permute-start | bytes 196616 | tf_op jit(solution)/shard_map/ppermute | solution.py:167
  38.1 1.4 %collective-permute-start.15 = (bf16[128,256]{1,0:T(8,128)(2,1)S(1)}, bf16[128,256]{1,0:T(8,128)(2,1)S(1)}, u32[]{:S(2)}, u32[]{:S(2)}) collective-permute-start(bf16[128,256]{1,0:T(8,128)(2,1)S(1)} %collective-permute-done.11.refs_9_), channel_id=1, source_target_pairs={{0,1},{1,0},{2,3},{3,2},{4,5},{5,4},{6,7},{7,6},{8,9},{9,8},{10,11... | collective-permute-start | bytes 196616 | tf_op jit(solution)/shard_map/ppermute | solution.py:167
  43.8 5.5 %collective-permute-start.18 = (bf16[128,256]{1,0:T(8,128)(2,1)S(1)}, bf16[128,256]{1,0:T(8,128)(2,1)S(1)}, u32[]{:S(2)}, u32[]{:S(2)}) collective-permute-start(bf16[128,256]{1,0:T(8,128)(2,1)S(1)} %get-tuple-element.22), channel_id=1, source_target_pairs={{0,4},{4,0},{8,12},{12,8},{1,5},{5,1},{9,13},{13,9},{2,6},{6,2},{1... | collective-permute-start | bytes 196616 | tf_op jit(solution)/shard_map/ppermute | solution.py:167
  44.0 8.4 %collective-permute-start.19 = (bf16[128,256]{1,0:T(8,128)(2,1)S(1)}, bf16[128,256]{1,0:T(8,128)(2,1)S(1)}, u32[]{:S(2)}, u32[]{:S(2)}) collective-permute-start(bf16[128,256]{1,0:T(8,128)(2,1)S(1)} %get-tuple-element.23), channel_id=1, source_target_pairs={{0,8},{4,12},{8,0},{12,4},{1,9},{5,13},{9,1},{13,5},{2,10},{6,14},... | collective-permute-start | bytes 196616 | tf_op jit(solution)/shard_map/ppermute | solution.py:167
  45.9 6.5 %collective-permute-start.20 = (bf16[128,256]{1,0:T(8,128)(2,1)S(1)}, bf16[128,256]{1,0:T(8,128)(2,1)S(1)}, u32[]{:S(2)}, u32[]{:S(2)}) collective-permute-start(bf16[128,256]{1,0:T(8,128)(2,1)S(1)} %get-tuple-element.24), channel_id=1, source_target_pairs={{0,12},{4,8},{8,4},{12,0},{1,13},{5,9},{9,5},{13,1},{2,14},{6,10},... | collective-permute-start | bytes 196616 | tf_op jit(solution)/shard_map/ppermute | solution.py:167
  52.4 4.4 %collective-permute-start.21 = (bf16[128,256]{1,0:T(8,128)(2,1)S(1)}, bf16[128,256]{1,0:T(8,128)(2,1)S(1)}, u32[]{:S(2)}, u32[]{:S(2)}) collective-permute-start(bf16[128,256]{1,0:T(8,128)(2,1)S(1)} %add_convert_fusion.1), channel_id=1, source_target_pairs={{0,2},{2,0},{1,3},{3,1},{4,6},{6,4},{5,7},{7,5},{8,10},{10,8},{9,1... | collective-permute-start | bytes 196616 | tf_op jit(solution)/shard_map/ppermute | solution.py:167

commit v4 on v3

--- a/solution.py
+++ b/solution.py
@@ -7,29 +7,41 @@
 from jax.experimental.pallas import tpu as pltpu
 from jax.sharding import PartitionSpec as P
 
+four_order = [0, 2, 1, 3]
+direct_distances = (3,)
 unroll_slots = 4
 wide_sectors = 4
 step_lefts = 2
 whole_vmem = pl.BlockSpec(memory_space=pltpu.VMEM)
-whole_smem = pl.BlockSpec(memory_space=pltpu.SMEM)
 stays_out = pl.BlockSpec(memory_space=pltpu.HBM)
+
+
+def target_order(sectors):
+    return four_order if sectors == 4 else list(range(sectors))
+
+
+def plan_length(slots):
+    return -(-(slots + unroll_slots) // 128) * 128
 
 
 def make_plan(me, left_index, right_index, source, target, live, sectors, lefts, rights):
     slots = left_index.shape[0]
-    padded = -(-slots // unroll_slots) * unroll_slots
+    length = plan_length(slots)
     number = jnp.arange(slots, dtype=jnp.int32)
     alive = number < live
-    group = jnp.where(alive, right_index * sectors + (target ^ me), rights * sectors)
+    distance = target ^ me
+    sent_at = sum(jnp.where(distance == far, place, 0) for place, far in enumerate(target_order(sectors)))
+    group = jnp.where(alive, right_index * sectors + sent_at, rights * sectors)
     half = jnp.where(alive, (source ^ me) * lefts + left_index, 0)
     same = group[None, :] == group[:, None]
     before = number[None, :] < number[:, None]
     place = jnp.sum(((group[None, :] < group[:, None]) | (same & before)).astype(jnp.int32), axis=1)
     goes_on = jnp.max((same & before).astype(jnp.int32), axis=1)
     word = half + (group << 12) + (goes_on << 24)
-    put = place[None, :] == jnp.arange(padded, dtype=jnp.int32)[:, None]
-    empty = jnp.arange(padded, dtype=jnp.int32) >= slots
-    return jnp.sum(jnp.where(put, word[None, :], 0), axis=1) + jnp.where(empty, (rights * sectors) << 12, 0)
+    at = jnp.arange(length, dtype=jnp.int32)
+    sorted_words = jnp.sum(jnp.where(place[None, :] == at[:, None], word[None, :], 0), axis=1)
+    rest = jnp.where(at == length - 1, live, (rights * sectors) << 12)
+    return jnp.where(at < slots, sorted_words, rest)[None]
 
 
 def half_products(sectors, left_ref, vector, halves):
@@ -43,15 +55,18 @@
             half = jnp.dot(rows, wide, preferred_element_type=jnp.float32).astype(jnp.bfloat16)
             for place, j in enumerate(chosen):
                 part = half[:, place * columns : (place + 1) * columns]
-                halves[j * lefts + left : j * lefts + left + step_lefts] = part.reshape(-1, half_rows, columns)
-
-
-def sum_halves(live, plan_ref, halves, sums):
+                part = part.reshape(-1, half_rows, columns).astype(jnp.float32)
+                halves[j * lefts + left : j * lefts + left + step_lefts] = part
+
+
+def sum_halves(plan_ref, halves, sums):
+    live = plan_ref[0, plan_ref.shape[1] - 1]
+
     def some_slots(turn, total):
         for step in range(unroll_slots):
-            word = plan_ref[turn * unroll_slots + step]
+            word = plan_ref[0, turn * unroll_slots + step]
             keep = (word >> 24).astype(jnp.float32)
-            total = total * keep + halves[word & 4095].astype(jnp.float32)
+            total = total * keep + halves[word & 4095]
             sums[(word >> 12) & 4095] = total.astype(jnp.bfloat16)
         return total
 
@@ -101,22 +116,29 @@
     )(*(pltpu.with_memory_space_constraint(x, pltpu.HBM) for x in arrays))
 
 
-def first_kernel(sectors, core_ref, count_ref, plan_ref, left, right, *refs):
-    psis, out_refs = refs[: 2 * sectors], refs[2 * sectors : -3]
-    vector, halves, sums = refs[-3:]
+def first_kernel(sectors, plan_in, left, right, *refs):
+    psis, out_refs = refs[: 2 * sectors], refs[2 * sectors : -5]
+    plan_ref, arrived, vector, halves, sums = refs[-5:]
+    core = lax.axis_index("pair")
+    plan_copy = pltpu.make_async_copy(plan_in, plan_ref, arrived)
+    plan_copy.start()
     sums[...] = jnp.zeros_like(sums)
     for j in range(sectors):
-        join(core_ref[0], vector, j, psis[j][...], psis[sectors + j][...])
+        join(core, vector, j, psis[j][...], psis[sectors + j][...])
     half_products(sectors, left, vector, halves)
-    sum_halves(count_ref[0], plan_ref, halves, sums)
+    plan_copy.wait()
+    sum_halves(plan_ref, halves, sums)
     all_targets(sectors, right, sums, out_refs)
 
 
-def second_kernel(sectors, core_ref, count_ref, plan_ref, left, right, *refs):
+def second_kernel(sectors, plan_in, left, right, *refs):
     pieces = 2 * sectors
     psis, sigmas = refs[:pieces], refs[pieces : 2 * pieces]
-    own_ref, *out_refs = refs[2 * pieces : -3]
-    vector, halves, sums = refs[-3:]
+    own_ref, *out_refs = refs[2 * pieces : -5]
+    plan_ref, arrived, vector, halves, sums = refs[-5:]
+    core = lax.axis_index("pair")
+    plan_copy = pltpu.make_async_copy(plan_in, plan_ref, arrived)
+    plan_copy.start()
     sums[...] = jnp.zeros_like(sums)
     norm = sum(wide_of(p) * wide_of(p) for p in psis)
     correlation = sum(wide_of(p) * wide_of(s) for p, s in zip(psis, sigmas))
@@ -133,13 +155,14 @@
         )
         if j == 0:
             own_ref[...] = mine
-        join(core_ref[0], vector, j, mine, other)
+        join(core, vector, j, mine, other)
     half_products(sectors, left, vector, halves)
-    sum_halves(count_ref[0], plan_ref, halves, sums)
+    plan_copy.wait()
+    sum_halves(plan_ref, halves, sums)
     all_targets(sectors, right, sums, out_refs)
 
 
-def call_product(kernel, sectors, lefts, rights, scalars, inside, kept):
+def call_product(kernel, sectors, lefts, rights, inside, kept):
     half_rows, columns = inside[-1].shape
     shape = (half_rows, columns)
     block_bytes = half_rows * columns * 2
@@ -147,20 +170,19 @@
     return pl.pallas_call(
         functools.partial(kernel, sectors),
         out_shape=outs,
-        in_specs=[whole_smem] * len(scalars) + [whole_vmem] * len(inside),
+        in_specs=[whole_vmem] * len(inside),
         out_specs=[whole_vmem] * len(outs),
         scratch_shapes=[
+            pltpu.SMEM(inside[0].shape, jnp.int32),
+            pltpu.SemaphoreType.DMA,
             pltpu.VMEM((sectors, 2 * half_rows, columns), jnp.bfloat16),
-            pltpu.VMEM((sectors * lefts, half_rows, columns), jnp.bfloat16),
+            pltpu.VMEM((sectors * lefts, half_rows, columns), jnp.float32),
             pltpu.VMEM((sectors * rights + 1, half_rows, columns), jnp.bfloat16),
         ],
         compiler_params=pltpu.CompilerParams(
-            vmem_limit_bytes=block_bytes * (sectors * (lefts + rights + 24) + 64)
+            vmem_limit_bytes=block_bytes * (sectors * (2 * lefts + rights + 24) + 64)
         ),
-    )(
-        *scalars,
-        *(pltpu.with_memory_space_constraint(x, pltpu.VMEM) for x in inside),
-    )
+    )(*(pltpu.with_memory_space_constraint(x, pltpu.VMEM) for x in inside))
 
 
 def swap(value, axis, bit):
@@ -176,16 +198,28 @@
     return [mine[j] for j in range(sectors)] + [other[j] for j in range(sectors)]
 
 
+def send(value, far, across):
+    sectors, subs = lax.axis_size("term"), lax.axis_size("sub")
+    route = [(t * subs + s, (t ^ far) * subs + (s ^ across)) for t in range(sectors) for s in range(subs)]
+    return lax.ppermute(value, ("term", "sub"), route)
+
+
 def owner_sum(parts):
-    sent = {j: swap(parts[j], "term", j) for j in reversed(range(1, len(parts)))}
+    subs = lax.axis_size("sub")
+    order = target_order(len(parts))
+    direct = [far for far in order if far in direct_distances and subs == 2 and len(parts) == 4]
     total = parts[0]
-    for j in range(1, len(parts)):
-        total = total + sent[j].astype(jnp.float32)
+    for place, far in enumerate(order):
+        if place > 0 and far not in direct:
+            total = total + send(parts[place], far, 0).astype(jnp.float32)
+    beside = [send(parts[order.index(far)], far, across).astype(jnp.float32) for far in direct for across in range(subs)]
     bit = 1
-    while bit < lax.axis_size("sub"):
+    while bit < subs:
         rounded = total.astype(jnp.bfloat16)
-        total = rounded.astype(jnp.float32) + swap(rounded, "sub", bit).astype(jnp.float32)
+        total = rounded.astype(jnp.float32) + send(rounded, 0, bit).astype(jnp.float32)
         bit *= 2
+    for one, two in zip(beside[::2], beside[1::2]):
+        total = total + (one + two)
     return total
 
 
@@ -203,21 +237,18 @@
     sectors = lax.axis_size("term")
     lefts, rights = left_blocks.shape[1], right_blocks.shape[1]
     me = lax.axis_index("term").astype(jnp.int32)
-    core = lax.axis_index("pair").astype(jnp.int32).reshape(1)
     own = psi[0]
     left, right, own_kept = fetch(left_blocks[0], right_blocks[0], own)
     psis = gather(own, own_kept)
     indices = (left_index[0], right_index[0], block_source[0], block_target[0])
     plan = make_plan(me, *indices, block_count[0], sectors, lefts, rights)
     energy = sector_energy[0]
-    call = functools.partial(
-        call_product, sectors=sectors, lefts=lefts, rights=rights, scalars=(core, block_count, plan)
-    )
-    parts = call(first_kernel, inside=[left, right, *psis], kept=[])
+    call = functools.partial(call_product, sectors=sectors, lefts=lefts, rights=rights)
+    parts = call(first_kernel, inside=[plan, left, right, *psis], kept=[])
     sigma_first = (owner_sum(parts) + energy * own.astype(jnp.float32)).astype(jnp.bfloat16)
     correction, *parts = call(
         second_kernel,
-        inside=[left, right, *psis, *gather(sigma_first, sigma_first)],
+        inside=[plan, left, right, *psis, *gather(sigma_first, sigma_first)],
         kept=[pltpu.VMEM(own.shape, own.dtype)],
     )
     sigma_second = (owner_sum(parts) + energy * correction.astype(jnp.float32)).astype(jnp.bfloat16)

time: 58 us -> 54.2 us (0.934)
  waiting for transfers between devices: 19.1 us -> 12.6 us
  starting transfers between devices: 24.9 us -> 30.2 us
  Pallas kernels: 9.1 us -> 6.61 us
    ppermute x0 -> x10, starting transfers between devices: none -> 18.3 us  [send(): return lax.ppermute(value, ('term', 'sub'), route)]
    ppermute x22 -> x14, starting transfers between devices: 24.9 us -> 11.9 us  [swap(): lax.ppermute(value, axis, [(i, i ^ bit) for i in range(lax.axis_size(axis...]
    ppermute x22 -> x14, waiting for transfers between devices: 19.1 us -> 6.46 us  [swap(): lax.ppermute(value, axis, [(i, i ^ bit) for i in range(lax.axis_size(axis...]
    ppermute x0 -> x10, waiting for transfers between devices: none -> 6.12 us  [send(): return lax.ppermute(value, ('term', 'sub'), route)]
    pallas_call x2, Pallas kernels: 7.69 us -> 5.19 us  [call_product(): pl.pallas_call(functools.partial(kernel, sectors), out_shape=outs, in_spe...]
  transfers between devices with their start and end apart: 22 -> 24, of which waited for: 14 -> 13; matrix products, arithmetic and copies ran while one was open for 1% -> 1% of each run, Pallas kernels for 2% -> 3%
where the time goes in v4:
time: 54.2 us; the launch traced here: 53.8 us
  starting transfers between devices  30.2 us (56%)
  waiting for transfers between devices  12.6 us (23%)
  Pallas kernels  6.61 us (12%)
  between operations  2.07 us (4%)
  local copies, waits for them, and re-layouts  1.33 us (2%)
  other arithmetic  1.08 us (2%)
    ppermute x10, starting transfers between devices, send(): return lax.ppermute(value, ('term', 'sub'), route)  18.3 us
    ppermute x14, starting transfers between devices, swap(): lax.ppermute(value, axis, [(i, i ^ bit) for i in range(lax.axis_size(axis...  11.9 us
    ppermute x14, waiting for transfers between devices, swap(): lax.ppermute(value, axis, [(i, i ^ bit) for i in range(lax.axis_size(axis...  6.46 us
    ppermute x10, waiting for transfers between devices, send(): return lax.ppermute(value, ('term', 'sub'), route)  6.12 us
    pallas_call x2, Pallas kernels, call_product(): pl.pallas_call(functools.partial(kernel, sectors), out_shape=outs, in_spe...  5.19 us
    pallas_call x1, Pallas kernels, fetch(): pl.pallas_call(fetch_kernel, out_shape=[pltpu.VMEM(x.shape, x.dtype) for...  1.42 us
    unnamed x12, local copies, waits for them, and re-layouts  1.33 us
  transfers between devices with their start and end apart: 24, of which 13 were waited for; matrix products, arithmetic and copies ran while one was open for 1% of the time, Pallas kernels for 3%

profile of v4, /device:TPU:0, one launch (start us, length us, event | category | flops | bytes accessed | tf_op | source)
XLA Modules:
  0.0 53.8 jit_solution(11395569769124789802)
XLA Ops:
  0.6 5.1 %collective-permute-start.2 = (bf16[128,256]{1,0:T(8,128)(2,1)}, bf16[128,256]{1,0:T(8,128)(2,1)S(1)}, u32[]{:S(2)}, u32[]{:S(2)}) collective-permute-start(bf16[128,256]{1,0:T(8,128)(2,1)} %bitcast.30), channel_id=1, source_target_pairs={{0,12},{4,8},{8,4},{12,0},{1,13},{5,9},{9,5},{13,1},{2,14},{6,10},... | collective-permute-start | bytes 196616 | tf_op jit(solution)/shard_map/ppermute | solution.py:189
  5.7 0.6 %collective-permute-start = (bf16[128,256]{1,0:T(8,128)(2,1)}, bf16[128,256]{1,0:T(8,128)(2,1)S(1)}, u32[]{:S(2)}, u32[]{:S(2)}) collective-permute-start(bf16[128,256]{1,0:T(8,128)(2,1)} %bitcast.32), channel_id=1, source_target_pairs={{0,4},{4,0},{8,12},{12,8},{1,5},{5,1},{9,13},{13,9},{2,6},{6,2},{1... | collective-permute-start | bytes 196616 | tf_op jit(solution)/shard_map/ppermute | solution.py:189
  6.4 1.4 %shard_map.104 = (bf16[8,128,256]{2,1,0:T(8,128)(2,1)S(1)}, bf16[8,256,256]{2,1,0:T(8,128)(2,1)S(1)}, bf16[128,256]{1,0:T(8,128)(2,1)S(1)}) custom-call(bf16[8,128,256]{2,1,0:T(8,128)(2,1)} %bitcast.29, bf16[8,256,256]{2,1,0:T(8,128)(2,1)} %bitcast.28, bf16[128,256]{1,0:T(8,128)(2,1)} %bitcast.33), custom_call_target="tpu_custom_call" | custom-call | tf_op jit(solution)/shard_map/pallas_call | solution.py:110
  8.6 0.6 %copy-done.4 = s32[1,72]{1,0:T(1,128)S(1)} copy-done((s32[1,72]{1,0:T(1,128)S(1)}, s32[1,72]{1,0:T(1,128)}, u32[]{:S(2)}) %copy-start.4) | copy-done | bytes 312
  9.4 0.6 %copy-done.2 = s32[1,72]{1,0:T(1,128)S(1)} copy-done((s32[1,72]{1,0:T(1,128)S(1)}, s32[1,72]{1,0:T(1,128)}, u32[]{:S(2)}) %copy-start.2) | copy-done | bytes 312
  10.2 0.6 %collective-permute-start.6 = (bf16[128,256]{1,0:T(8,128)(2,1)S(1)}, bf16[128,256]{1,0:T(8,128)(2,1)S(1)}, u32[]{:S(2)}, u32[]{:S(2)}) collective-permute-start(bf16[128,256]{1,0:T(8,128)(2,1)S(1)} %collective-permute-done.2.refs_3_), channel_id=1, source_target_pairs={{0,1},{1,0},{2,3},{3,2},{4,5},{5,4},{6,7},{7,6},{8,9},{9,8},{10,11... | collective-permute-start | bytes 196616 | tf_op jit(solution)/shard_map/ppermute | solution.py:189
  10.8 0.8 %collective-permute-done.1.refs_2_ = bf16[128,256]{1,0:T(8,128)(2,1)S(1)} collective-permute-done((bf16[128,256]{1,0:T(8,128)(2,1)}, bf16[128,256]{1,0:T(8,128)(2,1)S(1)}, u32[]{:S(2)}, u32[]{:S(2)}) %collective-permute-start.1) | collective-permute-done | bytes 65568 | tf_op jit(solution)/shard_map/ppermute | solution.py:189
  11.6 0.5 collective-permute-start.4
  12.1 0.7 %collective-permute-done.5.refs_6_ = bf16[128,256]{1,0:T(8,128)(2,1)S(1)} collective-permute-done((bf16[128,256]{1,0:T(8,128)(2,1)S(1)}, bf16[128,256]{1,0:T(8,128)(2,1)S(1)}, u32[]{:S(2)}, u32[]{:S(2)}) %collective-permute-start.5) | collective-permute-done | bytes 65568 | tf_op jit(solution)/shard_map/ppermute | solution.py:189
  13.0 2.2 %shard_map.105 = (f32[128,256]{1,0:T(8,128)S(1)}, bf16[128,256]{1,0:T(8,128)(2,1)S(1)}, bf16[128,256]{1,0:T(8,128)(2,1)S(1)}, bf16[128,256]{1,0:T(8,128)(2,1)S(1)}) custom-call(s32[1,128]{1,0:T(1,128)S(1)} %compare_select_fusion.5.plan_in, bf16[8,128,256]{2,1,0:T(8,128)(2,1)S(1)} %get-tuple-element.14.left, ...), custom_call_target="tpu_custom_call" | custom-call | tf_op jit(solution)/shard_map/pallas_call | solution.py:170
  15.2 2.0 %collective-permute-start.7 = (bf16[128,256]{1,0:T(8,128)(2,1)S(1)}, bf16[128,256]{1,0:T(8,128)(2,1)S(1)}, u32[]{:S(2)}, u32[]{:S(2)}) collective-permute-start(bf16[128,256]{1,0:T(8,128)(2,1)S(1)} %get-tuple-element.18), channel_id=1, source_target_pairs={{0,8},{2,10},{4,12},{6,14},{8,0},{10,2},{12,4},{14,6},{1,9},{3,11}... | collective-permute-start | bytes 196616 | tf_op jit(solution)/shard_map/ppermute | solution.py:204
  17.2 2.1 %collective-permute-start.8 = (bf16[128,256]{1,0:T(8,128)(2,1)S(1)}, bf16[128,256]{1,0:T(8,128)(2,1)S(1)}, u32[]{:S(2)}, u32[]{:S(2)}) collective-permute-start(bf16[128,256]{1,0:T(8,128)(2,1)S(1)} %get-tuple-element.19), channel_id=1, source_target_pairs={{0,4},{2,6},{4,0},{6,2},{8,12},{10,14},{12,8},{14,10},{1,5},{3,7},... | collective-permute-start | bytes 196616 | tf_op jit(solution)/shard_map/ppermute | solution.py:204
  19.3 1.6 %collective-permute-start.11 = (bf16[128,256]{1,0:T(8,128)(2,1)S(1)}, bf16[128,256]{1,0:T(8,128)(2,1)S(1)}, u32[]{:S(2)}, u32[]{:S(2)}) collective-permute-start(bf16[128,256]{1,0:T(8,128)(2,1)S(1)} %get-tuple-element.20), channel_id=1, source_target_pairs={{0,14},{2,12},{4,10},{6,8},{8,6},{10,4},{12,2},{14,0},{1,15},{3,13... | collective-permute-start | bytes 196616 | tf_op jit(solution)/shard_map/ppermute | solution.py:204
  20.9 2.8 %collective-permute-start.10 = (bf16[128,256]{1,0:T(8,128)(2,1)S(1)}, bf16[128,256]{1,0:T(8,128)(2,1)S(1)}, u32[]{:S(2)}, u32[]{:S(2)}) collective-permute-start(bf16[128,256]{1,0:T(8,128)(2,1)S(1)} %get-tuple-element.20), channel_id=1, source_target_pairs={{0,12},{2,14},{4,8},{6,10},{8,4},{10,6},{12,0},{14,2},{1,13},{3,15... | collective-permute-start | bytes 196616 | tf_op jit(solution)/shard_map/ppermute | solution.py:204
  23.7 1.0 %collective-permute-start.9 = (bf16[128,256]{1,0:T(8,128)(2,1)S(1)}, bf16[128,256]{1,0:T(8,128)(2,1)S(1)}, u32[]{:S(2)}, u32[]{:S(2)}) collective-permute-start(bf16[128,256]{1,0:T(8,128)(2,1)S(1)} %add_convert_fusion.3), channel_id=1, source_target_pairs={{0,2},{2,0},{4,6},{6,4},{8,10},{10,8},{12,14},{14,12},{1,3},{3,1},... | collective-permute-start | bytes 196616 | tf_op jit(solution)/shard_map/ppermute | solution.py:204
  25.4 1.3 %collective-permute-done.11 = bf16[128,256]{1,0:T(8,128)(2,1)S(1)} collective-permute-done((bf16[128,256]{1,0:T(8,128)(2,1)S(1)}, bf16[128,256]{1,0:T(8,128)(2,1)S(1)}, u32[]{:S(2)}, u32[]{:S(2)}) %collective-permute-start.11) | collective-permute-done | bytes 65568 | tf_op jit(solution)/shard_map/ppermute | solution.py:204
  27.0 1.1 %collective-permute-done.9 = bf16[128,256]{1,0:T(8,128)(2,1)S(1)} collective-permute-done((bf16[128,256]{1,0:T(8,128)(2,1)S(1)}, bf16[128,256]{1,0:T(8,128)(2,1)S(1)}, u32[]{:S(2)}, u32[]{:S(2)}) %collective-permute-start.9) | collective-permute-done | bytes 65568 | tf_op jit(solution)/shard_map/ppermute | solution.py:204
  28.1 2.1 %collective-permute-start.14 = (bf16[128,256]{1,0:T(8,128)(2,1)S(1)}, bf16[128,256]{1,0:T(8,128)(2,1)S(1)}, u32[]{:S(2)}, u32[]{:S(2)}) collective-permute-start(bf16[128,256]{1,0:T(8,128)(2,1)S(1)} %add_convert_fusion.2.refs_8_), channel_id=1, source_target_pairs={{0,12},{4,8},{8,4},{12,0},{1,13},{5,9},{9,5},{13,1},{2,14},{6,10},... | collective-permute-start | bytes 196616 | tf_op jit(solution)/shard_map/ppermute | solution.py:189
  30.2 2.4 %collective-permute-start.12 = (bf16[128,256]{1,0:T(8,128)(2,1)S(1)}, bf16[128,256]{1,0:T(8,128)(2,1)S(1)}, u32[]{:S(2)}, u32[]{:S(2)}) collective-permute-start(bf16[128,256]{1,0:T(8,128)(2,1)S(1)} %add_convert_fusion.2.refs_8_), channel_id=1, source_target_pairs={{0,4},{4,0},{8,12},{12,8},{1,5},{5,1},{9,13},{13,9},{2,6},{6,2},{1... | collective-permute-start | bytes 196616 | tf_op jit(solution)/shard_map/ppermute | solution.py:189
  32.6 2.3 %collective-permute-done.14.refs_11_ = bf16[128,256]{1,0:T(8,128)(2,1)S(1)} collective-permute-done((bf16[128,256]{1,0:T(8,128)(2,1)S(1)}, bf16[128,256]{1,0:T(8,128)(2,1)S(1)}, u32[]{:S(2)}, u32[]{:S(2)}) %collective-permute-start.14) | collective-permute-done | bytes 65568 | tf_op jit(solution)/shard_map/ppermute | solution.py:189
  34.9 1.5 %collective-permute-done.13.refs_10_ = bf16[128,256]{1,0:T(8,128)(2,1)S(1)} collective-permute-done((bf16[128,256]{1,0:T(8,128)(2,1)S(1)}, bf16[128,256]{1,0:T(8,128)(2,1)S(1)}, u32[]{:S(2)}, u32[]{:S(2)}) %collective-permute-start.13) | collective-permute-done | bytes 65568 | tf_op jit(solution)/shard_map/ppermute | solution.py:189
  37.0 0.7 %collective-permute-done.17.refs_14_ = bf16[128,256]{1,0:T(8,128)(2,1)S(1)} collective-permute-done((bf16[128,256]{1,0:T(8,128)(2,1)S(1)}, bf16[128,256]{1,0:T(8,128)(2,1)S(1)}, u32[]{:S(2)}, u32[]{:S(2)}) %collective-permute-start.17) | collective-permute-done | bytes 65568 | tf_op jit(solution)/shard_map/ppermute | solution.py:189
  37.9 3.0 %shard_map.106 = (bf16[128,256]{1,0:T(8,128)(2,1)S(1)}, f32[128,256]{1,0:T(8,128)S(1)}, bf16[128,256]{1,0:T(8,128)(2,1)S(1)}, bf16[128,256]{1,0:T(8,128)(2,1)S(1)}, bf16[128,256]{1,0:T(8,128)(2,1)S(1)}) custom-call(s32[1,128]{1,0:T(1,128)S(1)} %compare_select_fusion.5.plan_in, bf16[8,128,256]{2,1,0:T(8,128)(2,1)S(1)} %get-tuple-element.14.left, ...), custom_call_target="tpu_custom_call" | custom-call | tf_op jit(solution)/shard_map/pallas_call | solution.py:170
  40.9 1.3 %collective-permute-start.19 = (bf16[128,256]{1,0:T(8,128)(2,1)S(1)}, bf16[128,256]{1,0:T(8,128)(2,1)S(1)}, u32[]{:S(2)}, u32[]{:S(2)}) collective-permute-start(bf16[128,256]{1,0:T(8,128)(2,1)S(1)} %get-tuple-element.22), channel_id=1, source_target_pairs={{0,8},{2,10},{4,12},{6,14},{8,0},{10,2},{12,4},{14,6},{1,9},{3,11}... | collective-permute-start | bytes 196616 | tf_op jit(solution)/shard_map/ppermute | solution.py:204
  42.2 2.0 %collective-permute-start.20 = (bf16[128,256]{1,0:T(8,128)(2,1)S(1)}, bf16[128,256]{1,0:T(8,128)(2,1)S(1)}, u32[]{:S(2)}, u32[]{:S(2)}) collective-permute-start(bf16[128,256]{1,0:T(8,128)(2,1)S(1)} %get-tuple-element.23), channel_id=1, source_target_pairs={{0,4},{2,6},{4,0},{6,2},{8,12},{10,14},{12,8},{14,10},{1,5},{3,7},... | collective-permute-start | bytes 196616 | tf_op jit(solution)/shard_map/ppermute | solution.py:204
  44.2 2.1 %collective-permute-start.23 = (bf16[128,256]{1,0:T(8,128)(2,1)S(1)}, bf16[128,256]{1,0:T(8,128)(2,1)S(1)}, u32[]{:S(2)}, u32[]{:S(2)}) collective-permute-start(bf16[128,256]{1,0:T(8,128)(2,1)S(1)} %get-tuple-element.24), channel_id=1, source_target_pairs={{0,14},{2,12},{4,10},{6,8},{8,6},{10,4},{12,2},{14,0},{1,15},{3,13... | collective-permute-start | bytes 196616 | tf_op jit(solution)/shard_map/ppermute | solution.py:204
  46.3 2.5 %collective-permute-start.22 = (bf16[128,256]{1,0:T(8,128)(2,1)S(1)}, bf16[128,256]{1,0:T(8,128)(2,1)S(1)}, u32[]{:S(2)}, u32[]{:S(2)}) collective-permute-start(bf16[128,256]{1,0:T(8,128)(2,1)S(1)} %get-tuple-element.24), channel_id=1, source_target_pairs={{0,12},{2,14},{4,8},{6,10},{8,4},{10,6},{12,0},{14,2},{1,13},{3,15... | collective-permute-start | bytes 196616 | tf_op jit(solution)/shard_map/ppermute | solution.py:204
  48.8 0.9 %collective-permute-start.21 = (bf16[128,256]{1,0:T(8,128)(2,1)S(1)}, bf16[128,256]{1,0:T(8,128)(2,1)S(1)}, u32[]{:S(2)}, u32[]{:S(2)}) collective-permute-start(bf16[128,256]{1,0:T(8,128)(2,1)S(1)} %add_convert_fusion.1), channel_id=1, source_target_pairs={{0,2},{2,0},{4,6},{6,4},{8,10},{10,8},{12,14},{14,12},{1,3},{3,1},... | collective-permute-start | bytes 196616 | tf_op jit(solution)/shard_map/ppermute | solution.py:204
  49.8 1.9 %collective-permute-done.23 = bf16[128,256]{1,0:T(8,128)(2,1)S(1)} collective-permute-done((bf16[128,256]{1,0:T(8,128)(2,1)S(1)}, bf16[128,256]{1,0:T(8,128)(2,1)S(1)}, u32[]{:S(2)}, u32[]{:S(2)}) %collective-permute-start.23) | collective-permute-done | bytes 65568 | tf_op jit(solution)/shard_map/ppermute | solution.py:204
  51.7 0.7 %collective-permute-done.22 = bf16[128,256]{1,0:T(8,128)(2,1)S(1)} collective-permute-done((bf16[128,256]{1,0:T(8,128)(2,1)S(1)}, bf16[128,256]{1,0:T(8,128)(2,1)S(1)}, u32[]{:S(2)}, u32[]{:S(2)}) %collective-permute-start.22) | collective-permute-done | bytes 65568 | tf_op jit(solution)/shard_map/ppermute | solution.py:204
  52.4 0.8 %collective-permute-done.21 = bf16[128,256]{1,0:T(8,128)(2,1)S(1)} collective-permute-done((bf16[128,256]{1,0:T(8,128)(2,1)S(1)}, bf16[128,256]{1,0:T(8,128)(2,1)S(1)}, u32[]{:S(2)}, u32[]{:S(2)}) %collective-permute-start.21) | collective-permute-done | bytes 65568 | tf_op jit(solution)/shard_map/ppermute | solution.py:204
  53.2 0.7 %fusion = bf16[1,128,256]{2,1,0:T(8,128)(2,1)} fusion(bf16[128,256]{1,0:T(8,128)(2,1)S(1)} %get-tuple-element.25, bf16[128,256]{1,0:T(8,128)(2,1)S(1)} %collective-permute-done.23, bf16[128,256]{1,0:T(8,128)(2,1)S(1)} %collective-permute-done.22, bf16[128,256]{1,0:T(8,128)(2,1)S(1)} %collective-permute-done.21, bf16[128,256]{1,0:T(8,128)(2,1)S(1)} %add_convert_fusion.1, ...), kind=kLoop, calls=%fused_computation.4 | loop fusion | flops 360448 | bytes 393220 | tf_op jit(solution)/shard_map/broadcast_in_dim | solution.py:255
  (41 shorter events, 1.7 us)
Async XLA Ops:
  0.6 9.6 %collective-permute-start.2 = (bf16[128,256]{1,0:T(8,128)(2,1)}, bf16[128,256]{1,0:T(8,128)(2,1)S(1)}, u32[]{:S(2)}, u32[]{:S(2)}) collective-permute-start(bf16[128,256]{1,0:T(8,128)(2,1)} %bitcast.30), channel_id=1, source_target_pairs={{0,12},{4,8},{8,4},{12,0},{1,13},{5,9},{9,5},{13,1},{2,14},{6,10},... | collective-permute-start | bytes 196616 | tf_op jit(solution)/shard_map/ppermute | solution.py:189
  5.7 5.8 %collective-permute-start.1 = (bf16[128,256]{1,0:T(8,128)(2,1)}, bf16[128,256]{1,0:T(8,128)(2,1)S(1)}, u32[]{:S(2)}, u32[]{:S(2)}) collective-permute-start(bf16[128,256]{1,0:T(8,128)(2,1)} %bitcast.31), channel_id=1, source_target_pairs={{0,8},{4,12},{8,0},{12,4},{1,9},{5,13},{9,1},{13,5},{2,10},{6,14},... | collective-permute-start | bytes 196616 | tf_op jit(solution)/shard_map/ppermute | solution.py:189
  5.7 5.8 %collective-permute-start = (bf16[128,256]{1,0:T(8,128)(2,1)}, bf16[128,256]{1,0:T(8,128)(2,1)S(1)}, u32[]{:S(2)}, u32[]{:S(2)}) collective-permute-start(bf16[128,256]{1,0:T(8,128)(2,1)} %bitcast.32), channel_id=1, source_target_pairs={{0,4},{4,0},{8,12},{12,8},{1,5},{5,1},{9,13},{13,9},{2,6},{6,2},{1... | collective-permute-start | bytes 196616 | tf_op jit(solution)/shard_map/ppermute | solution.py:189
  7.8 4.3 %collective-permute-start.3 = (bf16[128,256]{1,0:T(8,128)(2,1)S(1)}, bf16[128,256]{1,0:T(8,128)(2,1)S(1)}, u32[]{:S(2)}, u32[]{:S(2)}) collective-permute-start(bf16[128,256]{1,0:T(8,128)(2,1)S(1)} %get-tuple-element.16.refs_0_), channel_id=1, source_target_pairs={{0,1},{1,0},{2,3},{3,2},{4,5},{5,4},{6,7},{7,6},{8,9},{9,8},{10,11... | collective-permute-start | bytes 196616 | tf_op jit(solution)/shard_map/ppermute | solution.py:189
  8.5 0.7 %copy-start.4 = (s32[1,72]{1,0:T(1,128)S(1)}, s32[1,72]{1,0:T(1,128)}, u32[]{:S(2)}) copy-start(s32[1,72]{1,0:T(1,128)} %param.15) | copy-start | bytes 868
  8.6 0.7 %copy-start.5 = (s32[1,72]{1,0:T(1,128)S(1)}, s32[1,72]{1,0:T(1,128)}, u32[]{:S(2)}) copy-start(s32[1,72]{1,0:T(1,128)} %param.13) | copy-start | bytes 868
  9.4 0.7 %copy-start.2 = (s32[1,72]{1,0:T(1,128)S(1)}, s32[1,72]{1,0:T(1,128)}, u32[]{:S(2)}) copy-start(s32[1,72]{1,0:T(1,128)} %param.12) | copy-start | bytes 868
  9.4 0.7 %copy-start.3 = (s32[1,72]{1,0:T(1,128)S(1)}, s32[1,72]{1,0:T(1,128)}, u32[]{:S(2)}) copy-start(s32[1,72]{1,0:T(1,128)} %param.14) | copy-start | bytes 868
  10.2 1.9 %collective-permute-start.6 = (bf16[128,256]{1,0:T(8,128)(2,1)S(1)}, bf16[128,256]{1,0:T(8,128)(2,1)S(1)}, u32[]{:S(2)}, u32[]{:S(2)}) collective-permute-start(bf16[128,256]{1,0:T(8,128)(2,1)S(1)} %collective-permute-done.2.refs_3_), channel_id=1, source_target_pairs={{0,1},{1,0},{2,3},{3,2},{4,5},{5,4},{6,7},{7,6},{8,9},{9,8},{10,11... | collective-permute-start | bytes 196616 | tf_op jit(solution)/shard_map/ppermute | solution.py:189
  11.6 1.3 %collective-permute-start.5 = (bf16[128,256]{1,0:T(8,128)(2,1)S(1)}, bf16[128,256]{1,0:T(8,128)(2,1)S(1)}, u32[]{:S(2)}, u32[]{:S(2)}) collective-permute-start(bf16[128,256]{1,0:T(8,128)(2,1)S(1)} %collective-permute-done.1.refs_2_), channel_id=1, source_target_pairs={{0,1},{1,0},{2,3},{3,2},{4,5},{5,4},{6,7},{7,6},{8,9},{9,8},{10,11... | collective-permute-start | bytes 196616 | tf_op jit(solution)/shard_map/ppermute | solution.py:189
  11.6 1.4 %collective-permute-start.4 = (bf16[128,256]{1,0:T(8,128)(2,1)S(1)}, bf16[128,256]{1,0:T(8,128)(2,1)S(1)}, u32[]{:S(2)}, u32[]{:S(2)}) collective-permute-start(bf16[128,256]{1,0:T(8,128)(2,1)S(1)} %collective-permute-done.refs_1_), channel_id=1, source_target_pairs={{0,1},{1,0},{2,3},{3,2},{4,5},{5,4},{6,7},{7,6},{8,9},{9,8},{10,11... | collective-permute-start | bytes 196616 | tf_op jit(solution)/shard_map/ppermute | solution.py:189
  15.2 8.5 %collective-permute-start.7 = (bf16[128,256]{1,0:T(8,128)(2,1)S(1)}, bf16[128,256]{1,0:T(8,128)(2,1)S(1)}, u32[]{:S(2)}, u32[]{:S(2)}) collective-permute-start(bf16[128,256]{1,0:T(8,128)(2,1)S(1)} %get-tuple-element.18), channel_id=1, source_target_pairs={{0,8},{2,10},{4,12},{6,14},{8,0},{10,2},{12,4},{14,6},{1,9},{3,11}... | collective-permute-start | bytes 196616 | tf_op jit(solution)/shard_map/ppermute | solution.py:204
  17.2 6.5 %collective-permute-start.8 = (bf16[128,256]{1,0:T(8,128)(2,1)S(1)}, bf16[128,256]{1,0:T(8,128)(2,1)S(1)}, u32[]{:S(2)}, u32[]{:S(2)}) collective-permute-start(bf16[128,256]{1,0:T(8,128)(2,1)S(1)} %get-tuple-element.19), channel_id=1, source_target_pairs={{0,4},{2,6},{4,0},{6,2},{8,12},{10,14},{12,8},{14,10},{1,5},{3,7},... | collective-permute-start | bytes 196616 | tf_op jit(solution)/shard_map/ppermute | solution.py:204
  19.3 7.4 %collective-permute-start.11 = (bf16[128,256]{1,0:T(8,128)(2,1)S(1)}, bf16[128,256]{1,0:T(8,128)(2,1)S(1)}, u32[]{:S(2)}, u32[]{:S(2)}) collective-permute-start(bf16[128,256]{1,0:T(8,128)(2,1)S(1)} %get-tuple-element.20), channel_id=1, source_target_pairs={{0,14},{2,12},{4,10},{6,8},{8,6},{10,4},{12,2},{14,0},{1,15},{3,13... | collective-permute-start | bytes 196616 | tf_op jit(solution)/shard_map/ppermute | solution.py:204
  20.9 6.1 %collective-permute-start.10 = (bf16[128,256]{1,0:T(8,128)(2,1)S(1)}, bf16[128,256]{1,0:T(8,128)(2,1)S(1)}, u32[]{:S(2)}, u32[]{:S(2)}) collective-permute-start(bf16[128,256]{1,0:T(8,128)(2,1)S(1)} %get-tuple-element.20), channel_id=1, source_target_pairs={{0,12},{2,14},{4,8},{6,10},{8,4},{10,6},{12,0},{14,2},{1,13},{3,15... | collective-permute-start | bytes 196616 | tf_op jit(solution)/shard_map/ppermute | solution.py:204
  23.7 4.4 %copy-start.1 = (bf16[1,128,256]{2,1,0:T(8,128)(2,1)S(1)}, bf16[1,128,256]{2,1,0:T(8,128)(2,1)}, u32[]{:S(2)}) copy-start(bf16[1,128,256]{2,1,0:T(8,128)(2,1)} %param.9) | copy-start | bytes 196612
  23.7 4.3 %collective-permute-start.9 = (bf16[128,256]{1,0:T(8,128)(2,1)S(1)}, bf16[128,256]{1,0:T(8,128)(2,1)S(1)}, u32[]{:S(2)}, u32[]{:S(2)}) collective-permute-start(bf16[128,256]{1,0:T(8,128)(2,1)S(1)} %add_convert_fusion.3), channel_id=1, source_target_pairs={{0,2},{2,0},{4,6},{6,4},{8,10},{10,8},{12,14},{14,12},{1,3},{3,1},... | collective-permute-start | bytes 196616 | tf_op jit(solution)/shard_map/ppermute | solution.py:204
  28.1 12.8 %copy-start = (bf16[128,256]{1,0:T(8,128)(2,1)}, bf16[128,256]{1,0:T(8,128)(2,1)S(1)}, u32[]{:S(2)}) copy-start(bf16[128,256]{1,0:T(8,128)(2,1)S(1)} %add_convert_fusion.2.refs_8_) | copy-start | bytes 196612
  28.1 6.8 %collective-permute-start.14 = (bf16[128,256]{1,0:T(8,128)(2,1)S(1)}, bf16[128,256]{1,0:T(8,128)(2,1)S(1)}, u32[]{:S(2)}, u32[]{:S(2)}) collective-permute-start(bf16[128,256]{1,0:T(8,128)(2,1)S(1)} %add_convert_fusion.2.refs_8_), channel_id=1, source_target_pairs={{0,12},{4,8},{8,4},{12,0},{1,13},{5,9},{9,5},{13,1},{2,14},{6,10},... | collective-permute-start | bytes 196616 | tf_op jit(solution)/shard_map/ppermute | solution.py:189
  30.2 6.3 %collective-permute-start.13 = (bf16[128,256]{1,0:T(8,128)(2,1)S(1)}, bf16[128,256]{1,0:T(8,128)(2,1)S(1)}, u32[]{:S(2)}, u32[]{:S(2)}) collective-permute-start(bf16[128,256]{1,0:T(8,128)(2,1)S(1)} %add_convert_fusion.2.refs_8_), channel_id=1, source_target_pairs={{0,8},{4,12},{8,0},{12,4},{1,9},{5,13},{9,1},{13,5},{2,10},{6,14},... | collective-permute-start | bytes 196616 | tf_op jit(solution)/shard_map/ppermute | solution.py:189
  30.2 6.3 %collective-permute-start.12 = (bf16[128,256]{1,0:T(8,128)(2,1)S(1)}, bf16[128,256]{1,0:T(8,128)(2,1)S(1)}, u32[]{:S(2)}, u32[]{:S(2)}) collective-permute-start(bf16[128,256]{1,0:T(8,128)(2,1)S(1)} %add_convert_fusion.2.refs_8_), channel_id=1, source_target_pairs={{0,4},{4,0},{8,12},{12,8},{1,5},{5,1},{9,13},{13,9},{2,6},{6,2},{1... | collective-permute-start | bytes 196616 | tf_op jit(solution)/shard_map/ppermute | solution.py:189
  32.6 4.4 %collective-permute-start.15 = (bf16[128,256]{1,0:T(8,128)(2,1)S(1)}, bf16[128,256]{1,0:T(8,128)(2,1)S(1)}, u32[]{:S(2)}, u32[]{:S(2)}) collective-permute-start(bf16[128,256]{1,0:T(8,128)(2,1)S(1)} %add_convert_fusion.2.refs_8_), channel_id=1, source_target_pairs={{0,1},{1,0},{2,3},{3,2},{4,5},{5,4},{6,7},{7,6},{8,9},{9,8},{10,11... | collective-permute-start | bytes 196616 | tf_op jit(solution)/shard_map/ppermute | solution.py:189
  34.9 2.1 %collective-permute-start.18 = (bf16[128,256]{1,0:T(8,128)(2,1)S(1)}, bf16[128,256]{1,0:T(8,128)(2,1)S(1)}, u32[]{:S(2)}, u32[]{:S(2)}) collective-permute-start(bf16[128,256]{1,0:T(8,128)(2,1)S(1)} %collective-permute-done.14.refs_11_), channel_id=1, source_target_pairs={{0,1},{1,0},{2,3},{3,2},{4,5},{5,4},{6,7},{7,6},{8,9},{9,8},{10,11... | collective-permute-start | bytes 196616 | tf_op jit(solution)/shard_map/ppermute | solution.py:189
  36.5 1.3 %collective-permute-start.17 = (bf16[128,256]{1,0:T(8,128)(2,1)S(1)}, bf16[128,256]{1,0:T(8,128)(2,1)S(1)}, u32[]{:S(2)}, u32[]{:S(2)}) collective-permute-start(bf16[128,256]{1,0:T(8,128)(2,1)S(1)} %collective-permute-done.13.refs_10_), channel_id=1, source_target_pairs={{0,1},{1,0},{2,3},{3,2},{4,5},{5,4},{6,7},{7,6},{8,9},{9,8},{10,11... | collective-permute-start | bytes 196616 | tf_op jit(solution)/shard_map/ppermute | solution.py:189
  36.5 1.4 %collective-permute-start.16 = (bf16[128,256]{1,0:T(8,128)(2,1)S(1)}, bf16[128,256]{1,0:T(8,128)(2,1)S(1)}, u32[]{:S(2)}, u32[]{:S(2)}) collective-permute-start(bf16[128,256]{1,0:T(8,128)(2,1)S(1)} %collective-permute-done.12.refs_9_), channel_id=1, source_target_pairs={{0,1},{1,0},{2,3},{3,2},{4,5},{5,4},{6,7},{7,6},{8,9},{9,8},{10,11... | collective-permute-start | bytes 196616 | tf_op jit(solution)/shard_map/ppermute | solution.py:189
  40.9 7.9 %collective-permute-start.19 = (bf16[128,256]{1,0:T(8,128)(2,1)S(1)}, bf16[128,256]{1,0:T(8,128)(2,1)S(1)}, u32[]{:S(2)}, u32[]{:S(2)}) collective-permute-start(bf16[128,256]{1,0:T(8,128)(2,1)S(1)} %get-tuple-element.22), channel_id=1, source_target_pairs={{0,8},{2,10},{4,12},{6,14},{8,0},{10,2},{12,4},{14,6},{1,9},{3,11}... | collective-permute-start | bytes 196616 | tf_op jit(solution)/shard_map/ppermute | solution.py:204
  42.2 6.6 %collective-permute-start.20 = (bf16[128,256]{1,0:T(8,128)(2,1)S(1)}, bf16[128,256]{1,0:T(8,128)(2,1)S(1)}, u32[]{:S(2)}, u32[]{:S(2)}) collective-permute-start(bf16[128,256]{1,0:T(8,128)(2,1)S(1)} %get-tuple-element.23), channel_id=1, source_target_pairs={{0,4},{2,6},{4,0},{6,2},{8,12},{10,14},{12,8},{14,10},{1,5},{3,7},... | collective-permute-start | bytes 196616 | tf_op jit(solution)/shard_map/ppermute | solution.py:204
  44.2 7.5 %collective-permute-start.23 = (bf16[128,256]{1,0:T(8,128)(2,1)S(1)}, bf16[128,256]{1,0:T(8,128)(2,1)S(1)}, u32[]{:S(2)}, u32[]{:S(2)}) collective-permute-start(bf16[128,256]{1,0:T(8,128)(2,1)S(1)} %get-tuple-element.24), channel_id=1, source_target_pairs={{0,14},{2,12},{4,10},{6,8},{8,6},{10,4},{12,2},{14,0},{1,15},{3,13... | collective-permute-start | bytes 196616 | tf_op jit(solution)/shard_map/ppermute | solution.py:204
  46.3 6.1 %collective-permute-start.22 = (bf16[128,256]{1,0:T(8,128)(2,1)S(1)}, bf16[128,256]{1,0:T(8,128)(2,1)S(1)}, u32[]{:S(2)}, u32[]{:S(2)}) collective-permute-start(bf16[128,256]{1,0:T(8,128)(2,1)S(1)} %get-tuple-element.24), channel_id=1, source_target_pairs={{0,12},{2,14},{4,8},{6,10},{8,4},{10,6},{12,0},{14,2},{1,13},{3,15... | collective-permute-start | bytes 196616 | tf_op jit(solution)/shard_map/ppermute | solution.py:204
  48.8 4.3 %collective-permute-start.21 = (bf16[128,256]{1,0:T(8,128)(2,1)S(1)}, bf16[128,256]{1,0:T(8,128)(2,1)S(1)}, u32[]{:S(2)}, u32[]{:S(2)}) collective-permute-start(bf16[128,256]{1,0:T(8,128)(2,1)S(1)} %add_convert_fusion.1), channel_id=1, source_target_pairs={{0,2},{2,0},{4,6},{6,4},{8,10},{10,8},{12,14},{14,12},{1,3},{3,1},... | collective-permute-start | bytes 196616 | tf_op jit(solution)/shard_map/ppermute | solution.py:204

commit v5 on v4

--- a/solution.py
+++ b/solution.py
@@ -7,7 +7,8 @@
 from jax.experimental.pallas import tpu as pltpu
 from jax.sharding import PartitionSpec as P
 
-four_order = [0, 2, 1, 3]
+gather_four = [0, 1, 3, 2]
+target_four = [0, 2, 1, 3]
 direct_distances = (3,)
 unroll_slots = 4
 wide_sectors = 4
@@ -16,8 +17,16 @@
 stays_out = pl.BlockSpec(memory_space=pltpu.HBM)
 
 
+def gather_order(sectors):
+    return gather_four if sectors == 4 else list(range(sectors))
+
+
 def target_order(sectors):
-    return four_order if sectors == 4 else list(range(sectors))
+    return target_four if sectors == 4 else list(range(sectors))
+
+
+def place_in(order, distance):
+    return sum(jnp.where(distance == far, place, 0) for place, far in enumerate(order))
 
 
 def plan_length(slots):
@@ -29,10 +38,9 @@
     length = plan_length(slots)
     number = jnp.arange(slots, dtype=jnp.int32)
     alive = number < live
-    distance = target ^ me
-    sent_at = sum(jnp.where(distance == far, place, 0) for place, far in enumerate(target_order(sectors)))
+    sent_at = place_in(target_order(sectors), target ^ me)
     group = jnp.where(alive, right_index * sectors + sent_at, rights * sectors)
-    half = jnp.where(alive, (source ^ me) * lefts + left_index, 0)
+    half = jnp.where(alive, place_in(gather_order(sectors), source ^ me) * lefts + left_index, 0)
     same = group[None, :] == group[:, None]
     before = number[None, :] < number[:, None]
     place = jnp.sum(((group[None, :] < group[:, None]) | (same & before)).astype(jnp.int32), axis=1)
@@ -191,9 +199,10 @@
 
 def gather(own, kept):
     sectors = lax.axis_size("term")
+    order = gather_order(sectors)
     mine = {0: kept}
     for j in reversed(range(1, sectors)):
-        mine[j] = swap(own, "term", j)
+        mine[j] = swap(own, "term", order[j])
     other = {j: swap(mine[j], "pair", 1) for j in (0, *reversed(range(1, sectors)))}
     return [mine[j] for j in range(sectors)] + [other[j] for j in range(sectors)]
 

time: 54.2 us -> 53.9 us (level)
  starting transfers between devices: 30.2 us -> 28.6 us
  waiting for transfers between devices: 12.6 us -> 13.5 us
    ppermute x14, starting transfers between devices: 11.9 us -> 10.4 us  [swap(): lax.ppermute(value, axis, [(i, i ^ bit) for i in range(lax.axis_size(axis...]
    ppermute x14, waiting for transfers between devices: 6.46 us -> 7.53 us  [swap(): lax.ppermute(value, axis, [(i, i ^ bit) for i in range(lax.axis_size(axis...]
  transfers between devices with their start and end apart: 24 -> 24, of which waited for: 13 -> 15; matrix products, arithmetic and copies ran while one was open for 1% -> 1% of each run, Pallas kernels for 3% -> 3%
where the time goes in v5:
time: 53.9 us; the launch traced here: 53.4 us
  starting transfers between devices  28.6 us (53%)
  waiting for transfers between devices  13.5 us (25%)
  Pallas kernels  6.85 us (13%)
  between operations  2.07 us (4%)
  local copies, waits for them, and re-layouts  1.33 us (2%)
  other arithmetic  1.08 us (2%)
    ppermute x10, starting transfers between devices, send(): return lax.ppermute(value, ('term', 'sub'), route)  18.1 us
    ppermute x14, starting transfers between devices, swap(): lax.ppermute(value, axis, [(i, i ^ bit) for i in range(lax.axis_size(axis...  10.4 us
    ppermute x14, waiting for transfers between devices, swap(): lax.ppermute(value, axis, [(i, i ^ bit) for i in range(lax.axis_size(axis...  7.53 us
    ppermute x10, waiting for transfers between devices, send(): return lax.ppermute(value, ('term', 'sub'), route)  5.95 us
    pallas_call x2, Pallas kernels, call_product(): pl.pallas_call(functools.partial(kernel, sectors), out_shape=outs, in_spe...  5.43 us
    pallas_call x1, Pallas kernels, fetch(): pl.pallas_call(fetch_kernel, out_shape=[pltpu.VMEM(x.shape, x.dtype) for...  1.42 us
    unnamed x12, local copies, waits for them, and re-layouts  1.33 us
  transfers between devices with their start and end apart: 24, of which 15 were waited for; matrix products, arithmetic and copies ran while one was open for 1% of the time, Pallas kernels for 3%

profile of v5, /device:TPU:0, one launch (start us, length us, event | category | flops | bytes accessed | tf_op | source)
XLA Modules:
  0.0 53.4 jit_solution(10525092765596740353)
XLA Ops:
  0.6 4.1 %collective-permute-start.2 = (bf16[128,256]{1,0:T(8,128)(2,1)}, bf16[128,256]{1,0:T(8,128)(2,1)S(1)}, u32[]{:S(2)}, u32[]{:S(2)}) collective-permute-start(bf16[128,256]{1,0:T(8,128)(2,1)} %bitcast.30), channel_id=1, source_target_pairs={{0,8},{4,12},{8,0},{12,4},{1,9},{5,13},{9,1},{13,5},{2,10},{6,14},... | collective-permute-start | bytes 196616 | tf_op jit(solution)/shard_map/ppermute | solution.py:197
  4.7 1.3 %collective-permute-start.1 = (bf16[128,256]{1,0:T(8,128)(2,1)}, bf16[128,256]{1,0:T(8,128)(2,1)S(1)}, u32[]{:S(2)}, u32[]{:S(2)}) collective-permute-start(bf16[128,256]{1,0:T(8,128)(2,1)} %bitcast.31), channel_id=1, source_target_pairs={{0,12},{4,8},{8,4},{12,0},{1,13},{5,9},{9,5},{13,1},{2,14},{6,10},... | collective-permute-start | bytes 196616 | tf_op jit(solution)/shard_map/ppermute | solution.py:197
  6.3 1.4 %shard_map.104 = (bf16[8,128,256]{2,1,0:T(8,128)(2,1)S(1)}, bf16[8,256,256]{2,1,0:T(8,128)(2,1)S(1)}, bf16[128,256]{1,0:T(8,128)(2,1)S(1)}) custom-call(bf16[8,128,256]{2,1,0:T(8,128)(2,1)} %bitcast.29, bf16[8,256,256]{2,1,0:T(8,128)(2,1)} %bitcast.28, bf16[128,256]{1,0:T(8,128)(2,1)} %bitcast.33), custom_call_target="tpu_custom_call" | custom-call | tf_op jit(solution)/shard_map/pallas_call | solution.py:118
  8.5 0.6 %copy-done.4 = s32[1,72]{1,0:T(1,128)S(1)} copy-done((s32[1,72]{1,0:T(1,128)S(1)}, s32[1,72]{1,0:T(1,128)}, u32[]{:S(2)}) %copy-start.4) | copy-done | bytes 312
  9.4 0.6 %copy-done.2 = s32[1,72]{1,0:T(1,128)S(1)} copy-done((s32[1,72]{1,0:T(1,128)S(1)}, s32[1,72]{1,0:T(1,128)}, u32[]{:S(2)}) %copy-start.2) | copy-done | bytes 312
  10.1 0.6 %collective-permute-start.6 = (bf16[128,256]{1,0:T(8,128)(2,1)S(1)}, bf16[128,256]{1,0:T(8,128)(2,1)S(1)}, u32[]{:S(2)}, u32[]{:S(2)}) collective-permute-start(bf16[128,256]{1,0:T(8,128)(2,1)S(1)} %collective-permute-done.2.refs_3_), channel_id=1, source_target_pairs={{0,1},{1,0},{2,3},{3,2},{4,5},{5,4},{6,7},{7,6},{8,9},{9,8},{10,11... | collective-permute-start | bytes 196616 | tf_op jit(solution)/shard_map/ppermute | solution.py:197
  11.7 0.7 %collective-permute-done.5.refs_6_ = bf16[128,256]{1,0:T(8,128)(2,1)S(1)} collective-permute-done((bf16[128,256]{1,0:T(8,128)(2,1)S(1)}, bf16[128,256]{1,0:T(8,128)(2,1)S(1)}, u32[]{:S(2)}, u32[]{:S(2)}) %collective-permute-start.5) | collective-permute-done | bytes 65568 | tf_op jit(solution)/shard_map/ppermute | solution.py:197
  12.6 2.3 %shard_map.105 = (f32[128,256]{1,0:T(8,128)S(1)}, bf16[128,256]{1,0:T(8,128)(2,1)S(1)}, bf16[128,256]{1,0:T(8,128)(2,1)S(1)}, bf16[128,256]{1,0:T(8,128)(2,1)S(1)}) custom-call(s32[1,128]{1,0:T(1,128)S(1)} %compare_select_fusion.8.plan_in, bf16[8,128,256]{2,1,0:T(8,128)(2,1)S(1)} %get-tuple-element.14.left, ...), custom_call_target="tpu_custom_call" | custom-call | tf_op jit(solution)/shard_map/pallas_call | solution.py:178
  14.9 3.2 %collective-permute-start.7 = (bf16[128,256]{1,0:T(8,128)(2,1)S(1)}, bf16[128,256]{1,0:T(8,128)(2,1)S(1)}, u32[]{:S(2)}, u32[]{:S(2)}) collective-permute-start(bf16[128,256]{1,0:T(8,128)(2,1)S(1)} %get-tuple-element.18), channel_id=1, source_target_pairs={{0,8},{2,10},{4,12},{6,14},{8,0},{10,2},{12,4},{14,6},{1,9},{3,11}... | collective-permute-start | bytes 196616 | tf_op jit(solution)/shard_map/ppermute | solution.py:213
  18.1 0.5 collective-permute-start.8
  18.7 1.9 %collective-permute-start.11 = (bf16[128,256]{1,0:T(8,128)(2,1)S(1)}, bf16[128,256]{1,0:T(8,128)(2,1)S(1)}, u32[]{:S(2)}, u32[]{:S(2)}) collective-permute-start(bf16[128,256]{1,0:T(8,128)(2,1)S(1)} %get-tuple-element.20), channel_id=1, source_target_pairs={{0,14},{2,12},{4,10},{6,8},{8,6},{10,4},{12,2},{14,0},{1,15},{3,13... | collective-permute-start | bytes 196616 | tf_op jit(solution)/shard_map/ppermute | solution.py:213
  20.6 2.9 %collective-permute-start.10 = (bf16[128,256]{1,0:T(8,128)(2,1)S(1)}, bf16[128,256]{1,0:T(8,128)(2,1)S(1)}, u32[]{:S(2)}, u32[]{:S(2)}) collective-permute-start(bf16[128,256]{1,0:T(8,128)(2,1)S(1)} %get-tuple-element.20), channel_id=1, source_target_pairs={{0,12},{2,14},{4,8},{6,10},{8,4},{10,6},{12,0},{14,2},{1,13},{3,15... | collective-permute-start | bytes 196616 | tf_op jit(solution)/shard_map/ppermute | solution.py:213
  23.5 1.0 %collective-permute-start.9 = (bf16[128,256]{1,0:T(8,128)(2,1)S(1)}, bf16[128,256]{1,0:T(8,128)(2,1)S(1)}, u32[]{:S(2)}, u32[]{:S(2)}) collective-permute-start(bf16[128,256]{1,0:T(8,128)(2,1)S(1)} %add_convert_fusion.3), channel_id=1, source_target_pairs={{0,2},{2,0},{4,6},{6,4},{8,10},{10,8},{12,14},{14,12},{1,3},{3,1},... | collective-permute-start | bytes 196616 | tf_op jit(solution)/shard_map/ppermute | solution.py:213
  25.2 1.1 %collective-permute-done.11 = bf16[128,256]{1,0:T(8,128)(2,1)S(1)} collective-permute-done((bf16[128,256]{1,0:T(8,128)(2,1)S(1)}, bf16[128,256]{1,0:T(8,128)(2,1)S(1)}, u32[]{:S(2)}, u32[]{:S(2)}) %collective-permute-start.11) | collective-permute-done | bytes 65568 | tf_op jit(solution)/shard_map/ppermute | solution.py:213
  26.3 0.6 %collective-permute-done.10 = bf16[128,256]{1,0:T(8,128)(2,1)S(1)} collective-permute-done((bf16[128,256]{1,0:T(8,128)(2,1)S(1)}, bf16[128,256]{1,0:T(8,128)(2,1)S(1)}, u32[]{:S(2)}, u32[]{:S(2)}) %collective-permute-start.10) | collective-permute-done | bytes 65568 | tf_op jit(solution)/shard_map/ppermute | solution.py:213
  26.9 1.0 %collective-permute-done.9 = bf16[128,256]{1,0:T(8,128)(2,1)S(1)} collective-permute-done((bf16[128,256]{1,0:T(8,128)(2,1)S(1)}, bf16[128,256]{1,0:T(8,128)(2,1)S(1)}, u32[]{:S(2)}, u32[]{:S(2)}) %collective-permute-start.9) | collective-permute-done | bytes 65568 | tf_op jit(solution)/shard_map/ppermute | solution.py:213
  27.9 1.6 %collective-permute-start.14 = (bf16[128,256]{1,0:T(8,128)(2,1)S(1)}, bf16[128,256]{1,0:T(8,128)(2,1)S(1)}, u32[]{:S(2)}, u32[]{:S(2)}) collective-permute-start(bf16[128,256]{1,0:T(8,128)(2,1)S(1)} %add_convert_fusion.2.refs_8_), channel_id=1, source_target_pairs={{0,8},{4,12},{8,0},{12,4},{1,9},{5,13},{9,1},{13,5},{2,10},{6,14},... | collective-permute-start | bytes 196616 | tf_op jit(solution)/shard_map/ppermute | solution.py:197
  29.5 2.1 %collective-permute-start.13 = (bf16[128,256]{1,0:T(8,128)(2,1)S(1)}, bf16[128,256]{1,0:T(8,128)(2,1)S(1)}, u32[]{:S(2)}, u32[]{:S(2)}) collective-permute-start(bf16[128,256]{1,0:T(8,128)(2,1)S(1)} %add_convert_fusion.2.refs_8_), channel_id=1, source_target_pairs={{0,12},{4,8},{8,4},{12,0},{1,13},{5,9},{9,5},{13,1},{2,14},{6,10},... | collective-permute-start | bytes 196616 | tf_op jit(solution)/shard_map/ppermute | solution.py:197
  31.6 1.6 %collective-permute-done.14.refs_11_ = bf16[128,256]{1,0:T(8,128)(2,1)S(1)} collective-permute-done((bf16[128,256]{1,0:T(8,128)(2,1)S(1)}, bf16[128,256]{1,0:T(8,128)(2,1)S(1)}, u32[]{:S(2)}, u32[]{:S(2)}) %collective-permute-start.14) | collective-permute-done | bytes 65568 | tf_op jit(solution)/shard_map/ppermute | solution.py:197
  33.2 2.8 %collective-permute-done.13.refs_10_ = bf16[128,256]{1,0:T(8,128)(2,1)S(1)} collective-permute-done((bf16[128,256]{1,0:T(8,128)(2,1)S(1)}, bf16[128,256]{1,0:T(8,128)(2,1)S(1)}, u32[]{:S(2)}, u32[]{:S(2)}) %collective-permute-start.13) | collective-permute-done | bytes 65568 | tf_op jit(solution)/shard_map/ppermute | solution.py:197
  36.0 0.5 collective-permute-done.12.refs_9_
  36.5 0.7 %collective-permute-done.17.refs_14_ = bf16[128,256]{1,0:T(8,128)(2,1)S(1)} collective-permute-done((bf16[128,256]{1,0:T(8,128)(2,1)S(1)}, bf16[128,256]{1,0:T(8,128)(2,1)S(1)}, u32[]{:S(2)}, u32[]{:S(2)}) %collective-permute-start.17) | collective-permute-done | bytes 65568 | tf_op jit(solution)/shard_map/ppermute | solution.py:197
  37.2 0.5 collective-permute-done.16.refs_13_
  37.7 3.1 %shard_map.106 = (bf16[128,256]{1,0:T(8,128)(2,1)S(1)}, f32[128,256]{1,0:T(8,128)S(1)}, bf16[128,256]{1,0:T(8,128)(2,1)S(1)}, bf16[128,256]{1,0:T(8,128)(2,1)S(1)}, bf16[128,256]{1,0:T(8,128)(2,1)S(1)}) custom-call(s32[1,128]{1,0:T(1,128)S(1)} %compare_select_fusion.8.plan_in, bf16[8,128,256]{2,1,0:T(8,128)(2,1)S(1)} %get-tuple-element.14.left, ...), custom_call_target="tpu_custom_call" | custom-call | tf_op jit(solution)/shard_map/pallas_call | solution.py:178
  40.9 1.2 %collective-permute-start.19 = (bf16[128,256]{1,0:T(8,128)(2,1)S(1)}, bf16[128,256]{1,0:T(8,128)(2,1)S(1)}, u32[]{:S(2)}, u32[]{:S(2)}) collective-permute-start(bf16[128,256]{1,0:T(8,128)(2,1)S(1)} %get-tuple-element.22), channel_id=1, source_target_pairs={{0,8},{2,10},{4,12},{6,14},{8,0},{10,2},{12,4},{14,6},{1,9},{3,11}... | collective-permute-start | bytes 196616 | tf_op jit(solution)/shard_map/ppermute | solution.py:213
  42.1 1.4 %collective-permute-start.20 = (bf16[128,256]{1,0:T(8,128)(2,1)S(1)}, bf16[128,256]{1,0:T(8,128)(2,1)S(1)}, u32[]{:S(2)}, u32[]{:S(2)}) collective-permute-start(bf16[128,256]{1,0:T(8,128)(2,1)S(1)} %get-tuple-element.23), channel_id=1, source_target_pairs={{0,4},{2,6},{4,0},{6,2},{8,12},{10,14},{12,8},{14,10},{1,5},{3,7},... | collective-permute-start | bytes 196616 | tf_op jit(solution)/shard_map/ppermute | solution.py:213
  43.5 2.9 %collective-permute-start.23 = (bf16[128,256]{1,0:T(8,128)(2,1)S(1)}, bf16[128,256]{1,0:T(8,128)(2,1)S(1)}, u32[]{:S(2)}, u32[]{:S(2)}) collective-permute-start(bf16[128,256]{1,0:T(8,128)(2,1)S(1)} %get-tuple-element.24), channel_id=1, source_target_pairs={{0,14},{2,12},{4,10},{6,8},{8,6},{10,4},{12,2},{14,0},{1,15},{3,13... | collective-permute-start | bytes 196616 | tf_op jit(solution)/shard_map/ppermute | solution.py:213
  46.3 2.0 %collective-permute-start.22 = (bf16[128,256]{1,0:T(8,128)(2,1)S(1)}, bf16[128,256]{1,0:T(8,128)(2,1)S(1)}, u32[]{:S(2)}, u32[]{:S(2)}) collective-permute-start(bf16[128,256]{1,0:T(8,128)(2,1)S(1)} %get-tuple-element.24), channel_id=1, source_target_pairs={{0,12},{2,14},{4,8},{6,10},{8,4},{10,6},{12,0},{14,2},{1,13},{3,15... | collective-permute-start | bytes 196616 | tf_op jit(solution)/shard_map/ppermute | solution.py:213
  48.4 1.0 %collective-permute-start.21 = (bf16[128,256]{1,0:T(8,128)(2,1)S(1)}, bf16[128,256]{1,0:T(8,128)(2,1)S(1)}, u32[]{:S(2)}, u32[]{:S(2)}) collective-permute-start(bf16[128,256]{1,0:T(8,128)(2,1)S(1)} %add_convert_fusion.1), channel_id=1, source_target_pairs={{0,2},{2,0},{4,6},{6,4},{8,10},{10,8},{12,14},{14,12},{1,3},{3,1},... | collective-permute-start | bytes 196616 | tf_op jit(solution)/shard_map/ppermute | solution.py:213
  49.4 1.7 %collective-permute-done.23 = bf16[128,256]{1,0:T(8,128)(2,1)S(1)} collective-permute-done((bf16[128,256]{1,0:T(8,128)(2,1)S(1)}, bf16[128,256]{1,0:T(8,128)(2,1)S(1)}, u32[]{:S(2)}, u32[]{:S(2)}) %collective-permute-start.23) | collective-permute-done | bytes 65568 | tf_op jit(solution)/shard_map/ppermute | solution.py:213
  51.0 1.4 %collective-permute-done.22 = bf16[128,256]{1,0:T(8,128)(2,1)S(1)} collective-permute-done((bf16[128,256]{1,0:T(8,128)(2,1)S(1)}, bf16[128,256]{1,0:T(8,128)(2,1)S(1)}, u32[]{:S(2)}, u32[]{:S(2)}) %collective-permute-start.22) | collective-permute-done | bytes 65568 | tf_op jit(solution)/shard_map/ppermute | solution.py:213
  52.7 0.7 %fusion = bf16[1,128,256]{2,1,0:T(8,128)(2,1)} fusion(bf16[128,256]{1,0:T(8,128)(2,1)S(1)} %get-tuple-element.25, bf16[128,256]{1,0:T(8,128)(2,1)S(1)} %collective-permute-done.23, bf16[128,256]{1,0:T(8,128)(2,1)S(1)} %collective-permute-done.22, bf16[128,256]{1,0:T(8,128)(2,1)S(1)} %collective-permute-done.21, bf16[128,256]{1,0:T(8,128)(2,1)S(1)} %add_convert_fusion.1, ...), kind=kLoop, calls=%fused_computation.4 | loop fusion | flops 360448 | bytes 393220 | tf_op jit(solution)/shard_map/broadcast_in_dim | solution.py:264
  (41 shorter events, 2.2 us)
Async XLA Ops:
  0.6 9.5 %collective-permute-start.2 = (bf16[128,256]{1,0:T(8,128)(2,1)}, bf16[128,256]{1,0:T(8,128)(2,1)S(1)}, u32[]{:S(2)}, u32[]{:S(2)}) collective-permute-start(bf16[128,256]{1,0:T(8,128)(2,1)} %bitcast.30), channel_id=1, source_target_pairs={{0,8},{4,12},{8,0},{12,4},{1,9},{5,13},{9,1},{13,5},{2,10},{6,14},... | collective-permute-start | bytes 196616 | tf_op jit(solution)/shard_map/ppermute | solution.py:197
  4.7 6.4 %collective-permute-start.1 = (bf16[128,256]{1,0:T(8,128)(2,1)}, bf16[128,256]{1,0:T(8,128)(2,1)S(1)}, u32[]{:S(2)}, u32[]{:S(2)}) collective-permute-start(bf16[128,256]{1,0:T(8,128)(2,1)} %bitcast.31), channel_id=1, source_target_pairs={{0,12},{4,8},{8,4},{12,0},{1,13},{5,9},{9,5},{13,1},{2,14},{6,10},... | collective-permute-start | bytes 196616 | tf_op jit(solution)/shard_map/ppermute | solution.py:197
  6.1 5.2 %collective-permute-start = (bf16[128,256]{1,0:T(8,128)(2,1)}, bf16[128,256]{1,0:T(8,128)(2,1)S(1)}, u32[]{:S(2)}, u32[]{:S(2)}) collective-permute-start(bf16[128,256]{1,0:T(8,128)(2,1)} %bitcast.32), channel_id=1, source_target_pairs={{0,4},{4,0},{8,12},{12,8},{1,5},{5,1},{9,13},{13,9},{2,6},{6,2},{1... | collective-permute-start | bytes 196616 | tf_op jit(solution)/shard_map/ppermute | solution.py:197
  7.7 4.0 %collective-permute-start.3 = (bf16[128,256]{1,0:T(8,128)(2,1)S(1)}, bf16[128,256]{1,0:T(8,128)(2,1)S(1)}, u32[]{:S(2)}, u32[]{:S(2)}) collective-permute-start(bf16[128,256]{1,0:T(8,128)(2,1)S(1)} %get-tuple-element.16.refs_0_), channel_id=1, source_target_pairs={{0,1},{1,0},{2,3},{3,2},{4,5},{5,4},{6,7},{7,6},{8,9},{9,8},{10,11... | collective-permute-start | bytes 196616 | tf_op jit(solution)/shard_map/ppermute | solution.py:197
  8.5 0.7 %copy-start.4 = (s32[1,72]{1,0:T(1,128)S(1)}, s32[1,72]{1,0:T(1,128)}, u32[]{:S(2)}) copy-start(s32[1,72]{1,0:T(1,128)} %param.15) | copy-start | bytes 868
  8.5 0.7 %copy-start.5 = (s32[1,72]{1,0:T(1,128)S(1)}, s32[1,72]{1,0:T(1,128)}, u32[]{:S(2)}) copy-start(s32[1,72]{1,0:T(1,128)} %param.13) | copy-start | bytes 868
  9.3 0.7 %copy-start.2 = (s32[1,72]{1,0:T(1,128)S(1)}, s32[1,72]{1,0:T(1,128)}, u32[]{:S(2)}) copy-start(s32[1,72]{1,0:T(1,128)} %param.12) | copy-start | bytes 868
  9.4 0.7 %copy-start.3 = (s32[1,72]{1,0:T(1,128)S(1)}, s32[1,72]{1,0:T(1,128)}, u32[]{:S(2)}) copy-start(s32[1,72]{1,0:T(1,128)} %param.14) | copy-start | bytes 868
  10.1 1.6 %collective-permute-start.6 = (bf16[128,256]{1,0:T(8,128)(2,1)S(1)}, bf16[128,256]{1,0:T(8,128)(2,1)S(1)}, u32[]{:S(2)}, u32[]{:S(2)}) collective-permute-start(bf16[128,256]{1,0:T(8,128)(2,1)S(1)} %collective-permute-done.2.refs_3_), channel_id=1, source_target_pairs={{0,1},{1,0},{2,3},{3,2},{4,5},{5,4},{6,7},{7,6},{8,9},{9,8},{10,11... | collective-permute-start | bytes 196616 | tf_op jit(solution)/shard_map/ppermute | solution.py:197
  11.2 1.3 %collective-permute-start.5 = (bf16[128,256]{1,0:T(8,128)(2,1)S(1)}, bf16[128,256]{1,0:T(8,128)(2,1)S(1)}, u32[]{:S(2)}, u32[]{:S(2)}) collective-permute-start(bf16[128,256]{1,0:T(8,128)(2,1)S(1)} %collective-permute-done.1.refs_2_), channel_id=1, source_target_pairs={{0,1},{1,0},{2,3},{3,2},{4,5},{5,4},{6,7},{7,6},{8,9},{9,8},{10,11... | collective-permute-start | bytes 196616 | tf_op jit(solution)/shard_map/ppermute | solution.py:197
  11.3 1.3 %collective-permute-start.4 = (bf16[128,256]{1,0:T(8,128)(2,1)S(1)}, bf16[128,256]{1,0:T(8,128)(2,1)S(1)}, u32[]{:S(2)}, u32[]{:S(2)}) collective-permute-start(bf16[128,256]{1,0:T(8,128)(2,1)S(1)} %collective-permute-done.refs_1_), channel_id=1, source_target_pairs={{0,1},{1,0},{2,3},{3,2},{4,5},{5,4},{6,7},{7,6},{8,9},{9,8},{10,11... | collective-permute-start | bytes 196616 | tf_op jit(solution)/shard_map/ppermute | solution.py:197
  14.9 8.6 %collective-permute-start.7 = (bf16[128,256]{1,0:T(8,128)(2,1)S(1)}, bf16[128,256]{1,0:T(8,128)(2,1)S(1)}, u32[]{:S(2)}, u32[]{:S(2)}) collective-permute-start(bf16[128,256]{1,0:T(8,128)(2,1)S(1)} %get-tuple-element.18), channel_id=1, source_target_pairs={{0,8},{2,10},{4,12},{6,14},{8,0},{10,2},{12,4},{14,6},{1,9},{3,11}... | collective-permute-start | bytes 196616 | tf_op jit(solution)/shard_map/ppermute | solution.py:213
  18.1 5.3 %collective-permute-start.8 = (bf16[128,256]{1,0:T(8,128)(2,1)S(1)}, bf16[128,256]{1,0:T(8,128)(2,1)S(1)}, u32[]{:S(2)}, u32[]{:S(2)}) collective-permute-start(bf16[128,256]{1,0:T(8,128)(2,1)S(1)} %get-tuple-element.19), channel_id=1, source_target_pairs={{0,4},{2,6},{4,0},{6,2},{8,12},{10,14},{12,8},{14,10},{1,5},{3,7},... | collective-permute-start | bytes 196616 | tf_op jit(solution)/shard_map/ppermute | solution.py:213
  18.7 7.6 %collective-permute-start.11 = (bf16[128,256]{1,0:T(8,128)(2,1)S(1)}, bf16[128,256]{1,0:T(8,128)(2,1)S(1)}, u32[]{:S(2)}, u32[]{:S(2)}) collective-permute-start(bf16[128,256]{1,0:T(8,128)(2,1)S(1)} %get-tuple-element.20), channel_id=1, source_target_pairs={{0,14},{2,12},{4,10},{6,8},{8,6},{10,4},{12,2},{14,0},{1,15},{3,13... | collective-permute-start | bytes 196616 | tf_op jit(solution)/shard_map/ppermute | solution.py:213
  20.6 6.3 %collective-permute-start.10 = (bf16[128,256]{1,0:T(8,128)(2,1)S(1)}, bf16[128,256]{1,0:T(8,128)(2,1)S(1)}, u32[]{:S(2)}, u32[]{:S(2)}) collective-permute-start(bf16[128,256]{1,0:T(8,128)(2,1)S(1)} %get-tuple-element.20), channel_id=1, source_target_pairs={{0,12},{2,14},{4,8},{6,10},{8,4},{10,6},{12,0},{14,2},{1,13},{3,15... | collective-permute-start | bytes 196616 | tf_op jit(solution)/shard_map/ppermute | solution.py:213
  23.5 4.4 %copy-start.1 = (bf16[1,128,256]{2,1,0:T(8,128)(2,1)S(1)}, bf16[1,128,256]{2,1,0:T(8,128)(2,1)}, u32[]{:S(2)}) copy-start(bf16[1,128,256]{2,1,0:T(8,128)(2,1)} %param.9) | copy-start | bytes 196612
  23.5 4.3 %collective-permute-start.9 = (bf16[128,256]{1,0:T(8,128)(2,1)S(1)}, bf16[128,256]{1,0:T(8,128)(2,1)S(1)}, u32[]{:S(2)}, u32[]{:S(2)}) collective-permute-start(bf16[128,256]{1,0:T(8,128)(2,1)S(1)} %add_convert_fusion.3), channel_id=1, source_target_pairs={{0,2},{2,0},{4,6},{6,4},{8,10},{10,8},{12,14},{14,12},{1,3},{3,1},... | collective-permute-start | bytes 196616 | tf_op jit(solution)/shard_map/ppermute | solution.py:213
  27.9 12.9 %copy-start = (bf16[128,256]{1,0:T(8,128)(2,1)}, bf16[128,256]{1,0:T(8,128)(2,1)S(1)}, u32[]{:S(2)}) copy-start(bf16[128,256]{1,0:T(8,128)(2,1)S(1)} %add_convert_fusion.2.refs_8_) | copy-start | bytes 196612
  27.9 5.3 %collective-permute-start.14 = (bf16[128,256]{1,0:T(8,128)(2,1)S(1)}, bf16[128,256]{1,0:T(8,128)(2,1)S(1)}, u32[]{:S(2)}, u32[]{:S(2)}) collective-permute-start(bf16[128,256]{1,0:T(8,128)(2,1)S(1)} %add_convert_fusion.2.refs_8_), channel_id=1, source_target_pairs={{0,8},{4,12},{8,0},{12,4},{1,9},{5,13},{9,1},{13,5},{2,10},{6,14},... | collective-permute-start | bytes 196616 | tf_op jit(solution)/shard_map/ppermute | solution.py:197
  29.5 6.4 %collective-permute-start.13 = (bf16[128,256]{1,0:T(8,128)(2,1)S(1)}, bf16[128,256]{1,0:T(8,128)(2,1)S(1)}, u32[]{:S(2)}, u32[]{:S(2)}) collective-permute-start(bf16[128,256]{1,0:T(8,128)(2,1)S(1)} %add_convert_fusion.2.refs_8_), channel_id=1, source_target_pairs={{0,12},{4,8},{8,4},{12,0},{1,13},{5,9},{9,5},{13,1},{2,14},{6,10},... | collective-permute-start | bytes 196616 | tf_op jit(solution)/shard_map/ppermute | solution.py:197
  31.6 4.9 %collective-permute-start.12 = (bf16[128,256]{1,0:T(8,128)(2,1)S(1)}, bf16[128,256]{1,0:T(8,128)(2,1)S(1)}, u32[]{:S(2)}, u32[]{:S(2)}) collective-permute-start(bf16[128,256]{1,0:T(8,128)(2,1)S(1)} %add_convert_fusion.2.refs_8_), channel_id=1, source_target_pairs={{0,4},{4,0},{8,12},{12,8},{1,5},{5,1},{9,13},{13,9},{2,6},{6,2},{1... | collective-permute-start | bytes 196616 | tf_op jit(solution)/shard_map/ppermute | solution.py:197
  31.6 4.9 %collective-permute-start.15 = (bf16[128,256]{1,0:T(8,128)(2,1)S(1)}, bf16[128,256]{1,0:T(8,128)(2,1)S(1)}, u32[]{:S(2)}, u32[]{:S(2)}) collective-permute-start(bf16[128,256]{1,0:T(8,128)(2,1)S(1)} %add_convert_fusion.2.refs_8_), channel_id=1, source_target_pairs={{0,1},{1,0},{2,3},{3,2},{4,5},{5,4},{6,7},{7,6},{8,9},{9,8},{10,11... | collective-permute-start | bytes 196616 | tf_op jit(solution)/shard_map/ppermute | solution.py:197
  33.2 3.3 %collective-permute-start.18 = (bf16[128,256]{1,0:T(8,128)(2,1)S(1)}, bf16[128,256]{1,0:T(8,128)(2,1)S(1)}, u32[]{:S(2)}, u32[]{:S(2)}) collective-permute-start(bf16[128,256]{1,0:T(8,128)(2,1)S(1)} %collective-permute-done.14.refs_11_), channel_id=1, source_target_pairs={{0,1},{1,0},{2,3},{3,2},{4,5},{5,4},{6,7},{7,6},{8,9},{9,8},{10,11... | collective-permute-start | bytes 196616 | tf_op jit(solution)/shard_map/ppermute | solution.py:197
  36.0 1.3 %collective-permute-start.17 = (bf16[128,256]{1,0:T(8,128)(2,1)S(1)}, bf16[128,256]{1,0:T(8,128)(2,1)S(1)}, u32[]{:S(2)}, u32[]{:S(2)}) collective-permute-start(bf16[128,256]{1,0:T(8,128)(2,1)S(1)} %collective-permute-done.13.refs_10_), channel_id=1, source_target_pairs={{0,1},{1,0},{2,3},{3,2},{4,5},{5,4},{6,7},{7,6},{8,9},{9,8},{10,11... | collective-permute-start | bytes 196616 | tf_op jit(solution)/shard_map/ppermute | solution.py:197
  36.5 1.3 %collective-permute-start.16 = (bf16[128,256]{1,0:T(8,128)(2,1)S(1)}, bf16[128,256]{1,0:T(8,128)(2,1)S(1)}, u32[]{:S(2)}, u32[]{:S(2)}) collective-permute-start(bf16[128,256]{1,0:T(8,128)(2,1)S(1)} %collective-permute-done.12.refs_9_), channel_id=1, source_target_pairs={{0,1},{1,0},{2,3},{3,2},{4,5},{5,4},{6,7},{7,6},{8,9},{9,8},{10,11... | collective-permute-start | bytes 196616 | tf_op jit(solution)/shard_map/ppermute | solution.py:197
  40.9 7.5 %collective-permute-start.19 = (bf16[128,256]{1,0:T(8,128)(2,1)S(1)}, bf16[128,256]{1,0:T(8,128)(2,1)S(1)}, u32[]{:S(2)}, u32[]{:S(2)}) collective-permute-start(bf16[128,256]{1,0:T(8,128)(2,1)S(1)} %get-tuple-element.22), channel_id=1, source_target_pairs={{0,8},{2,10},{4,12},{6,14},{8,0},{10,2},{12,4},{14,6},{1,9},{3,11}... | collective-permute-start | bytes 196616 | tf_op jit(solution)/shard_map/ppermute | solution.py:213
  42.1 6.3 %collective-permute-start.20 = (bf16[128,256]{1,0:T(8,128)(2,1)S(1)}, bf16[128,256]{1,0:T(8,128)(2,1)S(1)}, u32[]{:S(2)}, u32[]{:S(2)}) collective-permute-start(bf16[128,256]{1,0:T(8,128)(2,1)S(1)} %get-tuple-element.23), channel_id=1, source_target_pairs={{0,4},{2,6},{4,0},{6,2},{8,12},{10,14},{12,8},{14,10},{1,5},{3,7},... | collective-permute-start | bytes 196616 | tf_op jit(solution)/shard_map/ppermute | solution.py:213
  43.5 7.6 %collective-permute-start.23 = (bf16[128,256]{1,0:T(8,128)(2,1)S(1)}, bf16[128,256]{1,0:T(8,128)(2,1)S(1)}, u32[]{:S(2)}, u32[]{:S(2)}) collective-permute-start(bf16[128,256]{1,0:T(8,128)(2,1)S(1)} %get-tuple-element.24), channel_id=1, source_target_pairs={{0,14},{2,12},{4,10},{6,8},{8,6},{10,4},{12,2},{14,0},{1,15},{3,13... | collective-permute-start | bytes 196616 | tf_op jit(solution)/shard_map/ppermute | solution.py:213
  46.3 6.1 %collective-permute-start.22 = (bf16[128,256]{1,0:T(8,128)(2,1)S(1)}, bf16[128,256]{1,0:T(8,128)(2,1)S(1)}, u32[]{:S(2)}, u32[]{:S(2)}) collective-permute-start(bf16[128,256]{1,0:T(8,128)(2,1)S(1)} %get-tuple-element.24), channel_id=1, source_target_pairs={{0,12},{2,14},{4,8},{6,10},{8,4},{10,6},{12,0},{14,2},{1,13},{3,15... | collective-permute-start | bytes 196616 | tf_op jit(solution)/shard_map/ppermute | solution.py:213
  48.4 4.3 %collective-permute-start.21 = (bf16[128,256]{1,0:T(8,128)(2,1)S(1)}, bf16[128,256]{1,0:T(8,128)(2,1)S(1)}, u32[]{:S(2)}, u32[]{:S(2)}) collective-permute-start(bf16[128,256]{1,0:T(8,128)(2,1)S(1)} %add_convert_fusion.1), channel_id=1, source_target_pairs={{0,2},{2,0},{4,6},{6,4},{8,10},{10,8},{12,14},{14,12},{1,3},{3,1},... | collective-permute-start | bytes 196616 | tf_op jit(solution)/shard_map/ppermute | solution.py:213

commit v6 on v5

--- a/solution.py
+++ b/solution.py
@@ -10,7 +10,7 @@
 gather_four = [0, 1, 3, 2]
 target_four = [0, 2, 1, 3]
 direct_distances = (3,)
-unroll_slots = 4
+unroll_slots = 3
 wide_sectors = 4
 step_lefts = 2
 whole_vmem = pl.BlockSpec(memory_space=pltpu.VMEM)
@@ -125,7 +125,8 @@
 
 
 def first_kernel(sectors, plan_in, left, right, *refs):
-    psis, out_refs = refs[: 2 * sectors], refs[2 * sectors : -5]
+    psis = refs[: 2 * sectors]
+    norm_ref, *out_refs = refs[2 * sectors : -5]
     plan_ref, arrived, vector, halves, sums = refs[-5:]
     core = lax.axis_index("pair")
     plan_copy = pltpu.make_async_copy(plan_in, plan_ref, arrived)
@@ -133,34 +134,34 @@
     sums[...] = jnp.zeros_like(sums)
     for j in range(sectors):
         join(core, vector, j, psis[j][...], psis[sectors + j][...])
+    norm = sum(wide_of(p) * wide_of(p) for p in psis)
+    norm_ref[...] = jnp.sum(norm.reshape(-1, 8, norm.shape[1]), axis=0)
     half_products(sectors, left, vector, halves)
     plan_copy.wait()
     sum_halves(plan_ref, halves, sums)
     all_targets(sectors, right, sums, out_refs)
 
 
-def second_kernel(sectors, plan_in, left, right, *refs):
+def second_kernel(sectors, plan_in, left, right, norm_ref, *refs):
     pieces = 2 * sectors
     psis, sigmas = refs[:pieces], refs[pieces : 2 * pieces]
     own_ref, *out_refs = refs[2 * pieces : -5]
     plan_ref, arrived, vector, halves, sums = refs[-5:]
+    resids = halves
     core = lax.axis_index("pair")
     plan_copy = pltpu.make_async_copy(plan_in, plan_ref, arrived)
     plan_copy.start()
     sums[...] = jnp.zeros_like(sums)
-    norm = sum(wide_of(p) * wide_of(p) for p in psis)
     correlation = sum(wide_of(p) * wide_of(s) for p, s in zip(psis, sigmas))
-    theta = jnp.sum(correlation) / jnp.sum(norm)
-    square = jnp.zeros_like(norm)
-    for p, s in zip(psis, sigmas):
+    theta = jnp.sum(correlation) / jnp.sum(norm_ref[...])
+    square = 0
+    for i, (p, s) in enumerate(zip(psis, sigmas)):
         resid = wide_of(s) - theta * wide_of(p)
+        resids[i] = resid
         square = square + resid * resid
-    entries = pieces * norm.shape[0] * norm.shape[1]
-    scale = lax.rsqrt(jnp.sum(square) / entries + 1e-06)
+    scale = lax.rsqrt(jnp.sum(square) / (pieces * square.shape[0] * square.shape[1]) + 1e-06)
     for j in range(sectors):
-        mine, other = (
-            ((wide_of(sigmas[i]) - theta * wide_of(psis[i])) * scale).astype(jnp.bfloat16) for i in (j, sectors + j)
-        )
+        mine, other = ((resids[i] * scale).astype(jnp.bfloat16) for i in (j, sectors + j))
         if j == 0:
             own_ref[...] = mine
         join(core, vector, j, mine, other)
@@ -253,11 +254,13 @@
     plan = make_plan(me, *indices, block_count[0], sectors, lefts, rights)
     energy = sector_energy[0]
     call = functools.partial(call_product, sectors=sectors, lefts=lefts, rights=rights)
-    parts = call(first_kernel, inside=[plan, left, right, *psis], kept=[])
+    norm, *parts = call(
+        first_kernel, inside=[plan, left, right, *psis], kept=[pltpu.VMEM((8, own.shape[1]), jnp.float32)]
+    )
     sigma_first = (owner_sum(parts) + energy * own.astype(jnp.float32)).astype(jnp.bfloat16)
     correction, *parts = call(
         second_kernel,
-        inside=[plan, left, right, *psis, *gather(sigma_first, sigma_first)],
+        inside=[plan, left, right, norm, *psis, *gather(sigma_first, sigma_first)],
         kept=[pltpu.VMEM(own.shape, own.dtype)],
     )
     sigma_second = (owner_sum(parts) + energy * correction.astype(jnp.float32)).astype(jnp.bfloat16)

time: 53.9 us -> 54.4 us (level); the launches traced: 53.4 us -> 54.5 us
  starting transfers between devices: 28.6 us -> 31.1 us
  waiting for transfers between devices: 13.5 us -> 11.4 us
  Pallas kernels: 6.85 us -> 7.44 us
    ppermute x10, starting transfers between devices: 18.1 us -> 20.5 us  [send(): return lax.ppermute(value, ('term', 'sub'), route)]
    ppermute x10, waiting for transfers between devices: 5.95 us -> 4.04 us  [send(): return lax.ppermute(value, ('term', 'sub'), route)]
    pallas_call x2, Pallas kernels: 5.43 us -> 6.02 us  [call_product(): pl.pallas_call(functools.partial(kernel, sectors), out_shape=outs, in_spe...]
  transfers between devices with their start and end apart: 24 -> 24, of which waited for: 15 -> 14; matrix products, arithmetic and copies ran while one was open for 1% -> 1% of each run, Pallas kernels for 3% -> 3%
where the time goes in v6:
time: 54.4 us; the launch traced here: 54.5 us
  starting transfers between devices  31.1 us (57%)
  waiting for transfers between devices  11.4 us (21%)
  Pallas kernels  7.44 us (14%)
  between operations  2.07 us (4%)
  local copies, waits for them, and re-layouts  1.33 us (2%)
  other arithmetic  1.09 us (2%)
    ppermute x10, starting transfers between devices, send(): return lax.ppermute(value, ('term', 'sub'), route)  20.5 us
    ppermute x14, starting transfers between devices, swap(): lax.ppermute(value, axis, [(i, i ^ bit) for i in range(lax.axis_size(axis...  10.6 us
    ppermute x14, waiting for transfers between devices, swap(): lax.ppermute(value, axis, [(i, i ^ bit) for i in range(lax.axis_size(axis...  7.37 us
    pallas_call x2, Pallas kernels, call_product(): pl.pallas_call(functools.partial(kernel, sectors), out_shape=outs, in_spe...  6.02 us
    ppermute x10, waiting for transfers between devices, send(): return lax.ppermute(value, ('term', 'sub'), route)  4.04 us
    pallas_call x1, Pallas kernels, fetch(): pl.pallas_call(fetch_kernel, out_shape=[pltpu.VMEM(x.shape, x.dtype) for...  1.42 us
    unnamed x12, local copies, waits for them, and re-layouts  1.33 us
  transfers between devices with their start and end apart: 24, of which 14 were waited for; matrix products, arithmetic and copies ran while one was open for 1% of the time, Pallas kernels for 3%

profile of v6, /device:TPU:0, one launch (start us, length us, event | category | flops | bytes accessed | tf_op | source)
XLA Modules:
  0.0 54.5 jit_solution(10934570934762171540)
XLA Ops:
  0.6 4.1 %collective-permute-start.2 = (bf16[128,256]{1,0:T(8,128)(2,1)}, bf16[128,256]{1,0:T(8,128)(2,1)S(1)}, u32[]{:S(2)}, u32[]{:S(2)}) collective-permute-start(bf16[128,256]{1,0:T(8,128)(2,1)} %bitcast.30), channel_id=1, source_target_pairs={{0,8},{4,12},{8,0},{12,4},{1,9},{5,13},{9,1},{13,5},{2,10},{6,14},... | collective-permute-start | bytes 196616 | tf_op jit(solution)/shard_map/ppermute | solution.py:198
  4.7 1.3 %collective-permute-start.1 = (bf16[128,256]{1,0:T(8,128)(2,1)}, bf16[128,256]{1,0:T(8,128)(2,1)S(1)}, u32[]{:S(2)}, u32[]{:S(2)}) collective-permute-start(bf16[128,256]{1,0:T(8,128)(2,1)} %bitcast.31), channel_id=1, source_target_pairs={{0,12},{4,8},{8,4},{12,0},{1,13},{5,9},{9,5},{13,1},{2,14},{6,10},... | collective-permute-start | bytes 196616 | tf_op jit(solution)/shard_map/ppermute | solution.py:198
  6.3 1.4 %shard_map.104 = (bf16[8,128,256]{2,1,0:T(8,128)(2,1)S(1)}, bf16[8,256,256]{2,1,0:T(8,128)(2,1)S(1)}, bf16[128,256]{1,0:T(8,128)(2,1)S(1)}) custom-call(bf16[8,128,256]{2,1,0:T(8,128)(2,1)} %bitcast.29, bf16[8,256,256]{2,1,0:T(8,128)(2,1)} %bitcast.28, bf16[128,256]{1,0:T(8,128)(2,1)} %bitcast.33), custom_call_target="tpu_custom_call" | custom-call | tf_op jit(solution)/shard_map/pallas_call | solution.py:118
  8.5 0.6 %copy-done.4 = s32[1,72]{1,0:T(1,128)S(1)} copy-done((s32[1,72]{1,0:T(1,128)S(1)}, s32[1,72]{1,0:T(1,128)}, u32[]{:S(2)}) %copy-start.4) | copy-done | bytes 312
  9.4 0.6 %copy-done.2 = s32[1,72]{1,0:T(1,128)S(1)} copy-done((s32[1,72]{1,0:T(1,128)S(1)}, s32[1,72]{1,0:T(1,128)}, u32[]{:S(2)}) %copy-start.2) | copy-done | bytes 312
  10.1 0.6 %collective-permute-start.6 = (bf16[128,256]{1,0:T(8,128)(2,1)S(1)}, bf16[128,256]{1,0:T(8,128)(2,1)S(1)}, u32[]{:S(2)}, u32[]{:S(2)}) collective-permute-start(bf16[128,256]{1,0:T(8,128)(2,1)S(1)} %collective-permute-done.2.refs_3_), channel_id=1, source_target_pairs={{0,1},{1,0},{2,3},{3,2},{4,5},{5,4},{6,7},{7,6},{8,9},{9,8},{10,11... | collective-permute-start | bytes 196616 | tf_op jit(solution)/shard_map/ppermute | solution.py:198
  10.7 0.5 collective-permute-done.1.refs_2_
  11.3 0.4 collective-permute-start.4
  11.7 0.7 %collective-permute-done.5.refs_6_ = bf16[128,256]{1,0:T(8,128)(2,1)S(1)} collective-permute-done((bf16[128,256]{1,0:T(8,128)(2,1)S(1)}, bf16[128,256]{1,0:T(8,128)(2,1)S(1)}, u32[]{:S(2)}, u32[]{:S(2)}) %collective-permute-start.5) | collective-permute-done | bytes 65568 | tf_op jit(solution)/shard_map/ppermute | solution.py:198
  12.6 2.7 %shard_map.105 = (f32[8,256]{1,0:T(8,128)S(1)}, f32[128,256]{1,0:T(8,128)S(1)}, bf16[128,256]{1,0:T(8,128)(2,1)S(1)}, bf16[128,256]{1,0:T(8,128)(2,1)S(1)}, bf16[128,256]{1,0:T(8,128)(2,1)S(1)}) custom-call(s32[1,128]{1,0:T(1,128)S(1)} %compare_select_fusion.8.plan_in, bf16[8,128,256]{2,1,0:T(8,128)(2,1)S(1)} %get-tuple-element.15.left, ...), custom_call_target="tpu_custom_call" | custom-call | tf_op jit(solution)/shard_map/pallas_call | solution.py:179
  15.3 2.9 %collective-permute-start.7 = (bf16[128,256]{1,0:T(8,128)(2,1)S(1)}, bf16[128,256]{1,0:T(8,128)(2,1)S(1)}, u32[]{:S(2)}, u32[]{:S(2)}) collective-permute-start(bf16[128,256]{1,0:T(8,128)(2,1)S(1)} %get-tuple-element.19), channel_id=1, source_target_pairs={{0,8},{2,10},{4,12},{6,14},{8,0},{10,2},{12,4},{14,6},{1,9},{3,11}... | collective-permute-start | bytes 196616 | tf_op jit(solution)/shard_map/ppermute | solution.py:214
  18.5 2.1 %collective-permute-start.11 = (bf16[128,256]{1,0:T(8,128)(2,1)S(1)}, bf16[128,256]{1,0:T(8,128)(2,1)S(1)}, u32[]{:S(2)}, u32[]{:S(2)}) collective-permute-start(bf16[128,256]{1,0:T(8,128)(2,1)S(1)} %get-tuple-element.21), channel_id=1, source_target_pairs={{0,14},{2,12},{4,10},{6,8},{8,6},{10,4},{12,2},{14,0},{1,15},{3,13... | collective-permute-start | bytes 196616 | tf_op jit(solution)/shard_map/ppermute | solution.py:214
  20.7 2.8 %collective-permute-start.10 = (bf16[128,256]{1,0:T(8,128)(2,1)S(1)}, bf16[128,256]{1,0:T(8,128)(2,1)S(1)}, u32[]{:S(2)}, u32[]{:S(2)}) collective-permute-start(bf16[128,256]{1,0:T(8,128)(2,1)S(1)} %get-tuple-element.21), channel_id=1, source_target_pairs={{0,12},{2,14},{4,8},{6,10},{8,4},{10,6},{12,0},{14,2},{1,13},{3,15... | collective-permute-start | bytes 196616 | tf_op jit(solution)/shard_map/ppermute | solution.py:214
  23.5 1.9 %collective-permute-start.9 = (bf16[128,256]{1,0:T(8,128)(2,1)S(1)}, bf16[128,256]{1,0:T(8,128)(2,1)S(1)}, u32[]{:S(2)}, u32[]{:S(2)}) collective-permute-start(bf16[128,256]{1,0:T(8,128)(2,1)S(1)} %add_convert_fusion.3), channel_id=1, source_target_pairs={{0,2},{2,0},{4,6},{6,4},{8,10},{10,8},{12,14},{14,12},{1,3},{3,1},... | collective-permute-start | bytes 196616 | tf_op jit(solution)/shard_map/ppermute | solution.py:214
  26.2 0.8 %collective-permute-done.10 = bf16[128,256]{1,0:T(8,128)(2,1)S(1)} collective-permute-done((bf16[128,256]{1,0:T(8,128)(2,1)S(1)}, bf16[128,256]{1,0:T(8,128)(2,1)S(1)}, u32[]{:S(2)}, u32[]{:S(2)}) %collective-permute-start.10) | collective-permute-done | bytes 65568 | tf_op jit(solution)/shard_map/ppermute | solution.py:214
  27.0 0.9 %collective-permute-done.9 = bf16[128,256]{1,0:T(8,128)(2,1)S(1)} collective-permute-done((bf16[128,256]{1,0:T(8,128)(2,1)S(1)}, bf16[128,256]{1,0:T(8,128)(2,1)S(1)}, u32[]{:S(2)}, u32[]{:S(2)}) %collective-permute-start.9) | collective-permute-done | bytes 65568 | tf_op jit(solution)/shard_map/ppermute | solution.py:214
  27.9 1.5 %collective-permute-start.14 = (bf16[128,256]{1,0:T(8,128)(2,1)S(1)}, bf16[128,256]{1,0:T(8,128)(2,1)S(1)}, u32[]{:S(2)}, u32[]{:S(2)}) collective-permute-start(bf16[128,256]{1,0:T(8,128)(2,1)S(1)} %add_convert_fusion.2.refs_8_), channel_id=1, source_target_pairs={{0,8},{4,12},{8,0},{12,4},{1,9},{5,13},{9,1},{13,5},{2,10},{6,14},... | collective-permute-start | bytes 196616 | tf_op jit(solution)/shard_map/ppermute | solution.py:198
  29.4 2.2 %collective-permute-start.13 = (bf16[128,256]{1,0:T(8,128)(2,1)S(1)}, bf16[128,256]{1,0:T(8,128)(2,1)S(1)}, u32[]{:S(2)}, u32[]{:S(2)}) collective-permute-start(bf16[128,256]{1,0:T(8,128)(2,1)S(1)} %add_convert_fusion.2.refs_8_), channel_id=1, source_target_pairs={{0,12},{4,8},{8,4},{12,0},{1,13},{5,9},{9,5},{13,1},{2,14},{6,10},... | collective-permute-start | bytes 196616 | tf_op jit(solution)/shard_map/ppermute | solution.py:198
  31.7 1.5 %collective-permute-done.14.refs_11_ = bf16[128,256]{1,0:T(8,128)(2,1)S(1)} collective-permute-done((bf16[128,256]{1,0:T(8,128)(2,1)S(1)}, bf16[128,256]{1,0:T(8,128)(2,1)S(1)}, u32[]{:S(2)}, u32[]{:S(2)}) %collective-permute-start.14) | collective-permute-done | bytes 65568 | tf_op jit(solution)/shard_map/ppermute | solution.py:198
  33.2 2.9 %collective-permute-done.13.refs_10_ = bf16[128,256]{1,0:T(8,128)(2,1)S(1)} collective-permute-done((bf16[128,256]{1,0:T(8,128)(2,1)S(1)}, bf16[128,256]{1,0:T(8,128)(2,1)S(1)}, u32[]{:S(2)}, u32[]{:S(2)}) %collective-permute-start.13) | collective-permute-done | bytes 65568 | tf_op jit(solution)/shard_map/ppermute | solution.py:198
  36.0 0.4 collective-permute-done.12.refs_9_
  36.6 0.7 %collective-permute-done.17.refs_14_ = bf16[128,256]{1,0:T(8,128)(2,1)S(1)} collective-permute-done((bf16[128,256]{1,0:T(8,128)(2,1)S(1)}, bf16[128,256]{1,0:T(8,128)(2,1)S(1)}, u32[]{:S(2)}, u32[]{:S(2)}) %collective-permute-start.17) | collective-permute-done | bytes 65568 | tf_op jit(solution)/shard_map/ppermute | solution.py:198
  37.3 0.4 collective-permute-done.16.refs_13_
  37.7 3.4 %shard_map.106 = (bf16[128,256]{1,0:T(8,128)(2,1)S(1)}, f32[128,256]{1,0:T(8,128)S(1)}, bf16[128,256]{1,0:T(8,128)(2,1)S(1)}, bf16[128,256]{1,0:T(8,128)(2,1)S(1)}, bf16[128,256]{1,0:T(8,128)(2,1)S(1)}) custom-call(s32[1,128]{1,0:T(1,128)S(1)} %compare_select_fusion.8.plan_in, bf16[8,128,256]{2,1,0:T(8,128)(2,1)S(1)} %get-tuple-element.15.left, ...), custom_call_target="tpu_custom_call" | custom-call | tf_op jit(solution)/shard_map/pallas_call | solution.py:179
  41.1 1.0 %collective-permute-start.19 = (bf16[128,256]{1,0:T(8,128)(2,1)S(1)}, bf16[128,256]{1,0:T(8,128)(2,1)S(1)}, u32[]{:S(2)}, u32[]{:S(2)}) collective-permute-start(bf16[128,256]{1,0:T(8,128)(2,1)S(1)} %get-tuple-element.24), channel_id=1, source_target_pairs={{0,8},{2,10},{4,12},{6,14},{8,0},{10,2},{12,4},{14,6},{1,9},{3,11}... | collective-permute-start | bytes 196616 | tf_op jit(solution)/shard_map/ppermute | solution.py:214
  42.1 1.1 %collective-permute-start.20 = (bf16[128,256]{1,0:T(8,128)(2,1)S(1)}, bf16[128,256]{1,0:T(8,128)(2,1)S(1)}, u32[]{:S(2)}, u32[]{:S(2)}) collective-permute-start(bf16[128,256]{1,0:T(8,128)(2,1)S(1)} %get-tuple-element.25), channel_id=1, source_target_pairs={{0,4},{2,6},{4,0},{6,2},{8,12},{10,14},{12,8},{14,10},{1,5},{3,7},... | collective-permute-start | bytes 196616 | tf_op jit(solution)/shard_map/ppermute | solution.py:214
  43.1 3.1 %collective-permute-start.23 = (bf16[128,256]{1,0:T(8,128)(2,1)S(1)}, bf16[128,256]{1,0:T(8,128)(2,1)S(1)}, u32[]{:S(2)}, u32[]{:S(2)}) collective-permute-start(bf16[128,256]{1,0:T(8,128)(2,1)S(1)} %get-tuple-element.26), channel_id=1, source_target_pairs={{0,14},{2,12},{4,10},{6,8},{8,6},{10,4},{12,2},{14,0},{1,15},{3,13... | collective-permute-start | bytes 196616 | tf_op jit(solution)/shard_map/ppermute | solution.py:214
  46.2 2.0 %collective-permute-start.22 = (bf16[128,256]{1,0:T(8,128)(2,1)S(1)}, bf16[128,256]{1,0:T(8,128)(2,1)S(1)}, u32[]{:S(2)}, u32[]{:S(2)}) collective-permute-start(bf16[128,256]{1,0:T(8,128)(2,1)S(1)} %get-tuple-element.26), channel_id=1, source_target_pairs={{0,12},{2,14},{4,8},{6,10},{8,4},{10,6},{12,0},{14,2},{1,13},{3,15... | collective-permute-start | bytes 196616 | tf_op jit(solution)/shard_map/ppermute | solution.py:214
  48.2 3.3 %collective-permute-start.21 = (bf16[128,256]{1,0:T(8,128)(2,1)S(1)}, bf16[128,256]{1,0:T(8,128)(2,1)S(1)}, u32[]{:S(2)}, u32[]{:S(2)}) collective-permute-start(bf16[128,256]{1,0:T(8,128)(2,1)S(1)} %add_convert_fusion.1), channel_id=1, source_target_pairs={{0,2},{2,0},{4,6},{6,4},{8,10},{10,8},{12,14},{14,12},{1,3},{3,1},... | collective-permute-start | bytes 196616 | tf_op jit(solution)/shard_map/ppermute | solution.py:214
  51.5 0.8 %collective-permute-done.22 = bf16[128,256]{1,0:T(8,128)(2,1)S(1)} collective-permute-done((bf16[128,256]{1,0:T(8,128)(2,1)S(1)}, bf16[128,256]{1,0:T(8,128)(2,1)S(1)}, u32[]{:S(2)}, u32[]{:S(2)}) %collective-permute-start.22) | collective-permute-done | bytes 65568 | tf_op jit(solution)/shard_map/ppermute | solution.py:214
  52.3 1.5 %collective-permute-done.21 = bf16[128,256]{1,0:T(8,128)(2,1)S(1)} collective-permute-done((bf16[128,256]{1,0:T(8,128)(2,1)S(1)}, bf16[128,256]{1,0:T(8,128)(2,1)S(1)}, u32[]{:S(2)}, u32[]{:S(2)}) %collective-permute-start.21) | collective-permute-done | bytes 65568 | tf_op jit(solution)/shard_map/ppermute | solution.py:214
  53.8 0.7 %fusion = bf16[1,128,256]{2,1,0:T(8,128)(2,1)} fusion(bf16[128,256]{1,0:T(8,128)(2,1)S(1)} %get-tuple-element.27, bf16[128,256]{1,0:T(8,128)(2,1)S(1)} %collective-permute-done.23, bf16[128,256]{1,0:T(8,128)(2,1)S(1)} %collective-permute-done.22, bf16[128,256]{1,0:T(8,128)(2,1)S(1)} %collective-permute-done.21, bf16[128,256]{1,0:T(8,128)(2,1)S(1)} %add_convert_fusion.1, ...), kind=kLoop, calls=%fused_computation.4 | loop fusion | flops 360448 | bytes 393220 | tf_op jit(solution)/shard_map/broadcast_in_dim | solution.py:267
  (41 shorter events, 1.7 us)
Async XLA Ops:
  0.6 9.5 %collective-permute-start.2 = (bf16[128,256]{1,0:T(8,128)(2,1)}, bf16[128,256]{1,0:T(8,128)(2,1)S(1)}, u32[]{:S(2)}, u32[]{:S(2)}) collective-permute-start(bf16[128,256]{1,0:T(8,128)(2,1)} %bitcast.30), channel_id=1, source_target_pairs={{0,8},{4,12},{8,0},{12,4},{1,9},{5,13},{9,1},{13,5},{2,10},{6,14},... | collective-permute-start | bytes 196616 | tf_op jit(solution)/shard_map/ppermute | solution.py:198
  4.7 6.4 %collective-permute-start.1 = (bf16[128,256]{1,0:T(8,128)(2,1)}, bf16[128,256]{1,0:T(8,128)(2,1)S(1)}, u32[]{:S(2)}, u32[]{:S(2)}) collective-permute-start(bf16[128,256]{1,0:T(8,128)(2,1)} %bitcast.31), channel_id=1, source_target_pairs={{0,12},{4,8},{8,4},{12,0},{1,13},{5,9},{9,5},{13,1},{2,14},{6,10},... | collective-permute-start | bytes 196616 | tf_op jit(solution)/shard_map/ppermute | solution.py:198
  6.1 5.2 %collective-permute-start = (bf16[128,256]{1,0:T(8,128)(2,1)}, bf16[128,256]{1,0:T(8,128)(2,1)S(1)}, u32[]{:S(2)}, u32[]{:S(2)}) collective-permute-start(bf16[128,256]{1,0:T(8,128)(2,1)} %bitcast.32), channel_id=1, source_target_pairs={{0,4},{4,0},{8,12},{12,8},{1,5},{5,1},{9,13},{13,9},{2,6},{6,2},{1... | collective-permute-start | bytes 196616 | tf_op jit(solution)/shard_map/ppermute | solution.py:198
  7.7 4.0 %collective-permute-start.3 = (bf16[128,256]{1,0:T(8,128)(2,1)S(1)}, bf16[128,256]{1,0:T(8,128)(2,1)S(1)}, u32[]{:S(2)}, u32[]{:S(2)}) collective-permute-start(bf16[128,256]{1,0:T(8,128)(2,1)S(1)} %get-tuple-element.17.refs_0_), channel_id=1, source_target_pairs={{0,1},{1,0},{2,3},{3,2},{4,5},{5,4},{6,7},{7,6},{8,9},{9,8},{10,11... | collective-permute-start | bytes 196616 | tf_op jit(solution)/shard_map/ppermute | solution.py:198
  8.5 0.7 %copy-start.4 = (s32[1,72]{1,0:T(1,128)S(1)}, s32[1,72]{1,0:T(1,128)}, u32[]{:S(2)}) copy-start(s32[1,72]{1,0:T(1,128)} %param.15) | copy-start | bytes 868
  8.5 0.7 %copy-start.5 = (s32[1,72]{1,0:T(1,128)S(1)}, s32[1,72]{1,0:T(1,128)}, u32[]{:S(2)}) copy-start(s32[1,72]{1,0:T(1,128)} %param.13) | copy-start | bytes 868
  9.3 0.7 %copy-start.2 = (s32[1,72]{1,0:T(1,128)S(1)}, s32[1,72]{1,0:T(1,128)}, u32[]{:S(2)}) copy-start(s32[1,72]{1,0:T(1,128)} %param.12) | copy-start | bytes 868
  9.4 0.7 %copy-start.3 = (s32[1,72]{1,0:T(1,128)S(1)}, s32[1,72]{1,0:T(1,128)}, u32[]{:S(2)}) copy-start(s32[1,72]{1,0:T(1,128)} %param.14) | copy-start | bytes 868
  10.1 1.6 %collective-permute-start.6 = (bf16[128,256]{1,0:T(8,128)(2,1)S(1)}, bf16[128,256]{1,0:T(8,128)(2,1)S(1)}, u32[]{:S(2)}, u32[]{:S(2)}) collective-permute-start(bf16[128,256]{1,0:T(8,128)(2,1)S(1)} %collective-permute-done.2.refs_3_), channel_id=1, source_target_pairs={{0,1},{1,0},{2,3},{3,2},{4,5},{5,4},{6,7},{7,6},{8,9},{9,8},{10,11... | collective-permute-start | bytes 196616 | tf_op jit(solution)/shard_map/ppermute | solution.py:198
  11.2 1.3 %collective-permute-start.5 = (bf16[128,256]{1,0:T(8,128)(2,1)S(1)}, bf16[128,256]{1,0:T(8,128)(2,1)S(1)}, u32[]{:S(2)}, u32[]{:S(2)}) collective-permute-start(bf16[128,256]{1,0:T(8,128)(2,1)S(1)} %collective-permute-done.1.refs_2_), channel_id=1, source_target_pairs={{0,1},{1,0},{2,3},{3,2},{4,5},{5,4},{6,7},{7,6},{8,9},{9,8},{10,11... | collective-permute-start | bytes 196616 | tf_op jit(solution)/shard_map/ppermute | solution.py:198
  11.3 1.3 %collective-permute-start.4 = (bf16[128,256]{1,0:T(8,128)(2,1)S(1)}, bf16[128,256]{1,0:T(8,128)(2,1)S(1)}, u32[]{:S(2)}, u32[]{:S(2)}) collective-permute-start(bf16[128,256]{1,0:T(8,128)(2,1)S(1)} %collective-permute-done.refs_1_), channel_id=1, source_target_pairs={{0,1},{1,0},{2,3},{3,2},{4,5},{5,4},{6,7},{7,6},{8,9},{9,8},{10,11... | collective-permute-start | bytes 196616 | tf_op jit(solution)/shard_map/ppermute | solution.py:198
  15.3 8.2 %collective-permute-start.7 = (bf16[128,256]{1,0:T(8,128)(2,1)S(1)}, bf16[128,256]{1,0:T(8,128)(2,1)S(1)}, u32[]{:S(2)}, u32[]{:S(2)}) collective-permute-start(bf16[128,256]{1,0:T(8,128)(2,1)S(1)} %get-tuple-element.19), channel_id=1, source_target_pairs={{0,8},{2,10},{4,12},{6,14},{8,0},{10,2},{12,4},{14,6},{1,9},{3,11}... | collective-permute-start | bytes 196616 | tf_op jit(solution)/shard_map/ppermute | solution.py:214
  18.2 5.3 %collective-permute-start.8 = (bf16[128,256]{1,0:T(8,128)(2,1)S(1)}, bf16[128,256]{1,0:T(8,128)(2,1)S(1)}, u32[]{:S(2)}, u32[]{:S(2)}) collective-permute-start(bf16[128,256]{1,0:T(8,128)(2,1)S(1)} %get-tuple-element.20), channel_id=1, source_target_pairs={{0,4},{2,6},{4,0},{6,2},{8,12},{10,14},{12,8},{14,10},{1,5},{3,7},... | collective-permute-start | bytes 196616 | tf_op jit(solution)/shard_map/ppermute | solution.py:214
  18.5 7.7 %collective-permute-start.11 = (bf16[128,256]{1,0:T(8,128)(2,1)S(1)}, bf16[128,256]{1,0:T(8,128)(2,1)S(1)}, u32[]{:S(2)}, u32[]{:S(2)}) collective-permute-start(bf16[128,256]{1,0:T(8,128)(2,1)S(1)} %get-tuple-element.21), channel_id=1, source_target_pairs={{0,14},{2,12},{4,10},{6,8},{8,6},{10,4},{12,2},{14,0},{1,15},{3,13... | collective-permute-start | bytes 196616 | tf_op jit(solution)/shard_map/ppermute | solution.py:214
  20.7 6.3 %collective-permute-start.10 = (bf16[128,256]{1,0:T(8,128)(2,1)S(1)}, bf16[128,256]{1,0:T(8,128)(2,1)S(1)}, u32[]{:S(2)}, u32[]{:S(2)}) collective-permute-start(bf16[128,256]{1,0:T(8,128)(2,1)S(1)} %get-tuple-element.21), channel_id=1, source_target_pairs={{0,12},{2,14},{4,8},{6,10},{8,4},{10,6},{12,0},{14,2},{1,13},{3,15... | collective-permute-start | bytes 196616 | tf_op jit(solution)/shard_map/ppermute | solution.py:214
  23.5 4.4 %copy-start.1 = (bf16[1,128,256]{2,1,0:T(8,128)(2,1)S(1)}, bf16[1,128,256]{2,1,0:T(8,128)(2,1)}, u32[]{:S(2)}) copy-start(bf16[1,128,256]{2,1,0:T(8,128)(2,1)} %param.9) | copy-start | bytes 196612
  23.5 4.3 %collective-permute-start.9 = (bf16[128,256]{1,0:T(8,128)(2,1)S(1)}, bf16[128,256]{1,0:T(8,128)(2,1)S(1)}, u32[]{:S(2)}, u32[]{:S(2)}) collective-permute-start(bf16[128,256]{1,0:T(8,128)(2,1)S(1)} %add_convert_fusion.3), channel_id=1, source_target_pairs={{0,2},{2,0},{4,6},{6,4},{8,10},{10,8},{12,14},{14,12},{1,3},{3,1},... | collective-permute-start | bytes 196616 | tf_op jit(solution)/shard_map/ppermute | solution.py:214
  27.9 13.2 %copy-start = (bf16[128,256]{1,0:T(8,128)(2,1)}, bf16[128,256]{1,0:T(8,128)(2,1)S(1)}, u32[]{:S(2)}) copy-start(bf16[128,256]{1,0:T(8,128)(2,1)S(1)} %add_convert_fusion.2.refs_8_) | copy-start | bytes 196612
  27.9 5.3 %collective-permute-start.14 = (bf16[128,256]{1,0:T(8,128)(2,1)S(1)}, bf16[128,256]{1,0:T(8,128)(2,1)S(1)}, u32[]{:S(2)}, u32[]{:S(2)}) collective-permute-start(bf16[128,256]{1,0:T(8,128)(2,1)S(1)} %add_convert_fusion.2.refs_8_), channel_id=1, source_target_pairs={{0,8},{4,12},{8,0},{12,4},{1,9},{5,13},{9,1},{13,5},{2,10},{6,14},... | collective-permute-start | bytes 196616 | tf_op jit(solution)/shard_map/ppermute | solution.py:198
  29.4 6.6 %collective-permute-start.13 = (bf16[128,256]{1,0:T(8,128)(2,1)S(1)}, bf16[128,256]{1,0:T(8,128)(2,1)S(1)}, u32[]{:S(2)}, u32[]{:S(2)}) collective-permute-start(bf16[128,256]{1,0:T(8,128)(2,1)S(1)} %add_convert_fusion.2.refs_8_), channel_id=1, source_target_pairs={{0,12},{4,8},{8,4},{12,0},{1,13},{5,9},{9,5},{13,1},{2,14},{6,10},... | collective-permute-start | bytes 196616 | tf_op jit(solution)/shard_map/ppermute | solution.py:198
  31.7 4.8 %collective-permute-start.12 = (bf16[128,256]{1,0:T(8,128)(2,1)S(1)}, bf16[128,256]{1,0:T(8,128)(2,1)S(1)}, u32[]{:S(2)}, u32[]{:S(2)}) collective-permute-start(bf16[128,256]{1,0:T(8,128)(2,1)S(1)} %add_convert_fusion.2.refs_8_), channel_id=1, source_target_pairs={{0,4},{4,0},{8,12},{12,8},{1,5},{5,1},{9,13},{13,9},{2,6},{6,2},{1... | collective-permute-start | bytes 196616 | tf_op jit(solution)/shard_map/ppermute | solution.py:198
  31.7 4.9 %collective-permute-start.15 = (bf16[128,256]{1,0:T(8,128)(2,1)S(1)}, bf16[128,256]{1,0:T(8,128)(2,1)S(1)}, u32[]{:S(2)}, u32[]{:S(2)}) collective-permute-start(bf16[128,256]{1,0:T(8,128)(2,1)S(1)} %add_convert_fusion.2.refs_8_), channel_id=1, source_target_pairs={{0,1},{1,0},{2,3},{3,2},{4,5},{5,4},{6,7},{7,6},{8,9},{9,8},{10,11... | collective-permute-start | bytes 196616 | tf_op jit(solution)/shard_map/ppermute | solution.py:198
  33.2 3.4 %collective-permute-start.18 = (bf16[128,256]{1,0:T(8,128)(2,1)S(1)}, bf16[128,256]{1,0:T(8,128)(2,1)S(1)}, u32[]{:S(2)}, u32[]{:S(2)}) collective-permute-start(bf16[128,256]{1,0:T(8,128)(2,1)S(1)} %collective-permute-done.14.refs_11_), channel_id=1, source_target_pairs={{0,1},{1,0},{2,3},{3,2},{4,5},{5,4},{6,7},{7,6},{8,9},{9,8},{10,11... | collective-permute-start | bytes 196616 | tf_op jit(solution)/shard_map/ppermute | solution.py:198
  36.0 1.3 %collective-permute-start.17 = (bf16[128,256]{1,0:T(8,128)(2,1)S(1)}, bf16[128,256]{1,0:T(8,128)(2,1)S(1)}, u32[]{:S(2)}, u32[]{:S(2)}) collective-permute-start(bf16[128,256]{1,0:T(8,128)(2,1)S(1)} %collective-permute-done.13.refs_10_), channel_id=1, source_target_pairs={{0,1},{1,0},{2,3},{3,2},{4,5},{5,4},{6,7},{7,6},{8,9},{9,8},{10,11... | collective-permute-start | bytes 196616 | tf_op jit(solution)/shard_map/ppermute | solution.py:198
  36.5 1.3 %collective-permute-start.16 = (bf16[128,256]{1,0:T(8,128)(2,1)S(1)}, bf16[128,256]{1,0:T(8,128)(2,1)S(1)}, u32[]{:S(2)}, u32[]{:S(2)}) collective-permute-start(bf16[128,256]{1,0:T(8,128)(2,1)S(1)} %collective-permute-done.12.refs_9_), channel_id=1, source_target_pairs={{0,1},{1,0},{2,3},{3,2},{4,5},{5,4},{6,7},{7,6},{8,9},{9,8},{10,11... | collective-permute-start | bytes 196616 | tf_op jit(solution)/shard_map/ppermute | solution.py:198
  41.1 7.1 %collective-permute-start.19 = (bf16[128,256]{1,0:T(8,128)(2,1)S(1)}, bf16[128,256]{1,0:T(8,128)(2,1)S(1)}, u32[]{:S(2)}, u32[]{:S(2)}) collective-permute-start(bf16[128,256]{1,0:T(8,128)(2,1)S(1)} %get-tuple-element.24), channel_id=1, source_target_pairs={{0,8},{2,10},{4,12},{6,14},{8,0},{10,2},{12,4},{14,6},{1,9},{3,11}... | collective-permute-start | bytes 196616 | tf_op jit(solution)/shard_map/ppermute | solution.py:214
  42.1 6.1 %collective-permute-start.20 = (bf16[128,256]{1,0:T(8,128)(2,1)S(1)}, bf16[128,256]{1,0:T(8,128)(2,1)S(1)}, u32[]{:S(2)}, u32[]{:S(2)}) collective-permute-start(bf16[128,256]{1,0:T(8,128)(2,1)S(1)} %get-tuple-element.25), channel_id=1, source_target_pairs={{0,4},{2,6},{4,0},{6,2},{8,12},{10,14},{12,8},{14,10},{1,5},{3,7},... | collective-permute-start | bytes 196616 | tf_op jit(solution)/shard_map/ppermute | solution.py:214
  43.1 8.4 %collective-permute-start.23 = (bf16[128,256]{1,0:T(8,128)(2,1)S(1)}, bf16[128,256]{1,0:T(8,128)(2,1)S(1)}, u32[]{:S(2)}, u32[]{:S(2)}) collective-permute-start(bf16[128,256]{1,0:T(8,128)(2,1)S(1)} %get-tuple-element.26), channel_id=1, source_target_pairs={{0,14},{2,12},{4,10},{6,8},{8,6},{10,4},{12,2},{14,0},{1,15},{3,13... | collective-permute-start | bytes 196616 | tf_op jit(solution)/shard_map/ppermute | solution.py:214
  46.2 6.1 %collective-permute-start.22 = (bf16[128,256]{1,0:T(8,128)(2,1)S(1)}, bf16[128,256]{1,0:T(8,128)(2,1)S(1)}, u32[]{:S(2)}, u32[]{:S(2)}) collective-permute-start(bf16[128,256]{1,0:T(8,128)(2,1)S(1)} %get-tuple-element.26), channel_id=1, source_target_pairs={{0,12},{2,14},{4,8},{6,10},{8,4},{10,6},{12,0},{14,2},{1,13},{3,15... | collective-permute-start | bytes 196616 | tf_op jit(solution)/shard_map/ppermute | solution.py:214
  48.2 5.5 %collective-permute-start.21 = (bf16[128,256]{1,0:T(8,128)(2,1)S(1)}, bf16[128,256]{1,0:T(8,128)(2,1)S(1)}, u32[]{:S(2)}, u32[]{:S(2)}) collective-permute-start(bf16[128,256]{1,0:T(8,128)(2,1)S(1)} %add_convert_fusion.1), channel_id=1, source_target_pairs={{0,2},{2,0},{4,6},{6,4},{8,10},{10,8},{12,14},{14,12},{1,3},{3,1},... | collective-permute-start | bytes 196616 | tf_op jit(solution)/shard_map/ppermute | solution.py:214

commit v7 on v5

--- a/solution.py
+++ b/solution.py
@@ -10,7 +10,9 @@
 gather_four = [0, 1, 3, 2]
 target_four = [0, 2, 1, 3]
 direct_distances = (3,)
+first_four = [0, 1, 3, 2]
 unroll_slots = 4
+group_bit, last_bit = 8, 17
 wide_sectors = 4
 step_lefts = 2
 whole_vmem = pl.BlockSpec(memory_space=pltpu.VMEM)
@@ -25,6 +27,10 @@
     return target_four if sectors == 4 else list(range(sectors))
 
 
+def first_order(sectors):
+    return [i + at for at in (0, sectors) for i in (first_four if sectors == 4 else range(sectors))]
+
+
 def place_in(order, distance):
     return sum(jnp.where(distance == far, place, 0) for place, far in enumerate(order))
 
@@ -33,23 +39,31 @@
     return -(-(slots + unroll_slots) // 128) * 128
 
 
-def make_plan(me, left_index, right_index, source, target, live, sectors, lefts, rights):
-    slots = left_index.shape[0]
-    length = plan_length(slots)
-    number = jnp.arange(slots, dtype=jnp.int32)
-    alive = number < live
+def make_plan(sectors, lefts, rights, live, left_index, right_index, source, target, length):
+    slots = left_index.shape[1]
+    me = lax.axis_index("term")
+
+    def columns_of(shape, dimension):
+        return lax.broadcasted_iota(jnp.int32, shape, dimension)
+
+    def total(chosen, values, axis):
+        return jnp.sum(jnp.where(chosen, values, 0.0), axis=axis, keepdims=True)
+
+    alive = columns_of((1, slots), 1) < live
     sent_at = place_in(target_order(sectors), target ^ me)
-    group = jnp.where(alive, right_index * sectors + sent_at, rights * sectors)
-    half = jnp.where(alive, place_in(gather_order(sectors), source ^ me) * lefts + left_index, 0)
-    same = group[None, :] == group[:, None]
-    before = number[None, :] < number[:, None]
-    place = jnp.sum(((group[None, :] < group[:, None]) | (same & before)).astype(jnp.int32), axis=1)
-    goes_on = jnp.max((same & before).astype(jnp.int32), axis=1)
-    word = half + (group << 12) + (goes_on << 24)
-    at = jnp.arange(length, dtype=jnp.int32)
-    sorted_words = jnp.sum(jnp.where(place[None, :] == at[:, None], word[None, :], 0), axis=1)
-    rest = jnp.where(at == length - 1, live, (rights * sectors) << 12)
-    return jnp.where(at < slots, sorted_words, rest)[None]
+    group = jnp.where(alive, right_index * sectors + sent_at, rights * sectors).astype(jnp.float32)
+    half = jnp.where(alive, place_in(gather_order(sectors), source ^ me) * lefts + left_index, 0).astype(jnp.float32)
+    square = (slots, slots)
+    one, two = columns_of(square, 0), columns_of(square, 1)
+    group_here, half_here = (total(one == two, row, 1) for row in (group, half))
+    earlier = (group == group_here) & (two < one)
+    place = total((group < group_here) | earlier, 1.0, 1)
+    goes_on = jnp.max(jnp.where(earlier, 1.0, 0.0), axis=1, keepdims=True)
+    word = half_here + group_here * (1 << group_bit) + goes_on * (1 << last_bit)
+    at = columns_of((slots, length), 1).astype(jnp.float32)
+    sorted_words = total(place == at, word, 0).astype(jnp.int32)
+    at = columns_of((1, length), 1)
+    return jnp.where(at < slots, sorted_words, jnp.where(at == length - 1, live, (rights * sectors) << group_bit))
 
 
 def half_products(sectors, left_ref, vector, halves):
@@ -73,9 +87,9 @@
     def some_slots(turn, total):
         for step in range(unroll_slots):
             word = plan_ref[0, turn * unroll_slots + step]
-            keep = (word >> 24).astype(jnp.float32)
-            total = total * keep + halves[word & 4095]
-            sums[(word >> 12) & 4095] = total.astype(jnp.bfloat16)
+            keep = (word >> last_bit).astype(jnp.float32)
+            total = total * keep + halves[word & ((1 << group_bit) - 1)]
+            sums[(word >> group_bit) & ((1 << (last_bit - group_bit)) - 1)] = total.astype(jnp.bfloat16)
         return total
 
     turns = (live + unroll_slots - 1) // unroll_slots
@@ -104,28 +118,36 @@
     return ref[...].astype(jnp.float32)
 
 
-def fetch_kernel(*refs):
-    arrived = refs[-1]
-    count = len(refs) // 2
-    copies = [pltpu.make_async_copy(refs[i], refs[count + i], arrived.at[i]) for i in range(count)]
+def prepare_kernel(sectors, count_ref, *refs):
+    sources, kept, plan_ref = refs[:7], refs[7:10], refs[10]
+    indices, arrived = refs[11:15], refs[15]
+    copies = [pltpu.make_async_copy(*pair, arrived.at[i]) for i, pair in enumerate(zip(sources, (*indices, *kept)))]
     for copy in copies:
         copy.start()
-    for copy in copies:
+    for copy in copies[:4]:
         copy.wait()
-
-
-def fetch(*arrays):
+    lefts, rights = kept[0].shape[0], kept[1].shape[0]
+    rows = [ref[...] for ref in indices]
+    plan_ref[...] = make_plan(sectors, lefts, rights, count_ref[0], *rows, plan_ref.shape[1])
+    for copy in copies[4:]:
+        copy.wait()
+
+
+def prepare(sectors, indices, count, arrays):
+    sources = (*indices, *arrays)
     return pl.pallas_call(
-        fetch_kernel,
-        out_shape=[pltpu.VMEM(x.shape, x.dtype) for x in arrays],
-        in_specs=[stays_out] * len(arrays),
-        out_specs=[whole_vmem] * len(arrays),
-        scratch_shapes=[pltpu.SemaphoreType.DMA((len(arrays),))],
-    )(*(pltpu.with_memory_space_constraint(x, pltpu.HBM) for x in arrays))
+        functools.partial(prepare_kernel, sectors),
+        out_shape=[pltpu.VMEM(x.shape, x.dtype) for x in arrays]
+        + [pltpu.VMEM((1, plan_length(indices[0].shape[1])), jnp.int32)],
+        in_specs=[pl.BlockSpec(memory_space=pltpu.SMEM)] + [stays_out] * len(sources),
+        out_specs=[whole_vmem] * (len(arrays) + 1),
+        scratch_shapes=[pltpu.VMEM(x.shape, x.dtype) for x in indices] + [pltpu.SemaphoreType.DMA((len(sources),))],
+    )(count, *(pltpu.with_memory_space_constraint(x, pltpu.HBM) for x in sources))
 
 
 def first_kernel(sectors, plan_in, left, right, *refs):
-    psis, out_refs = refs[: 2 * sectors], refs[2 * sectors : -5]
+    given, out_refs = refs[: 2 * sectors], refs[2 * sectors : -5]
+    psis = [given[first_order(sectors).index(i)] for i in range(2 * sectors)]
     plan_ref, arrived, vector, halves, sums = refs[-5:]
     core = lax.axis_index("pair")
     plan_copy = pltpu.make_async_copy(plan_in, plan_ref, arrived)
@@ -245,15 +267,14 @@
 ):
     sectors = lax.axis_size("term")
     lefts, rights = left_blocks.shape[1], right_blocks.shape[1]
-    me = lax.axis_index("term").astype(jnp.int32)
     own = psi[0]
-    left, right, own_kept = fetch(left_blocks[0], right_blocks[0], own)
+    indices = (left_index, right_index, block_source, block_target)
+    left, right, own_kept, plan = prepare(sectors, indices, block_count, (left_blocks[0], right_blocks[0], own))
     psis = gather(own, own_kept)
-    indices = (left_index[0], right_index[0], block_source[0], block_target[0])
-    plan = make_plan(me, *indices, block_count[0], sectors, lefts, rights)
     energy = sector_energy[0]
     call = functools.partial(call_product, sectors=sectors, lefts=lefts, rights=rights)
-    parts = call(first_kernel, inside=[plan, left, right, *psis], kept=[])
+    handed = [psis[i] for i in first_order(sectors)]
+    parts = call(first_kernel, inside=[plan, left, right, *handed], kept=[])
     sigma_first = (owner_sum(parts) + energy * own.astype(jnp.float32)).astype(jnp.bfloat16)
     correction, *parts = call(
         second_kernel,

time: 53.9 us -> 53.5 us (level)
  local copies, waits for them, and re-layouts: 1.33 us -> 0.01 us
  waiting for transfers between devices: 13.5 us -> 14.8 us
    unnamed x12 -> x4, local copies, waits for them, and re-layouts: 1.33 us -> 0.01 us
    ppermute x14, waiting for transfers between devices: 7.53 us -> 8.52 us  [swap(): lax.ppermute(value, axis, [(i, i ^ bit) for i in range(lax.axis_size(axis...]
  transfers between devices with their start and end apart: 24 -> 24, of which waited for: 15 -> 14; matrix products, arithmetic and copies ran while one was open for 1% -> 0% of each run, Pallas kernels for 3% -> 3%
where the time goes in v7:
time: 53.5 us; the launch traced here: 53.4 us
  starting transfers between devices  28.6 us (53%)
  waiting for transfers between devices  14.8 us (28%)
  Pallas kernels  7.29 us (14%)
  between operations  2.03 us (4%)
  other arithmetic  0.77 us (1%)
    ppermute x10, starting transfers between devices, send(): return lax.ppermute(value, ('term', 'sub'), route)  17.7 us
    ppermute x14, starting transfers between devices, swap(): lax.ppermute(value, axis, [(i, i ^ bit) for i in range(lax.axis_size(axis...  10.9 us
    ppermute x14, waiting for transfers between devices, swap(): lax.ppermute(value, axis, [(i, i ^ bit) for i in range(lax.axis_size(axis...  8.52 us
    ppermute x10, waiting for transfers between devices, send(): return lax.ppermute(value, ('term', 'sub'), route)  6.25 us
    pallas_call x2, Pallas kernels, call_product(): pl.pallas_call(functools.partial(kernel, sectors), out_shape=outs, in_spe...  5.78 us
    pallas_call x1, Pallas kernels, prepare(): pl.pallas_call(functools.partial(prepare_kernel, sectors), out_shape=[plt...  1.51 us
  transfers between devices with their start and end apart: 24, of which 14 were waited for; matrix products, arithmetic and copies ran while one was open for 0% of the time, Pallas kernels for 3%

profile of v7, /device:TPU:0, one launch (start us, length us, event | category | flops | bytes accessed | tf_op | source)
XLA Modules:
  0.0 53.4 jit_solution(895467786067756732)
XLA Ops:
  0.6 5.1 %collective-permute-start.2 = (bf16[128,256]{1,0:T(8,128)(2,1)}, bf16[128,256]{1,0:T(8,128)(2,1)S(1)}, u32[]{:S(2)}, u32[]{:S(2)}) collective-permute-start(bf16[128,256]{1,0:T(8,128)(2,1)} %bitcast.13), channel_id=1, source_target_pairs={{0,12},{4,8},{8,4},{12,0},{1,13},{5,9},{9,5},{13,1},{2,14},{6,10},... | collective-permute-start | bytes 196616 | tf_op jit(solution)/shard_map/ppermute | solution.py:219
  5.8 0.6 %collective-permute-start = (bf16[128,256]{1,0:T(8,128)(2,1)}, bf16[128,256]{1,0:T(8,128)(2,1)S(1)}, u32[]{:S(2)}, u32[]{:S(2)}) collective-permute-start(bf16[128,256]{1,0:T(8,128)(2,1)} %bitcast.15), channel_id=1, source_target_pairs={{0,4},{4,0},{8,12},{12,8},{1,5},{5,1},{9,13},{13,9},{2,6},{6,2},{1... | collective-permute-start | bytes 196616 | tf_op jit(solution)/shard_map/ppermute | solution.py:219
  7.0 1.5 %shard_map.104 = (bf16[8,128,256]{2,1,0:T(8,128)(2,1)S(1)}, bf16[8,256,256]{2,1,0:T(8,128)(2,1)S(1)}, bf16[128,256]{1,0:T(8,128)(2,1)S(1)}, s32[1,128]{1,0:T(1,128)S(1)}) custom-call(s32[1]{0:T(128)S(6)} %copy.11.count_ref, s32[1,72]{1,0:T(1,128)} %refs_0_.1, s32[1,72]{1,0:T(1,128)} %refs_1_.1, s32[1,72]{1,0:T(1,128)} %refs_2_.1, s32[1,72]{1,0:T(1,128)} %refs_3_.1, ...), custom_call_target="tpu_custom_call" | custom-call | tf_op jit(solution)/shard_map/pallas_call | solution.py:138
  8.7 0.5 collective-permute-start.6
  9.1 2.4 %collective-permute-done.1.refs_2_.refs_3_ = bf16[128,256]{1,0:T(8,128)(2,1)S(1)} collective-permute-done((bf16[128,256]{1,0:T(8,128)(2,1)}, bf16[128,256]{1,0:T(8,128)(2,1)S(1)}, u32[]{:S(2)}, u32[]{:S(2)}) %collective-permute-start.1) | collective-permute-done | bytes 65568 | tf_op jit(solution)/shard_map/ppermute | solution.py:219
  11.6 0.5 collective-permute-start.4
  12.1 0.7 %collective-permute-done.5.refs_6_.refs_7_ = bf16[128,256]{1,0:T(8,128)(2,1)S(1)} collective-permute-done((bf16[128,256]{1,0:T(8,128)(2,1)S(1)}, bf16[128,256]{1,0:T(8,128)(2,1)S(1)}, u32[]{:S(2)}, u32[]{:S(2)}) %collective-permute-start.5) | collective-permute-done | bytes 65568 | tf_op jit(solution)/shard_map/ppermute | solution.py:219
  13.0 2.5 %shard_map.105 = (f32[128,256]{1,0:T(8,128)S(1)}, bf16[128,256]{1,0:T(8,128)(2,1)S(1)}, bf16[128,256]{1,0:T(8,128)(2,1)S(1)}, bf16[128,256]{1,0:T(8,128)(2,1)S(1)}) custom-call(s32[1,128]{1,0:T(1,128)S(1)} %get-tuple-element.15.plan_in, bf16[8,128,256]{2,1,0:T(8,128)(2,1)S(1)} %get-tuple-element.16.left, bf16[8,256,256]{2,1,0:T(8,128)(2,1)S(1)} %get-tuple-element.17.right, ...), custom_call_target="tpu_custom_call" | custom-call | tf_op jit(solution)/shard_map/pallas_call | solution.py:200
  15.5 1.4 %collective-permute-start.7 = (bf16[128,256]{1,0:T(8,128)(2,1)S(1)}, bf16[128,256]{1,0:T(8,128)(2,1)S(1)}, u32[]{:S(2)}, u32[]{:S(2)}) collective-permute-start(bf16[128,256]{1,0:T(8,128)(2,1)S(1)} %get-tuple-element.20), channel_id=1, source_target_pairs={{0,8},{2,10},{4,12},{6,14},{8,0},{10,2},{12,4},{14,6},{1,9},{3,11}... | collective-permute-start | bytes 196616 | tf_op jit(solution)/shard_map/ppermute | solution.py:235
  16.9 2.0 %collective-permute-start.8 = (bf16[128,256]{1,0:T(8,128)(2,1)S(1)}, bf16[128,256]{1,0:T(8,128)(2,1)S(1)}, u32[]{:S(2)}, u32[]{:S(2)}) collective-permute-start(bf16[128,256]{1,0:T(8,128)(2,1)S(1)} %get-tuple-element.21), channel_id=1, source_target_pairs={{0,4},{2,6},{4,0},{6,2},{8,12},{10,14},{12,8},{14,10},{1,5},{3,7},... | collective-permute-start | bytes 196616 | tf_op jit(solution)/shard_map/ppermute | solution.py:235
  18.9 2.2 %collective-permute-start.11 = (bf16[128,256]{1,0:T(8,128)(2,1)S(1)}, bf16[128,256]{1,0:T(8,128)(2,1)S(1)}, u32[]{:S(2)}, u32[]{:S(2)}) collective-permute-start(bf16[128,256]{1,0:T(8,128)(2,1)S(1)} %get-tuple-element.22), channel_id=1, source_target_pairs={{0,14},{2,12},{4,10},{6,8},{8,6},{10,4},{12,2},{14,0},{1,15},{3,13... | collective-permute-start | bytes 196616 | tf_op jit(solution)/shard_map/ppermute | solution.py:235
  21.1 2.5 %collective-permute-start.10 = (bf16[128,256]{1,0:T(8,128)(2,1)S(1)}, bf16[128,256]{1,0:T(8,128)(2,1)S(1)}, u32[]{:S(2)}, u32[]{:S(2)}) collective-permute-start(bf16[128,256]{1,0:T(8,128)(2,1)S(1)} %get-tuple-element.22), channel_id=1, source_target_pairs={{0,12},{2,14},{4,8},{6,10},{8,4},{10,6},{12,0},{14,2},{1,13},{3,15... | collective-permute-start | bytes 196616 | tf_op jit(solution)/shard_map/ppermute | solution.py:235
  23.7 0.6 %collective-permute-start.9 = (bf16[128,256]{1,0:T(8,128)(2,1)S(1)}, bf16[128,256]{1,0:T(8,128)(2,1)S(1)}, u32[]{:S(2)}, u32[]{:S(2)}) collective-permute-start(bf16[128,256]{1,0:T(8,128)(2,1)S(1)} %add_convert_fusion.3), channel_id=1, source_target_pairs={{0,2},{2,0},{4,6},{6,4},{8,10},{10,8},{12,14},{14,12},{1,3},{3,1},... | collective-permute-start | bytes 196616 | tf_op jit(solution)/shard_map/ppermute | solution.py:235
  24.9 1.3 %collective-permute-done.11 = bf16[128,256]{1,0:T(8,128)(2,1)S(1)} collective-permute-done((bf16[128,256]{1,0:T(8,128)(2,1)S(1)}, bf16[128,256]{1,0:T(8,128)(2,1)S(1)}, u32[]{:S(2)}, u32[]{:S(2)}) %collective-permute-start.11) | collective-permute-done | bytes 65568 | tf_op jit(solution)/shard_map/ppermute | solution.py:235
  26.3 0.9 %collective-permute-done.10 = bf16[128,256]{1,0:T(8,128)(2,1)S(1)} collective-permute-done((bf16[128,256]{1,0:T(8,128)(2,1)S(1)}, bf16[128,256]{1,0:T(8,128)(2,1)S(1)}, u32[]{:S(2)}, u32[]{:S(2)}) %collective-permute-start.10) | collective-permute-done | bytes 65568 | tf_op jit(solution)/shard_map/ppermute | solution.py:235
  27.2 0.8 %collective-permute-done.9 = bf16[128,256]{1,0:T(8,128)(2,1)S(1)} collective-permute-done((bf16[128,256]{1,0:T(8,128)(2,1)S(1)}, bf16[128,256]{1,0:T(8,128)(2,1)S(1)}, u32[]{:S(2)}, u32[]{:S(2)}) %collective-permute-start.9) | collective-permute-done | bytes 65568 | tf_op jit(solution)/shard_map/ppermute | solution.py:235
  28.1 1.1 %collective-permute-start.14 = (bf16[128,256]{1,0:T(8,128)(2,1)S(1)}, bf16[128,256]{1,0:T(8,128)(2,1)S(1)}, u32[]{:S(2)}, u32[]{:S(2)}) collective-permute-start(bf16[128,256]{1,0:T(8,128)(2,1)S(1)} %add_convert_fusion.2.refs_8_), channel_id=1, source_target_pairs={{0,8},{4,12},{8,0},{12,4},{1,9},{5,13},{9,1},{13,5},{2,10},{6,14},... | collective-permute-start | bytes 196616 | tf_op jit(solution)/shard_map/ppermute | solution.py:219
  29.2 1.7 %collective-permute-start.13 = (bf16[128,256]{1,0:T(8,128)(2,1)S(1)}, bf16[128,256]{1,0:T(8,128)(2,1)S(1)}, u32[]{:S(2)}, u32[]{:S(2)}) collective-permute-start(bf16[128,256]{1,0:T(8,128)(2,1)S(1)} %add_convert_fusion.2.refs_8_), channel_id=1, source_target_pairs={{0,12},{4,8},{8,4},{12,0},{1,13},{5,9},{9,5},{13,1},{2,14},{6,10},... | collective-permute-start | bytes 196616 | tf_op jit(solution)/shard_map/ppermute | solution.py:219
  30.9 0.8 %collective-permute-start.12 = (bf16[128,256]{1,0:T(8,128)(2,1)S(1)}, bf16[128,256]{1,0:T(8,128)(2,1)S(1)}, u32[]{:S(2)}, u32[]{:S(2)}) collective-permute-start(bf16[128,256]{1,0:T(8,128)(2,1)S(1)} %add_convert_fusion.2.refs_8_), channel_id=1, source_target_pairs={{0,4},{4,0},{8,12},{12,8},{1,5},{5,1},{9,13},{13,9},{2,6},{6,2},{1... | collective-permute-start | bytes 196616 | tf_op jit(solution)/shard_map/ppermute | solution.py:219
  31.6 3.9 %collective-permute-done.14.refs_11_ = bf16[128,256]{1,0:T(8,128)(2,1)S(1)} collective-permute-done((bf16[128,256]{1,0:T(8,128)(2,1)S(1)}, bf16[128,256]{1,0:T(8,128)(2,1)S(1)}, u32[]{:S(2)}, u32[]{:S(2)}) %collective-permute-start.14) | collective-permute-done | bytes 65568 | tf_op jit(solution)/shard_map/ppermute | solution.py:219
  35.5 0.5 collective-permute-start.17
  36.1 0.7 %collective-permute-done.18.refs_15_ = bf16[128,256]{1,0:T(8,128)(2,1)S(1)} collective-permute-done((bf16[128,256]{1,0:T(8,128)(2,1)S(1)}, bf16[128,256]{1,0:T(8,128)(2,1)S(1)}, u32[]{:S(2)}, u32[]{:S(2)}) %collective-permute-start.18) | collective-permute-done | bytes 65568 | tf_op jit(solution)/shard_map/ppermute | solution.py:219
  36.9 0.4 collective-permute-done.16.refs_13_
  37.4 3.3 %shard_map.106 = (bf16[128,256]{1,0:T(8,128)(2,1)S(1)}, f32[128,256]{1,0:T(8,128)S(1)}, bf16[128,256]{1,0:T(8,128)(2,1)S(1)}, bf16[128,256]{1,0:T(8,128)(2,1)S(1)}, bf16[128,256]{1,0:T(8,128)(2,1)S(1)}) custom-call(s32[1,128]{1,0:T(1,128)S(1)} %get-tuple-element.15.plan_in, bf16[8,128,256]{2,1,0:T(8,128)(2,1)S(1)} %get-tuple-element.16.left, ...), custom_call_target="tpu_custom_call" | custom-call | tf_op jit(solution)/shard_map/pallas_call | solution.py:200
  40.7 1.1 %collective-permute-start.19 = (bf16[128,256]{1,0:T(8,128)(2,1)S(1)}, bf16[128,256]{1,0:T(8,128)(2,1)S(1)}, u32[]{:S(2)}, u32[]{:S(2)}) collective-permute-start(bf16[128,256]{1,0:T(8,128)(2,1)S(1)} %get-tuple-element.24), channel_id=1, source_target_pairs={{0,8},{2,10},{4,12},{6,14},{8,0},{10,2},{12,4},{14,6},{1,9},{3,11}... | collective-permute-start | bytes 196616 | tf_op jit(solution)/shard_map/ppermute | solution.py:235
  41.7 1.4 %collective-permute-start.20 = (bf16[128,256]{1,0:T(8,128)(2,1)S(1)}, bf16[128,256]{1,0:T(8,128)(2,1)S(1)}, u32[]{:S(2)}, u32[]{:S(2)}) collective-permute-start(bf16[128,256]{1,0:T(8,128)(2,1)S(1)} %get-tuple-element.25), channel_id=1, source_target_pairs={{0,4},{2,6},{4,0},{6,2},{8,12},{10,14},{12,8},{14,10},{1,5},{3,7},... | collective-permute-start | bytes 196616 | tf_op jit(solution)/shard_map/ppermute | solution.py:235
  43.2 3.2 %collective-permute-start.23 = (bf16[128,256]{1,0:T(8,128)(2,1)S(1)}, bf16[128,256]{1,0:T(8,128)(2,1)S(1)}, u32[]{:S(2)}, u32[]{:S(2)}) collective-permute-start(bf16[128,256]{1,0:T(8,128)(2,1)S(1)} %get-tuple-element.26), channel_id=1, source_target_pairs={{0,14},{2,12},{4,10},{6,8},{8,6},{10,4},{12,2},{14,0},{1,15},{3,13... | collective-permute-start | bytes 196616 | tf_op jit(solution)/shard_map/ppermute | solution.py:235
  46.4 2.0 %collective-permute-start.22 = (bf16[128,256]{1,0:T(8,128)(2,1)S(1)}, bf16[128,256]{1,0:T(8,128)(2,1)S(1)}, u32[]{:S(2)}, u32[]{:S(2)}) collective-permute-start(bf16[128,256]{1,0:T(8,128)(2,1)S(1)} %get-tuple-element.26), channel_id=1, source_target_pairs={{0,12},{2,14},{4,8},{6,10},{8,4},{10,6},{12,0},{14,2},{1,13},{3,15... | collective-permute-start | bytes 196616 | tf_op jit(solution)/shard_map/ppermute | solution.py:235
  48.4 1.2 %collective-permute-start.21 = (bf16[128,256]{1,0:T(8,128)(2,1)S(1)}, bf16[128,256]{1,0:T(8,128)(2,1)S(1)}, u32[]{:S(2)}, u32[]{:S(2)}) collective-permute-start(bf16[128,256]{1,0:T(8,128)(2,1)S(1)} %add_convert_fusion.1), channel_id=1, source_target_pairs={{0,2},{2,0},{4,6},{6,4},{8,10},{10,8},{12,14},{14,12},{1,3},{3,1},... | collective-permute-start | bytes 196616 | tf_op jit(solution)/shard_map/ppermute | solution.py:235
  49.6 1.0 %collective-permute-done.23 = bf16[128,256]{1,0:T(8,128)(2,1)S(1)} collective-permute-done((bf16[128,256]{1,0:T(8,128)(2,1)S(1)}, bf16[128,256]{1,0:T(8,128)(2,1)S(1)}, u32[]{:S(2)}, u32[]{:S(2)}) %collective-permute-start.23) | collective-permute-done | bytes 65568 | tf_op jit(solution)/shard_map/ppermute | solution.py:235
  50.6 2.0 %collective-permute-done.22 = bf16[128,256]{1,0:T(8,128)(2,1)S(1)} collective-permute-done((bf16[128,256]{1,0:T(8,128)(2,1)S(1)}, bf16[128,256]{1,0:T(8,128)(2,1)S(1)}, u32[]{:S(2)}, u32[]{:S(2)}) %collective-permute-start.22) | collective-permute-done | bytes 65568 | tf_op jit(solution)/shard_map/ppermute | solution.py:235
  52.8 0.7 %fusion = bf16[1,128,256]{2,1,0:T(8,128)(2,1)} fusion(bf16[128,256]{1,0:T(8,128)(2,1)S(1)} %get-tuple-element.27, bf16[128,256]{1,0:T(8,128)(2,1)S(1)} %collective-permute-done.23, bf16[128,256]{1,0:T(8,128)(2,1)S(1)} %collective-permute-done.22, bf16[128,256]{1,0:T(8,128)(2,1)S(1)} %collective-permute-done.21, bf16[128,256]{1,0:T(8,128)(2,1)S(1)} %add_convert_fusion.1, ...), kind=kLoop, calls=%fused_computation.4 | loop fusion | flops 360448 | bytes 393220 | tf_op jit(solution)/shard_map/broadcast_in_dim | solution.py:285
  (27 shorter events, 0.9 us)
Async XLA Ops:
  0.6 8.0 %collective-permute-start.2 = (bf16[128,256]{1,0:T(8,128)(2,1)}, bf16[128,256]{1,0:T(8,128)(2,1)S(1)}, u32[]{:S(2)}, u32[]{:S(2)}) collective-permute-start(bf16[128,256]{1,0:T(8,128)(2,1)} %bitcast.13), channel_id=1, source_target_pairs={{0,12},{4,8},{8,4},{12,0},{1,13},{5,9},{9,5},{13,1},{2,14},{6,10},... | collective-permute-start | bytes 196616 | tf_op jit(solution)/shard_map/ppermute | solution.py:219
  5.7 5.8 %collective-permute-start.1 = (bf16[128,256]{1,0:T(8,128)(2,1)}, bf16[128,256]{1,0:T(8,128)(2,1)S(1)}, u32[]{:S(2)}, u32[]{:S(2)}) collective-permute-start(bf16[128,256]{1,0:T(8,128)(2,1)} %bitcast.14), channel_id=1, source_target_pairs={{0,8},{4,12},{8,0},{12,4},{1,9},{5,13},{9,1},{13,5},{2,10},{6,14},... | collective-permute-start | bytes 196616 | tf_op jit(solution)/shard_map/ppermute | solution.py:219
  5.8 5.8 %collective-permute-start = (bf16[128,256]{1,0:T(8,128)(2,1)}, bf16[128,256]{1,0:T(8,128)(2,1)S(1)}, u32[]{:S(2)}, u32[]{:S(2)}) collective-permute-start(bf16[128,256]{1,0:T(8,128)(2,1)} %bitcast.15), channel_id=1, source_target_pairs={{0,4},{4,0},{8,12},{12,8},{1,5},{5,1},{9,13},{13,9},{2,6},{6,2},{1... | collective-permute-start | bytes 196616 | tf_op jit(solution)/shard_map/ppermute | solution.py:219
  8.6 3.5 %collective-permute-start.3 = (bf16[128,256]{1,0:T(8,128)(2,1)S(1)}, bf16[128,256]{1,0:T(8,128)(2,1)S(1)}, u32[]{:S(2)}, u32[]{:S(2)}) collective-permute-start(bf16[128,256]{1,0:T(8,128)(2,1)S(1)} %get-tuple-element.18.refs_0_), channel_id=1, source_target_pairs={{0,1},{1,0},{2,3},{3,2},{4,5},{5,4},{6,7},{7,6},{8,9},{9,8},{10,11... | collective-permute-start | bytes 196616 | tf_op jit(solution)/shard_map/ppermute | solution.py:219
  8.7 3.4 %collective-permute-start.6 = (bf16[128,256]{1,0:T(8,128)(2,1)S(1)}, bf16[128,256]{1,0:T(8,128)(2,1)S(1)}, u32[]{:S(2)}, u32[]{:S(2)}) collective-permute-start(bf16[128,256]{1,0:T(8,128)(2,1)S(1)} %collective-permute-done.2.refs_3_.refs_2_), channel_id=1, source_target_pairs={{0,1},{1,0},{2,3},{3,2},{4,5},{5,4},{6,7},{7,6},{8,9},{9,8},{10,11... | collective-permute-start | bytes 196616 | tf_op jit(solution)/shard_map/ppermute | solution.py:219
  11.6 1.3 %collective-permute-start.5 = (bf16[128,256]{1,0:T(8,128)(2,1)S(1)}, bf16[128,256]{1,0:T(8,128)(2,1)S(1)}, u32[]{:S(2)}, u32[]{:S(2)}) collective-permute-start(bf16[128,256]{1,0:T(8,128)(2,1)S(1)} %collective-permute-done.1.refs_2_.refs_3_), channel_id=1, source_target_pairs={{0,1},{1,0},{2,3},{3,2},{4,5},{5,4},{6,7},{7,6},{8,9},{9,8},{10,11... | collective-permute-start | bytes 196616 | tf_op jit(solution)/shard_map/ppermute | solution.py:219
  11.6 1.4 %collective-permute-start.4 = (bf16[128,256]{1,0:T(8,128)(2,1)S(1)}, bf16[128,256]{1,0:T(8,128)(2,1)S(1)}, u32[]{:S(2)}, u32[]{:S(2)}) collective-permute-start(bf16[128,256]{1,0:T(8,128)(2,1)S(1)} %collective-permute-done.refs_1_), channel_id=1, source_target_pairs={{0,1},{1,0},{2,3},{3,2},{4,5},{5,4},{6,7},{7,6},{8,9},{9,8},{10,11... | collective-permute-start | bytes 196616 | tf_op jit(solution)/shard_map/ppermute | solution.py:219
  15.5 8.2 %collective-permute-start.7 = (bf16[128,256]{1,0:T(8,128)(2,1)S(1)}, bf16[128,256]{1,0:T(8,128)(2,1)S(1)}, u32[]{:S(2)}, u32[]{:S(2)}) collective-permute-start(bf16[128,256]{1,0:T(8,128)(2,1)S(1)} %get-tuple-element.20), channel_id=1, source_target_pairs={{0,8},{2,10},{4,12},{6,14},{8,0},{10,2},{12,4},{14,6},{1,9},{3,11}... | collective-permute-start | bytes 196616 | tf_op jit(solution)/shard_map/ppermute | solution.py:235
  16.9 6.7 %collective-permute-start.8 = (bf16[128,256]{1,0:T(8,128)(2,1)S(1)}, bf16[128,256]{1,0:T(8,128)(2,1)S(1)}, u32[]{:S(2)}, u32[]{:S(2)}) collective-permute-start(bf16[128,256]{1,0:T(8,128)(2,1)S(1)} %get-tuple-element.21), channel_id=1, source_target_pairs={{0,4},{2,6},{4,0},{6,2},{8,12},{10,14},{12,8},{14,10},{1,5},{3,7},... | collective-permute-start | bytes 196616 | tf_op jit(solution)/shard_map/ppermute | solution.py:235
  18.9 7.4 %collective-permute-start.11 = (bf16[128,256]{1,0:T(8,128)(2,1)S(1)}, bf16[128,256]{1,0:T(8,128)(2,1)S(1)}, u32[]{:S(2)}, u32[]{:S(2)}) collective-permute-start(bf16[128,256]{1,0:T(8,128)(2,1)S(1)} %get-tuple-element.22), channel_id=1, source_target_pairs={{0,14},{2,12},{4,10},{6,8},{8,6},{10,4},{12,2},{14,0},{1,15},{3,13... | collective-permute-start | bytes 196616 | tf_op jit(solution)/shard_map/ppermute | solution.py:235
  21.1 6.1 %collective-permute-start.10 = (bf16[128,256]{1,0:T(8,128)(2,1)S(1)}, bf16[128,256]{1,0:T(8,128)(2,1)S(1)}, u32[]{:S(2)}, u32[]{:S(2)}) collective-permute-start(bf16[128,256]{1,0:T(8,128)(2,1)S(1)} %get-tuple-element.22), channel_id=1, source_target_pairs={{0,12},{2,14},{4,8},{6,10},{8,4},{10,6},{12,0},{14,2},{1,13},{3,15... | collective-permute-start | bytes 196616 | tf_op jit(solution)/shard_map/ppermute | solution.py:235
  23.6 4.4 %copy-start.1 = (bf16[1,128,256]{2,1,0:T(8,128)(2,1)S(1)}, bf16[1,128,256]{2,1,0:T(8,128)(2,1)}, u32[]{:S(2)}) copy-start(bf16[1,128,256]{2,1,0:T(8,128)(2,1)} %param.9) | copy-start | bytes 196612
  23.7 4.3 %collective-permute-start.9 = (bf16[128,256]{1,0:T(8,128)(2,1)S(1)}, bf16[128,256]{1,0:T(8,128)(2,1)S(1)}, u32[]{:S(2)}, u32[]{:S(2)}) collective-permute-start(bf16[128,256]{1,0:T(8,128)(2,1)S(1)} %add_convert_fusion.3), channel_id=1, source_target_pairs={{0,2},{2,0},{4,6},{6,4},{8,10},{10,8},{12,14},{14,12},{1,3},{3,1},... | collective-permute-start | bytes 196616 | tf_op jit(solution)/shard_map/ppermute | solution.py:235
  28.1 12.6 %copy-start = (bf16[128,256]{1,0:T(8,128)(2,1)}, bf16[128,256]{1,0:T(8,128)(2,1)S(1)}, u32[]{:S(2)}) copy-start(bf16[128,256]{1,0:T(8,128)(2,1)S(1)} %add_convert_fusion.2.refs_8_) | copy-start | bytes 196612
  28.1 7.4 %collective-permute-start.14 = (bf16[128,256]{1,0:T(8,128)(2,1)S(1)}, bf16[128,256]{1,0:T(8,128)(2,1)S(1)}, u32[]{:S(2)}, u32[]{:S(2)}) collective-permute-start(bf16[128,256]{1,0:T(8,128)(2,1)S(1)} %add_convert_fusion.2.refs_8_), channel_id=1, source_target_pairs={{0,8},{4,12},{8,0},{12,4},{1,9},{5,13},{9,1},{13,5},{2,10},{6,14},... | collective-permute-start | bytes 196616 | tf_op jit(solution)/shard_map/ppermute | solution.py:219
  29.2 6.3 %collective-permute-start.13 = (bf16[128,256]{1,0:T(8,128)(2,1)S(1)}, bf16[128,256]{1,0:T(8,128)(2,1)S(1)}, u32[]{:S(2)}, u32[]{:S(2)}) collective-permute-start(bf16[128,256]{1,0:T(8,128)(2,1)S(1)} %add_convert_fusion.2.refs_8_), channel_id=1, source_target_pairs={{0,12},{4,8},{8,4},{12,0},{1,13},{5,9},{9,5},{13,1},{2,14},{6,10},... | collective-permute-start | bytes 196616 | tf_op jit(solution)/shard_map/ppermute | solution.py:219
  30.9 5.2 %collective-permute-start.12 = (bf16[128,256]{1,0:T(8,128)(2,1)S(1)}, bf16[128,256]{1,0:T(8,128)(2,1)S(1)}, u32[]{:S(2)}, u32[]{:S(2)}) collective-permute-start(bf16[128,256]{1,0:T(8,128)(2,1)S(1)} %add_convert_fusion.2.refs_8_), channel_id=1, source_target_pairs={{0,4},{4,0},{8,12},{12,8},{1,5},{5,1},{9,13},{13,9},{2,6},{6,2},{1... | collective-permute-start | bytes 196616 | tf_op jit(solution)/shard_map/ppermute | solution.py:219
  31.6 4.5 %collective-permute-start.15 = (bf16[128,256]{1,0:T(8,128)(2,1)S(1)}, bf16[128,256]{1,0:T(8,128)(2,1)S(1)}, u32[]{:S(2)}, u32[]{:S(2)}) collective-permute-start(bf16[128,256]{1,0:T(8,128)(2,1)S(1)} %add_convert_fusion.2.refs_8_), channel_id=1, source_target_pairs={{0,1},{1,0},{2,3},{3,2},{4,5},{5,4},{6,7},{7,6},{8,9},{9,8},{10,11... | collective-permute-start | bytes 196616 | tf_op jit(solution)/shard_map/ppermute | solution.py:219
  35.5 1.3 %collective-permute-start.18 = (bf16[128,256]{1,0:T(8,128)(2,1)S(1)}, bf16[128,256]{1,0:T(8,128)(2,1)S(1)}, u32[]{:S(2)}, u32[]{:S(2)}) collective-permute-start(bf16[128,256]{1,0:T(8,128)(2,1)S(1)} %collective-permute-done.14.refs_11_), channel_id=1, source_target_pairs={{0,1},{1,0},{2,3},{3,2},{4,5},{5,4},{6,7},{7,6},{8,9},{9,8},{10,11... | collective-permute-start | bytes 196616 | tf_op jit(solution)/shard_map/ppermute | solution.py:219
  35.5 1.4 %collective-permute-start.17 = (bf16[128,256]{1,0:T(8,128)(2,1)S(1)}, bf16[128,256]{1,0:T(8,128)(2,1)S(1)}, u32[]{:S(2)}, u32[]{:S(2)}) collective-permute-start(bf16[128,256]{1,0:T(8,128)(2,1)S(1)} %collective-permute-done.13.refs_10_), channel_id=1, source_target_pairs={{0,1},{1,0},{2,3},{3,2},{4,5},{5,4},{6,7},{7,6},{8,9},{9,8},{10,11... | collective-permute-start | bytes 196616 | tf_op jit(solution)/shard_map/ppermute | solution.py:219
  36.1 1.3 %collective-permute-start.16 = (bf16[128,256]{1,0:T(8,128)(2,1)S(1)}, bf16[128,256]{1,0:T(8,128)(2,1)S(1)}, u32[]{:S(2)}, u32[]{:S(2)}) collective-permute-start(bf16[128,256]{1,0:T(8,128)(2,1)S(1)} %collective-permute-done.12.refs_9_), channel_id=1, source_target_pairs={{0,1},{1,0},{2,3},{3,2},{4,5},{5,4},{6,7},{7,6},{8,9},{9,8},{10,11... | collective-permute-start | bytes 196616 | tf_op jit(solution)/shard_map/ppermute | solution.py:219
  40.7 7.7 %collective-permute-start.19 = (bf16[128,256]{1,0:T(8,128)(2,1)S(1)}, bf16[128,256]{1,0:T(8,128)(2,1)S(1)}, u32[]{:S(2)}, u32[]{:S(2)}) collective-permute-start(bf16[128,256]{1,0:T(8,128)(2,1)S(1)} %get-tuple-element.24), channel_id=1, source_target_pairs={{0,8},{2,10},{4,12},{6,14},{8,0},{10,2},{12,4},{14,6},{1,9},{3,11}... | collective-permute-start | bytes 196616 | tf_op jit(solution)/shard_map/ppermute | solution.py:235
  41.7 6.7 %collective-permute-start.20 = (bf16[128,256]{1,0:T(8,128)(2,1)S(1)}, bf16[128,256]{1,0:T(8,128)(2,1)S(1)}, u32[]{:S(2)}, u32[]{:S(2)}) collective-permute-start(bf16[128,256]{1,0:T(8,128)(2,1)S(1)} %get-tuple-element.25), channel_id=1, source_target_pairs={{0,4},{2,6},{4,0},{6,2},{8,12},{10,14},{12,8},{14,10},{1,5},{3,7},... | collective-permute-start | bytes 196616 | tf_op jit(solution)/shard_map/ppermute | solution.py:235
  43.2 7.4 %collective-permute-start.23 = (bf16[128,256]{1,0:T(8,128)(2,1)S(1)}, bf16[128,256]{1,0:T(8,128)(2,1)S(1)}, u32[]{:S(2)}, u32[]{:S(2)}) collective-permute-start(bf16[128,256]{1,0:T(8,128)(2,1)S(1)} %get-tuple-element.26), channel_id=1, source_target_pairs={{0,14},{2,12},{4,10},{6,8},{8,6},{10,4},{12,2},{14,0},{1,15},{3,13... | collective-permute-start | bytes 196616 | tf_op jit(solution)/shard_map/ppermute | solution.py:235
  46.4 6.1 %collective-permute-start.22 = (bf16[128,256]{1,0:T(8,128)(2,1)S(1)}, bf16[128,256]{1,0:T(8,128)(2,1)S(1)}, u32[]{:S(2)}, u32[]{:S(2)}) collective-permute-start(bf16[128,256]{1,0:T(8,128)(2,1)S(1)} %get-tuple-element.26), channel_id=1, source_target_pairs={{0,12},{2,14},{4,8},{6,10},{8,4},{10,6},{12,0},{14,2},{1,13},{3,15... | collective-permute-start | bytes 196616 | tf_op jit(solution)/shard_map/ppermute | solution.py:235
  48.4 4.3 %collective-permute-start.21 = (bf16[128,256]{1,0:T(8,128)(2,1)S(1)}, bf16[128,256]{1,0:T(8,128)(2,1)S(1)}, u32[]{:S(2)}, u32[]{:S(2)}) collective-permute-start(bf16[128,256]{1,0:T(8,128)(2,1)S(1)} %add_convert_fusion.1), channel_id=1, source_target_pairs={{0,2},{2,0},{4,6},{6,4},{8,10},{10,8},{12,14},{14,12},{1,3},{3,1},... | collective-permute-start | bytes 196616 | tf_op jit(solution)/shard_map/ppermute | solution.py:235
